TPU v7x, 256 devices: a whole 4x4x8 slice. The times are simulated.
256 devices in a mesh: rep: 16 (over z_lo, y, core), fsdp: 16 (over x, z_hi).
Axes of the slice: x: 4, y: 4, z: 8 (z_hi: 4, z_lo: 2; z = z_hi * 2 + z_lo), core: 2. Of those that a mesh axis runs over, the one named last changes fastest.
Arguments:
- activations: bfloat16 [229376, 4096], P(('rep', 'fsdp')), may hold values from -24 to 24
- cotangent: bfloat16 [229376, 1024], P(('rep', 'fsdp')), may hold values from -0.046875 to 0.046875
- momentum: float32 [16, 4096, 1024], P('rep', 'fsdp'), may hold values from -6 to 6
- band: int32 [32], replicated, may hold values from 0 to 975, as said below
Outputs:
- new_momentum: float32 [16, 4096, 1024], P('rep', 'fsdp')
- update: bfloat16 [4096, 1024], P('fsdp')
Inputs may be any that keep to these rules, and one draw needn't show every extreme that they name: `band`: the 32 entries are distinct; each is u * 64 + v with u and v below 16.
All inputs are finite; a program needn't handle non-finite values.
Results may differ from a plain program's by a relative error of at most 0.015.
Values may be sent and summed in bfloat16 or wider, within the bound.
No kernel may reach another device: no remote copies, remote signals or barrier semaphores. Data moves between devices by JAX's collectives and lax.ppermute only.
A program may use at most 128 MiB of HBM per device.

v0:
```python
import math

import jax
import jax.numpy as jnp
from jax import lax
from jax.sharding import PartitionSpec as P

BLOCK = 64
BAND = 32


DECAY = 0.9


def cosine_table(width):
    freq = jnp.arange(width, dtype=jnp.float32)[:, None]
    place = jnp.arange(width, dtype=jnp.float32)[None, :]
    factor = jnp.where(freq == 0, math.sqrt(1.0 / width), math.sqrt(2.0 / width))
    return factor * jnp.cos(math.pi * (2.0 * place + 1.0) * freq / (2.0 * width))


def per_device(activations, cotangent, momentum, band):
    nrows = momentum.shape[1]
    ncols = momentum.shape[2]
    side = BLOCK
    table = cosine_table(side)
    highest = lax.Precision.HIGHEST
    gradient = lax.psum_scatter(
        lax.dot_general(
            activations, cotangent, (((0,), (0,)), ((), ())), preferred_element_type=jnp.float32
        ).astype(jnp.bfloat16),
        "fsdp",
        scatter_dimension=0,
        tiled=True,
    ).astype(jnp.float32)
    updated = DECAY * momentum[0] + gradient
    blocks = updated.reshape(nrows // side, side, ncols // side, side)
    selector = (jnp.arange(side * side, dtype=jnp.int32)[:, None] == band[None, :]).astype(
        jnp.float32
    )

    def inverse(values):
        grid = jnp.einsum("abk,pk->abp", values, selector, precision=highest)
        grid = grid.reshape(nrows // side, ncols // side, side, side)
        back = jnp.einsum("ui,abuv,vj->aibj", table, grid, table, precision=highest)
        return back.reshape(nrows, ncols)

    coeffs = jnp.einsum("ui,aibj,vj->abuv", table, blocks, table, precision=highest)
    flat = coeffs.reshape(nrows // side, ncols // side, side * side)
    values = jnp.einsum("abp,pk->abk", flat, selector, precision=highest)
    fresh = (updated - inverse(values))[None]
    summed = lax.psum(values, "rep")
    scale = side / math.sqrt(BAND * lax.axis_size("rep"))
    update = (inverse(summed) * scale).astype(jnp.bfloat16)
    return (fresh, update)


def solution(mesh):
    in_specs = (P(("rep", "fsdp"), None), P(("rep", "fsdp"), None), P("rep", "fsdp", None), P())
    out_specs = (P("rep", "fsdp", None), P("fsdp", None))
    return jax.shard_map(
        per_device, mesh=mesh, in_specs=in_specs, out_specs=out_specs, check_vma=False
    )
```

profile of v0, /device:TPU:6, one launch (start us, length us, event | category | flops | bytes accessed | tf_op | source)
XLA Modules:
  0.0 253.1 jit_solution(1335164445480183616)
XLA Ops:
  7.2 0.0 copy-start
  7.2 0.0 reduce-scatter.2.cloned.1.call-start
  7.2 1.4 copy-done
  8.7 14.3 %convolution_convert_fusion = bf16[4096,1024]{1,0:T(8,128)(2,1)} fusion(bf16[896,4096]{1,0:T(8,128)(2,1)} %param.4, bf16[896,1024]{1,0:T(8,128)(2,1)S(1)} %copy-done), kind=kOutput, calls=%fused_computation | convolution fusion | flops 7520387072 | bytes 17563648 | tf_op jit(solution)/shard_map/dot_general | solution.py:29
  23.0 0.0 reduce-scatter.2.cloned.1.call-update
  23.1 124.0 %reduce-scatter.2.cloned.1.call-done = bf16[256,1024]{1,0:T(8,128)(2,1)} async-done(((bf16[4096,1024]{1,0:T(8,128)(2,1)}), bf16[256,1024]{1,0:T(8,128)(2,1)}) %reduce-scatter.2.cloned.1.call-update) | async-done | bytes 524304 | tf_op jit(solution)/shard_map/reduce_scatter | solution.py:28
  147.1 1.5 bitcast_add_fusion
  148.6 1.9 reshape.42
  150.5 4.2 %fusion = f32[4,16,64,64]{2,3,1,0:T(8,128)S(1)} fusion(f32[4,64,16,64]{3,2,1,0:T(8,128)} %reshape.42, f32[64]{0:T(128)S(1)} %get-tuple-element.3, f32[64]{0:T(128)S(1)} %get-tuple-element.2), kind=kOutput, calls=%fused_computation.1 | convolution fusion | flops 201338880 | bytes 2097664 | tf_op jit(solution)/shard_map/ui,aibj,vj->abuv/dot_general | solution.py:48
  154.8 3.3 %fusion.19 = f32[4,16,64,64]{3,2,1,0:T(8,128)} fusion(f32[4,16,64,64]{2,3,1,0:T(8,128)S(1)} %fusion, f32[64]{0:T(128)S(1)} %get-tuple-element.3, f32[64]{0:T(128)S(1)} %get-tuple-element.2), kind=kOutput, calls=%fused_computation.22 | convolution fusion | flops 201338880 | bytes 2097664 | tf_op jit(solution)/shard_map/ui,aibj,vj->abuv/dot_general | solution.py:48
  158.0 0.0 copy-start.1
  158.0 2.9 %reshape.43 = f32[4,16,4096]{2,1,0:T(8,128)} reshape(f32[4,16,64,64]{3,2,1,0:T(8,128)} %fusion.19) | data formatting | bytes 2097152 | tf_op jit(solution)/shard_map/reshape | solution.py:49
  160.9 0.0 copy-done.1
  160.9 1.9 fusion.8
  162.8 1.6 fusion.6
  164.4 54.8 %psum.7 = f32[4,16,32]{2,1,0:T(8,128)S(1)} all-reduce(f32[4,16,32]{2,1,0:T(8,128)S(1)} %fusion.8), channel_id=1, replica_groups=mesh['rep'=16,'fsdp'=16] {'rep'}, use_global_device_ids=true, to_apply=%region_1.2 | all-reduce | flops 2048 | bytes 16384 | tf_op jit(solution)/shard_map/psum | solution.py:52
  219.2 3.1 %reshape.44 = f32[4,16,64,64]{3,2,1,0:T(8,128)} reshape(f32[4,16,4096]{2,1,0:T(8,128)} %fusion.6) | data formatting | bytes 2097152 | tf_op jit(solution)/shard_map/reshape | solution.py:44
  222.4 3.6 %fusion.17 = f32[4,16,64,64]{2,3,1,0:T(8,128)S(1)} fusion(f32[4,16,64,64]{3,2,1,0:T(8,128)} %reshape.44, f32[64]{0:T(128)S(1)} %get-tuple-element.3, f32[64]{0:T(128)S(1)} %get-tuple-element.2), kind=kOutput, calls=%fused_computation.20 | convolution fusion | flops 201338880 | bytes 2097664 | tf_op jit(solution)/shard_map/ui,abuv,vj->aibj/dot_general | solution.py:45
  226.0 2.0 convolution_bitcast_fusion
  228.0 2.6 %copy.7 = f32[4,64,16,64]{3,2,1,0:T(8,128)} copy(f32[4,64,16,64]{3,1,2,0:T(8,128)S(1)} %convolution_bitcast_fusion) | data formatting | bytes 2097152 | tf_op jit(solution)/shard_map/ui,abuv,vj->aibj/transpose | solution.py:45
  230.6 2.7 %reshape.45 = f32[256,1024]{1,0:T(8,128)} reshape(f32[4,64,16,64]{3,2,1,0:T(8,128)} %copy.7) | data formatting | bytes 2097152 | tf_op jit(solution)/shard_map/reshape | solution.py:46
  233.3 2.3 subtract_bitcast_fusion
  235.6 0.6 fusion.4
  236.3 2.2 reshape.46
  238.5 3.6 %fusion.14 = f32[4,16,64,64]{2,3,1,0:T(8,128)S(1)} fusion(f32[4,16,64,64]{3,2,1,0:T(8,128)} %reshape.46, f32[64]{0:T(128)S(1)} %get-tuple-element.3, f32[64]{0:T(128)S(1)} %get-tuple-element.2), kind=kOutput, calls=%fused_computation.17 | convolution fusion | flops 201338880 | bytes 2097664 | tf_op jit(solution)/shard_map/ui,abuv,vj->aibj/dot_general | solution.py:45
  242.1 1.9 fusion.2
  244.0 0.7 copy.8
  244.7 1.5 convert_element_type.20
  (1 shorter events, 0.0 us)
Async XLA Ops:
  7.2 1.5 copy-start
  7.2 139.9 %reduce-scatter.2.cloned.1.call-start = ((), (), s32[]{:S(2)}) async-start(), calls=%async_computation.1 | async-start | bytes 8912896 | tf_op jit(solution)/shard_map/reduce_scatter | solution.py:28
  158.0 2.9 %copy-start.1 = (s32[32]{0:T(128)S(1)}, s32[32]{0:T(128)}, u32[]{:S(2)}) copy-start(s32[32]{0:T(128)} %param.7) | copy-start | bytes 388
Sparse Core Ops, SparseCore 0:
  23.2 123.8 reduce-scatter.1
where the time goes:
time: 254 us; the launch traced here: 253 us
  waiting for transfers between devices  124 us (49%)
  blocking collectives  54.8 us (22%)
  matrix products  37.2 us (15%)
  local copies, waits for them, and re-layouts  19 us (7%)
  between operations  14.1 us (6%)
  other arithmetic  3.87 us (2%)
    reduce_scatter x1, waiting for transfers between devices, per_device(): lax.psum_scatter(lax.dot_general(activations, cotangent, (((0,), (0,)), (...  124 us
    psum x1, blocking collectives, per_device(): summed = lax.psum(values, 'rep')  54.8 us
    dot_general x1, matrix products, per_device(): lax.dot_general(activations, cotangent, (((0,), (0,)), ((), ())), preferr...  14.3 us
    dot_general x4, matrix products, inverse(): back = jnp.einsum('ui,abuv,vj->aibj', table, grid, table, precision=highest)  11.2 us
    dot_general x2, matrix products, per_device(): jnp.einsum('ui,aibj,vj->abuv', table, blocks, table, precision=highest)  7.49 us
    reshape x2, local copies, waits for them, and re-layouts, inverse(): grid = grid.reshape(nrows // side, ncols // side, side, side)  5.3 us
  transfers between devices with their start and end apart: 1, of which 1 were waited for; matrix products, arithmetic and copies ran while one was open for 0% of the time, Pallas kernels for 0%

commit v1 on v0

v1 whole, which is shorter than its diff:
```python
import functools
import math

import jax
import jax.numpy as jnp
import numpy as np
from jax import lax
from jax.experimental import pallas as pl
from jax.experimental.pallas import tpu as pltpu
from jax.sharding import PartitionSpec as P

BLOCK = 64
BAND = 32
LOW = 16
DECAY = 0.9
ROWS = 256
HALVES = (((1, 2), (0, 3), (1, 2, 0, 3)), ((3, 2), (0, 1), (3, 2, 0, 1)))
X_MASKS = (4, 12)
Z_MASKS = (1, 3)
CHUNKS = {"a1": (True, 0, 256), "a2": (True, 512, 128), "b": (False, 768, 128)}
HIGHEST = lax.Precision.HIGHEST
VMEM = 32 * 1024 * 1024


def low_table():
    freq = np.arange(LOW, dtype=np.float64)[:, None]
    place = np.arange(BLOCK, dtype=np.float64)[None, :]
    factor = np.where(freq == 0, math.sqrt(1.0 / BLOCK), math.sqrt(2.0 / BLOCK))
    table = factor * np.cos(math.pi * (2.0 * place + 1.0) * freq / (2.0 * BLOCK))
    return np.kron(np.eye(ROWS // BLOCK), table).astype(np.float32)


def swap(value, axis, mask):
    n = lax.axis_size(axis)
    return lax.ppermute(value, axis, [(i, i ^ mask) for i in range(n)])


def targets_of(chunk, part):
    x_first = CHUNKS[chunk][0]
    steps = {ka: [] for ka in range(4)}
    for half, (sends, keeps, second) in enumerate(HALVES):
        for i, k1 in enumerate(sends if part == "send" else keeps):
            for j, k2 in enumerate(second):
                ka, kb = (k1, k2) if x_first else (k2, k1)
                steps[ka].append((half, i, j, kb))
    return steps


def term_kernel(jobs, first, pos_ref, act_ref, *refs):
    n_gt = first["n_gt"]
    gts = refs[:n_gt]
    outs = refs[n_gt:]
    step = pl.program_id(0)
    if first["transpose"] is not None:
        gt_out = outs[-1]
        col0, ncol = first["transpose"]

        @pl.when(step == 0)
        def _():
            gt_out[...] = gts[0][...].T

        gts = (gt_out,)
    for at, job in enumerate(jobs):

        @pl.when(step == at)
        def _(job=job):
            for gt, row, rows, out, i, j, kb in job:
                offset = pl.multiple_of((pos_ref[0] ^ kb) * ROWS, ROWS)
                block = act_ref[:, pl.ds(offset, ROWS)]
                outs[out][i, j] = jnp.dot(
                    gts[gt][row : row + rows, :], block, preferred_element_type=jnp.float32
                ).astype(jnp.bfloat16)


def position(order):
    me = lax.axis_index("fsdp")
    a, b = me // 4, me % 4
    return jnp.stack([b] + [a ^ k for k in order]).astype(jnp.int32)


def terms_to_send(activations, cotangent, chunk):
    _, col, half_cols = CHUNKS[chunk]
    tokens = activations.shape[0]
    steps = targets_of(chunk, "send")
    order = [k for k in (2, 1, 3, 0) if steps[k]]
    jobs = [[(0, h * half_cols, half_cols, h, i, j, kb) for h, i, j, kb in steps[k]] for k in order]
    ncol = 2 * half_cols
    block = jax.ShapeDtypeStruct((2, 4, half_cols, ROWS), jnp.bfloat16)
    whole = pl.BlockSpec((2, 4, half_cols, ROWS), lambda s, p: (0, 0, 0, 0))
    return pl.pallas_call(
        functools.partial(term_kernel, jobs, dict(n_gt=1, transpose=(col, ncol))),
        grid_spec=pltpu.PrefetchScalarGridSpec(
            num_scalar_prefetch=1,
            grid=(len(order),),
            in_specs=[
                pl.BlockSpec((tokens, 4 * ROWS), lambda s, p: (0, p[1 + s])),
                pl.BlockSpec((tokens, ncol), lambda s, p: (0, col // ncol)),
            ],
            out_specs=[whole, whole, pl.BlockSpec((ncol, tokens), lambda s, p: (0, 0))],
        ),
        out_shape=[block, block, jax.ShapeDtypeStruct((ncol, tokens), jnp.bfloat16)],
        compiler_params=pltpu.CompilerParams(vmem_limit_bytes=VMEM),
        cost_estimate=pl.CostEstimate(
            flops=16 * half_cols * ROWS * tokens * 2, bytes_accessed=tokens * 4096 * 2, transcendentals=0
        ),
        name="terms_" + chunk,
    )(position(order), activations, cotangent)


def terms_to_keep(activations, gts, chunks):
    tokens = activations.shape[0]
    order = [0, 1, 3, 2]
    jobs = [[] for _ in order]
    out_shape, out_specs = [], []
    for at, chunk in enumerate(chunks):
        half_cols = CHUNKS[chunk][2]
        steps = targets_of(chunk, "keep")
        for s, k in enumerate(order):
            jobs[s] += [(at, h * half_cols, half_cols, 2 * at + h, i, j, kb) for h, i, j, kb in steps[k]]
        out_shape += [jax.ShapeDtypeStruct((2, 4, half_cols, ROWS), jnp.bfloat16)] * 2
        out_specs += [pl.BlockSpec((2, 4, half_cols, ROWS), lambda s, p: (0, 0, 0, 0))] * 2
    used = [s for s in range(4) if jobs[s]]
    order, jobs = [order[s] for s in used], [jobs[s] for s in used]
    outs = pl.pallas_call(
        functools.partial(term_kernel, jobs, dict(n_gt=len(chunks), transpose=None)),
        grid_spec=pltpu.PrefetchScalarGridSpec(
            num_scalar_prefetch=1,
            grid=(len(order),),
            in_specs=[pl.BlockSpec((tokens, 4 * ROWS), lambda s, p: (0, p[1 + s]))]
            + [pl.BlockSpec(g.shape, lambda s, p: (0, 0)) for g in gts],
            out_specs=out_specs,
        ),
        out_shape=out_shape,
        compiler_params=pltpu.CompilerParams(vmem_limit_bytes=VMEM),
        cost_estimate=pl.CostEstimate(
            flops=sum(j[2] for job in jobs for j in job) * ROWS * tokens * 2,
            bytes_accessed=tokens * 4096 * 2,
            transcendentals=0,
        ),
        name="terms_keep_" + "_".join(chunks),
    )(position(order), activations, *gts)
    return {c: (outs[2 * i], outs[2 * i + 1]) for i, c in enumerate(chunks)}


def f32(x):
    return x.astype(jnp.float32)


def dot(a, b, dims=((1,), (0,))):
    return lax.dot_general(a, b, (dims, ((), ())), precision=HIGHEST, preferred_element_type=jnp.float32)


def final_kernel(half_cols, first_call, *refs):
    pieces = refs[:10]
    mom_ref, mask_ref, low_ref = refs[10:13]
    fresh_ref, coeff_ref = refs[13:] if first_call else refs[14:]
    halves = []
    for h in range(2):
        k, r, q, rz, qz = (ref[...].reshape(half_cols, ROWS) for ref in pieces[5 * h : 5 * h + 5])
        halves.append(f32(k) + f32(r) + f32(q) + f32(rz) + f32(qz))
    gradient = jnp.concatenate(halves, axis=0)
    low = low_ref[...]
    mask = mask_ref[...]
    for g in range(2 * half_cols // ROWS):
        cols = slice(g * ROWS, (g + 1) * ROWS)
        updated = DECAY * mom_ref[0, :, cols] + gradient[cols, :].T
        coeff = dot(dot(low, updated), low, ((1,), (1,))) * mask
        coeff_ref[g] = coeff
        fresh_ref[0, :, cols] = updated - dot(dot(low, coeff, ((0,), (0,))), low)


def finish(pieces, momentum, mask, low, chunk, fresh):
    _, col, half_cols = CHUNKS[chunk]
    ncol = 2 * half_cols
    groups = ncol // ROWS
    specs = []
    for _ in range(2):
        specs += [
            pl.BlockSpec((1, 1, half_cols, ROWS), lambda s: (0, 2, 0, 0)),
            pl.BlockSpec((1, 1, half_cols, ROWS), lambda s: (0, 2, 0, 0)),
            pl.BlockSpec((1, half_cols, ROWS), lambda s: (2, 0, 0)),
            pl.BlockSpec((1, half_cols, ROWS), lambda s: (0, 0, 0)),
            pl.BlockSpec((half_cols, ROWS), lambda s: (0, 0)),
        ]
    columns = pl.BlockSpec((1, ROWS, ncol), lambda s: (0, 0, col // ncol))
    specs += [columns, pl.BlockSpec((64, 64), lambda s: (0, 0)), pl.BlockSpec((64, ROWS), lambda s: (0, 0))]
    args = [*pieces[0], *pieces[1], momentum, mask, low]
    aliases = {}
    if fresh is not None:
        specs.append(pl.BlockSpec(memory_space=pl.ANY))
        args.append(fresh)
        aliases = {13: 0}
    return pl.pallas_call(
        functools.partial(final_kernel, half_cols, fresh is None),
        grid=(1,),
        in_specs=specs,
        out_specs=[columns, pl.BlockSpec((groups, 64, 64), lambda s: (0, 0, 0))],
        out_shape=[
            jax.ShapeDtypeStruct(momentum.shape, jnp.float32),
            jax.ShapeDtypeStruct((groups, 64, 64), jnp.float32),
        ],
        input_output_aliases=aliases,
        compiler_params=pltpu.CompilerParams(vmem_limit_bytes=VMEM),
        cost_estimate=pl.CostEstimate(flops=ncol * 1000000, bytes_accessed=ncol * 256 * 16, transcendentals=0),
        name="finish_" + chunk,
    )(*args)


def update_kernel(scale, parts, *refs):
    low_ref, out_ref = refs[-2:]
    low = low_ref[...]
    g = 0
    for ref, n in zip(refs[:-2], parts):
        for i in range(n):
            value = dot(dot(low, ref[i], ((0,), (0,))), low) * scale
            out_ref[:, g * ROWS : (g + 1) * ROWS] = value.astype(jnp.bfloat16)
            g += 1


def make_update(sums, low, ncols, scale):
    return pl.pallas_call(
        functools.partial(update_kernel, scale, [s.shape[0] for s in sums]),
        out_shape=jax.ShapeDtypeStruct((ROWS, ncols), jnp.bfloat16),
        compiler_params=pltpu.CompilerParams(vmem_limit_bytes=VMEM),
        name="update",
    )(*sums, low)


def per_device(activations, cotangent, momentum, band):
    low = jnp.asarray(low_table())
    spots = jnp.arange(LOW)[:, None] * BLOCK + jnp.arange(LOW)[None, :]
    chosen = (spots[:, :, None] == band[None, None, :]).any(axis=-1).astype(jnp.float32)
    mask = jnp.tile(chosen, (4, 4))

    sends, gts = {}, {}
    for c in ("a1", "b", "a2"):
        s1, s2, gts[c] = terms_to_send(activations, cotangent, c)
        sends[c] = (s1, s2)
    keeps = terms_to_keep(activations, [gts[c] for c in ("a1", "b", "a2")], ("a1", "b", "a2"))

    def masks(c):
        return (X_MASKS, Z_MASKS) if CHUNKS[c][0] else (Z_MASKS, X_MASKS)

    def chunk_flow(c):
        (m1, m2), (n1, n2) = masks(c)
        k = keeps[c]
        r = (swap(sends[c][0], "fsdp", m1), swap(sends[c][1], "fsdp", m2))
        t = [(f32(k[h][1]) + f32(r[h][1])).astype(jnp.bfloat16) for h in range(2)]
        q = (swap(t[0], "fsdp", m2), swap(t[1], "fsdp", m1))

        def total(h, j):
            return f32(k[h][0, j]) + f32(r[h][0, j]) + f32(q[h][j])

        v = [total(h, slice(0, 2)).astype(jnp.bfloat16) for h in range(2)]
        rz = (swap(v[0], "fsdp", n1), swap(v[1], "fsdp", n2))
        w = [(total(h, 3) + f32(rz[h][1])).astype(jnp.bfloat16) for h in range(2)]
        qz = (swap(w[0], "fsdp", n2), swap(w[1], "fsdp", n1))
        return [(k[h], r[h], q[h], rz[h], qz[h]) for h in range(2)]

    fresh = None
    coeffs = {}
    for c in ("b", "a1", "a2"):
        fresh, coeffs[c] = finish(chunk_flow(c), momentum, mask, low, c, fresh)
    summed = jnp.concatenate([coeffs[c] for c in ("a1", "a2", "b")], axis=0)
    for m in (1, 8, 2, 6):
        summed = summed + swap(summed, "rep", m)
    scale = BLOCK / math.sqrt(BAND * lax.axis_size("rep"))
    update = make_update([summed], low, momentum.shape[2], scale)
    return (fresh, update)


def solution(mesh):
    in_specs = (P(("rep", "fsdp"), None), P(("rep", "fsdp"), None), P("rep", "fsdp", None), P())
    out_specs = (P("rep", "fsdp", None), P("fsdp", None))
    return jax.shard_map(
        per_device, mesh=mesh, in_specs=in_specs, out_specs=out_specs, check_vma=False
    )
```

time: 254 us -> 154 us (0.61)
  waiting for transfers between devices: 124 us -> 42.3 us
  blocking collectives: 54.8 us -> 0 us
  starting transfers between devices: 0.04 us -> 45 us
  matrix products: 37.2 us -> 0 us
  Pallas kernels: 0 us -> 31.1 us
  between operations: 14.1 us -> 0.97 us
  other arithmetic: 3.87 us -> 14.3 us
    reduce_scatter x1 -> x0, waiting for transfers between devices: 124 us -> none  [per_device(): lax.psum_scatter(lax.dot_general(activations, cotangent, (((0,), (0,)), (...]
    psum x1 -> x0, blocking collectives: 54.8 us -> none  [per_device(): summed = lax.psum(values, 'rep')]
    ppermute x0 -> x28, starting transfers between devices: none -> 45 us  [swap(): return lax.ppermute(value, axis, [(i, i ^ mask) for i in range(n)])]
    ppermute x0 -> x28, waiting for transfers between devices: none -> 42.3 us  [swap(): return lax.ppermute(value, axis, [(i, i ^ mask) for i in range(n)])]
    dot_general x10 -> x0, matrix products: 37.2 us -> none  [the longest x1 14.3 us: per_device(): lax.dot_general(activations, cotangent, (((0,), (0,)), ((), ())), preferr...]
    pallas_call x0 -> x8, Pallas kernels: none -> 31.1 us  [the longest x3 13 us: terms_to_send(): pl.pallas_call(functools.partial(term_kernel, jobs, dict(n_gt=1, transpos...]
    unnamed x4 -> x54, local copies, waits for them, and re-layouts: 1.46 us -> 19.5 us
    convert_element_type x0 -> x19, other arithmetic: none -> 13.6 us  [the longest x6 6.61 us: chunk_flow(): t = [(f32(k[h][1]) + f32(r[h][1])).astype(jnp.bfloat16) for h in range(2)]]
  transfers between devices with their start and end apart: 1 -> 28, of which waited for: 1 -> 13; matrix products, arithmetic and copies ran while one was open for 0% -> 9% of each run, Pallas kernels for 0% -> 14%
where the time goes in v1:
time: 154 us; the launch traced here: 153 us
  starting transfers between devices  45 us (29%)
  waiting for transfers between devices  42.3 us (27%)
  Pallas kernels  31.1 us (20%)
  local copies, waits for them, and re-layouts  19.8 us (13%)
  other arithmetic  14.3 us (9%)
    ppermute x28, starting transfers between devices, swap(): return lax.ppermute(value, axis, [(i, i ^ mask) for i in range(n)])  45 us
    ppermute x28, waiting for transfers between devices, swap(): return lax.ppermute(value, axis, [(i, i ^ mask) for i in range(n)])  42.3 us
    unnamed x54, local copies, waits for them, and re-layouts  19.5 us
    pallas_call x3, Pallas kernels, terms_to_send(): pl.pallas_call(functools.partial(term_kernel, jobs, dict(n_gt=1, transpos...  13 us
    pallas_call x3, Pallas kernels, finish(): pl.pallas_call(functools.partial(final_kernel, half_cols, fresh is None),...  9.11 us
    convert_element_type x6, other arithmetic, chunk_flow(): t = [(f32(k[h][1]) + f32(r[h][1])).astype(jnp.bfloat16) for h in range(2)]  6.61 us
    pallas_call x1, Pallas kernels, terms_to_keep(): pl.pallas_call(functools.partial(term_kernel, jobs, dict(n_gt=len(chunks)...  6.38 us
    convert_element_type x6, other arithmetic, chunk_flow(): v = [total(h, slice(0, 2)).astype(jnp.bfloat16) for h in range(2)]  4.2 us
  transfers between devices with their start and end apart: 28, of which 13 were waited for; matrix products, arithmetic and copies ran while one was open for 9% of the time, Pallas kernels for 14%

profile of v1, /device:TPU:6, one launch (start us, length us, event | category | flops | bytes accessed | tf_op | source)
XLA Modules:
  0.0 153.5 jit_solution(15519300628864662520)
XLA Ops:
  0.7 3.1 %copy-done = bf16[896,4096]{1,0:T(8,128)(2,1)S(1)} copy-done((bf16[896,4096]{1,0:T(8,128)(2,1)S(1)}, bf16[896,4096]{1,0:T(8,128)(2,1)}, u32[]{:S(2)}) %copy-start) | copy-done | bytes 7340056
  5.3 4.2 %terms_b.1 = (bf16[2,4,128,256]{3,2,1,0:T(8,128)(2,1)}, bf16[2,4,128,256]{3,2,1,0:T(8,128)(2,1)}, bf16[256,896]{1,0:T(8,128)(2,1)S(1)}) custom-call(s32[5]{0:T(128)S(1)} %stack.45.pos_ref, bf16[896,4096]{1,0:T(8,128)(2,1)S(1)} %copy-done, bf16[896,1024]{1,0:T(8,128)(2,1)S(1)} %copy-done.3), custom_call_target="tpu_custom_call" | custom-call | flops 939524096 | bytes 7340032 | tf_op jit(solution)/shard_map/terms_b/pallas_call | solution.py:90
  10.3 6.3 %collective-permute-start.20 = (bf16[2,4,128,256]{3,2,1,0:T(8,128)(2,1)}, bf16[2,4,128,256]{3,2,1,0:T(8,128)(2,1)}, u32[]{:S(2)}, u32[]{:S(2)}) collective-permute-start(bf16[2,4,128,256]{3,2,1,0:T(8,128)(2,1)} %get-tuple-element.37), channel_id=1, source_target_pairs={{0,3},{1,2},{2,1},{3,0},{4,7},{5,6},{6,5},{7,4},{8,11},{9,10},{10,... | collective-permute-start | bytes 1572872 | tf_op jit(solution)/shard_map/ppermute | solution.py:35
  18.1 5.2 %terms_a1.1 = (bf16[2,4,256,256]{3,2,1,0:T(8,128)(2,1)}, bf16[2,4,256,256]{3,2,1,0:T(8,128)(2,1)}, bf16[512,896]{1,0:T(8,128)(2,1)S(1)}) custom-call(s32[4]{0:T(128)S(1)} %pad_add_fusion.pos_ref, bf16[896,4096]{1,0:T(8,128)(2,1)S(1)} %copy-done.1, bf16[896,1024]{1,0:T(8,128)(2,1)S(1)} %copy-done.3), custom_call_target="tpu_custom_call" | custom-call | flops 1879048192 | bytes 7340032 | tf_op jit(solution)/shard_map/terms_a1/pallas_call | solution.py:90
  25.6 3.6 %terms_a2.1 = (bf16[2,4,128,256]{3,2,1,0:T(8,128)(2,1)S(1)}, bf16[2,4,128,256]{3,2,1,0:T(8,128)(2,1)}, bf16[256,896]{1,0:T(8,128)(2,1)S(1)}) custom-call(s32[4]{0:T(128)S(1)} %pad_add_fusion.pos_ref, bf16[896,4096]{1,0:T(8,128)(2,1)S(1)} %copy-done.1, bf16[896,1024]{1,0:T(8,128)(2,1)S(1)} %copy-done.3), custom_call_target="tpu_custom_call" | custom-call | flops 939524096 | bytes 7340032 | tf_op jit(solution)/shard_map/terms_a2/pallas_call | solution.py:90
  30.8 2.1 %collective-permute-start.4 = (bf16[2,4,128,256]{3,2,1,0:T(8,128)(2,1)}, bf16[2,4,128,256]{3,2,1,0:T(8,128)(2,1)}, u32[]{:S(2)}, u32[]{:S(2)}) collective-permute-start(bf16[2,4,128,256]{3,2,1,0:T(8,128)(2,1)} %get-tuple-element.29), channel_id=1, source_target_pairs={{0,12},{1,13},{2,14},{3,15},{4,8},{5,9},{6,10},{7,11},{8,4},{9,5},... | collective-permute-start | bytes 1572872 | tf_op jit(solution)/shard_map/ppermute | solution.py:35
  33.0 3.1 %copy-done.2 = bf16[896,4096]{1,0:T(8,128)(2,1)S(1)} copy-done((bf16[896,4096]{1,0:T(8,128)(2,1)S(1)}, bf16[896,4096]{1,0:T(8,128)(2,1)}, u32[]{:S(2)}) %copy-start.2) | copy-done | bytes 7340056
  39.3 6.4 %terms_keep_a1_b_a2.1 = (bf16[2,4,256,256]{3,2,1,0:T(8,128)(2,1)S(1)}, bf16[2,4,256,256]{3,2,1,0:T(8,128)(2,1)S(1)}, bf16[2,4,128,256]{3,2,1,0:T(8,128)(2,1)S(1)...) custom-call(s32[5]{0:T(128)S(1)} %stack.21.pos_ref, ...), custom_call_target="tpu_custom_call" | custom-call | flops 3758096384 | bytes 7340032 | tf_op jit(solution)/shard_map/terms_keep_a1_b_a2/pallas_call | solution.py:124
  54.1 1.6 %collective-permute-start.21 = (bf16[4,128,256]{2,1,0:T(8,128)(2,1)S(1)}, bf16[4,128,256]{2,1,0:T(8,128)(2,1)S(1)}, u32[]{:S(2)}, u32[]{:S(2)}) collective-permute-start(bf16[4,128,256]{2,1,0:T(8,128)(2,1)S(1)} %fusion.7), channel_id=1, source_target_pairs={{0,1},{1,0},{2,3},{3,2},{4,5},{5,4},{6,7},{7,6},{8,9},{9,8},{10,11... | collective-permute-start | bytes 786440 | tf_op jit(solution)/shard_map/ppermute | solution.py:35
  56.8 4.6 %collective-permute-done.4.refs_6_ = bf16[2,4,128,256]{3,2,1,0:T(8,128)(2,1)} collective-permute-done((bf16[2,4,128,256]{3,2,1,0:T(8,128)(2,1)}, bf16[2,4,128,256]{3,2,1,0:T(8,128)(2,1)}, u32[]{:S(2)}, u32[]{:S(2)}) %collective-permute-start.4) | collective-permute-done | bytes 524320 | tf_op jit(solution)/shard_map/ppermute | solution.py:35
  62.8 1.6 %collective-permute-done.refs_1_ = bf16[2,4,128,256]{3,2,1,0:T(8,128)(2,1)S(1)} collective-permute-done((bf16[2,4,128,256]{3,2,1,0:T(8,128)(2,1)}, bf16[2,4,128,256]{3,2,1,0:T(8,128)(2,1)S(1)}, u32[]{:S(2)}, u32[]{:S(2)}) %collective-permute-start) | collective-permute-done | bytes 524320 | tf_op jit(solution)/shard_map/ppermute | solution.py:35
  69.4 3.1 %collective-permute-done.17.refs_2_ = bf16[4,128,256]{2,1,0:T(8,128)(2,1)S(1)} collective-permute-done((bf16[4,128,256]{2,1,0:T(8,128)(2,1)S(1)}, bf16[4,128,256]{2,1,0:T(8,128)(2,1)S(1)}, u32[]{:S(2)}, u32[]{:S(2)}) %collective-permute-start.17) | collective-permute-done | bytes 262176 | tf_op jit(solution)/shard_map/ppermute | solution.py:35
  77.2 3.8 %collective-permute-start.2 = (bf16[2,128,256]{2,1,0:T(8,128)(2,1)S(1)}, bf16[2,128,256]{2,1,0:T(8,128)(2,1)S(1)}, u32[]{:S(2)}, u32[]{:S(2)}) collective-permute-start(bf16[2,128,256]{2,1,0:T(8,128)(2,1)S(1)} %fusion.13), channel_id=1, source_target_pairs={{0,1},{1,0},{2,3},{3,2},{4,5},{5,4},{6,7},{7,6},{8,9},{9,8},{10,11... | collective-permute-start | bytes 393224 | tf_op jit(solution)/shard_map/ppermute | solution.py:35
  82.2 2.1 %collective-permute-start.13 = (bf16[4,256,256]{2,1,0:T(8,128)(2,1)S(1)}, bf16[4,256,256]{2,1,0:T(8,128)(2,1)S(1)}, u32[]{:S(2)}, u32[]{:S(2)}) collective-permute-start(bf16[4,256,256]{2,1,0:T(8,128)(2,1)S(1)} %fusion.1), channel_id=1, source_target_pairs={{0,4},{1,5},{2,6},{3,7},{4,0},{5,1},{6,2},{7,3},{8,12},{9,13},{10,... | collective-permute-start | bytes 1572872 | tf_op jit(solution)/shard_map/ppermute | solution.py:35
  85.5 2.8 %collective-permute-start.9 = (bf16[4,256,256]{2,1,0:T(8,128)(2,1)S(1)}, bf16[4,256,256]{2,1,0:T(8,128)(2,1)S(1)}, u32[]{:S(2)}, u32[]{:S(2)}) collective-permute-start(bf16[4,256,256]{2,1,0:T(8,128)(2,1)S(1)} %fusion), channel_id=1, source_target_pairs={{0,12},{1,13},{2,14},{3,15},{4,8},{5,9},{6,10},{7,11},{8,4},{9,5},... | collective-permute-start | bytes 1572872 | tf_op jit(solution)/shard_map/ppermute | solution.py:35
  90.4 4.9 %collective-permute-done.13.refs_7_ = bf16[4,256,256]{2,1,0:T(8,128)(2,1)S(1)} collective-permute-done((bf16[4,256,256]{2,1,0:T(8,128)(2,1)S(1)}, bf16[4,256,256]{2,1,0:T(8,128)(2,1)S(1)}, u32[]{:S(2)}, u32[]{:S(2)}) %collective-permute-start.13) | collective-permute-done | bytes 524320 | tf_op jit(solution)/shard_map/ppermute | solution.py:35
  95.3 3.0 %collective-permute-start.19 = (bf16[128,256]{1,0:T(8,128)(2,1)S(1)}, bf16[128,256]{1,0:T(8,128)(2,1)S(1)}, u32[]{:S(2)}, u32[]{:S(2)}) collective-permute-start(bf16[128,256]{1,0:T(8,128)(2,1)S(1)} %fusion.15), channel_id=1, source_target_pairs={{0,12},{1,13},{2,14},{3,15},{4,8},{5,9},{6,10},{7,11},{8,4},{9,5},... | collective-permute-start | bytes 196616 | tf_op jit(solution)/shard_map/ppermute | solution.py:35
  99.2 2.1 %collective-permute-start.14 = (bf16[2,256,256]{2,1,0:T(8,128)(2,1)S(1)}, bf16[2,256,256]{2,1,0:T(8,128)(2,1)S(1)}, u32[]{:S(2)}, u32[]{:S(2)}) collective-permute-start(bf16[2,256,256]{2,1,0:T(8,128)(2,1)S(1)} %fusion.2), channel_id=1, source_target_pairs={{0,3},{1,2},{2,1},{3,0},{4,7},{5,6},{6,5},{7,4},{8,11},{9,10},{10,... | collective-permute-start | bytes 786440 | tf_op jit(solution)/shard_map/ppermute | solution.py:35
  101.4 1.6 %collective-permute-start.10 = (bf16[2,256,256]{2,1,0:T(8,128)(2,1)S(1)}, bf16[2,256,256]{2,1,0:T(8,128)(2,1)S(1)}, u32[]{:S(2)}, u32[]{:S(2)}) collective-permute-start(bf16[2,256,256]{2,1,0:T(8,128)(2,1)S(1)} %fusion.3), channel_id=1, source_target_pairs={{0,1},{1,0},{2,3},{3,2},{4,5},{5,4},{6,7},{7,6},{8,9},{9,8},{10,11... | collective-permute-start | bytes 786440 | tf_op jit(solution)/shard_map/ppermute | solution.py:35
  103.9 5.8 %collective-permute-done.14.refs_8_ = bf16[2,256,256]{2,1,0:T(8,128)(2,1)S(1)} collective-permute-done((bf16[2,256,256]{2,1,0:T(8,128)(2,1)S(1)}, bf16[2,256,256]{2,1,0:T(8,128)(2,1)S(1)}, u32[]{:S(2)}, u32[]{:S(2)}) %collective-permute-start.14) | collective-permute-done | bytes 262176 | tf_op jit(solution)/shard_map/ppermute | solution.py:35
  109.7 2.6 %collective-permute-start.7 = (bf16[128,256]{1,0:T(8,128)(2,1)S(1)}, bf16[128,256]{1,0:T(8,128)(2,1)S(1)}, u32[]{:S(2)}, u32[]{:S(2)}) collective-permute-start(bf16[128,256]{1,0:T(8,128)(2,1)S(1)} %fusion.16), channel_id=1, source_target_pairs={{0,1},{1,0},{2,3},{3,2},{4,5},{5,4},{6,7},{7,6},{8,9},{9,8},{10,11... | collective-permute-start | bytes 196616 | tf_op jit(solution)/shard_map/ppermute | solution.py:35
  112.3 4.7 %collective-permute-done.10.refs_3_ = bf16[2,256,256]{2,1,0:T(8,128)(2,1)S(1)} collective-permute-done((bf16[2,256,256]{2,1,0:T(8,128)(2,1)S(1)}, bf16[2,256,256]{2,1,0:T(8,128)(2,1)S(1)}, u32[]{:S(2)}, u32[]{:S(2)}) %collective-permute-start.10) | collective-permute-done | bytes 262176 | tf_op jit(solution)/shard_map/ppermute | solution.py:35
  117.1 2.3 %collective-permute-start.11 = (bf16[256,256]{1,0:T(8,128)(2,1)S(1)}, bf16[256,256]{1,0:T(8,128)(2,1)S(1)}, u32[]{:S(2)}, u32[]{:S(2)}) collective-permute-start(bf16[256,256]{1,0:T(8,128)(2,1)S(1)} %fusion.9), channel_id=1, source_target_pairs={{0,3},{1,2},{2,1},{3,0},{4,7},{5,6},{6,5},{7,4},{8,11},{9,10},{10,... | collective-permute-start | bytes 393224 | tf_op jit(solution)/shard_map/ppermute | solution.py:35
  119.5 2.0 %collective-permute-start.3 = (bf16[128,256]{1,0:T(8,128)(2,1)S(1)}, bf16[128,256]{1,0:T(8,128)(2,1)S(1)}, u32[]{:S(2)}, u32[]{:S(2)}) collective-permute-start(bf16[128,256]{1,0:T(8,128)(2,1)S(1)} %fusion.17), channel_id=1, source_target_pairs={{0,3},{1,2},{2,1},{3,0},{4,7},{5,6},{6,5},{7,4},{8,11},{9,10},{10,... | collective-permute-start | bytes 196616 | tf_op jit(solution)/shard_map/ppermute | solution.py:35
  121.5 3.0 %finish_b.1 = (f32[1,256,1024]{2,1,0:T(8,128)}, f32[1,64,64]{2,1,0:T(8,128)S(1)}) custom-call(bf16[2,4,128,256]{3,2,1,0:T(8,128)(2,1)S(1)} %copy-done.14, bf16[2,4,128,256]{3,2,1,0:T(8,128)(2,1)} %collective-permute-done.16.refs_1_, bf16[4,128,256]{2,1,0:T(8,128)(2,1)S(1)} %collective-permute-done.17.refs_2_, ...), custom_call_target="tpu_custom_call" | custom-call | flops 256000000 | bytes 1048576 | tf_op jit(solution)/shard_map/finish_b/pallas_call | solution.py:193
  124.5 3.2 %finish_a1.1 = (f32[1,256,1024]{2,1,0:T(8,128)}, f32[2,64,64]{2,1,0:T(8,128)S(1)}) custom-call(bf16[2,4,256,256]{3,2,1,0:T(8,128)(2,1)S(1)} %copy-done.6, bf16[2,4,256,256]{3,2,1,0:T(8,128)(2,1)S(1)} %collective-permute-done.8.refs_1_, bf16[4,256,256]{2,1,0:T(8,128)(2,1)S(1)} %collective-permute-done.9.refs_2_, ...), custom_call_target="tpu_custom_call", output_to_operand_aliasing={{0}: (13, {})} | custom-call | flops 512000000 | bytes 2097152 | tf_op jit(solution)/shard_map/finish_a1/pallas_call | solution.py:193
  127.7 2.9 %finish_a2.1 = (f32[1,256,1024]{2,1,0:T(8,128)}, f32[1,64,64]{2,1,0:T(8,128)S(1)}) custom-call(bf16[2,4,128,256]{3,2,1,0:T(8,128)(2,1)S(1)} %copy-done.10, bf16[2,4,128,256]{3,2,1,0:T(8,128)(2,1)S(1)} %collective-permute-done.refs_1_, bf16[4,128,256]{2,1,0:T(8,128)(2,1)S(1)} %collective-permute-done.1.refs_2_, ...), custom_call_target="tpu_custom_call", output_to_operand_aliasing={{0}: (13, {})} | custom-call | flops 256000000 | bytes 1048576 | tf_op jit(solution)/shard_map/finish_a2/pallas_call | solution.py:193
  132.1 3.5 %collective-permute-start.25 = (f32[4,64,64]{2,1,0:T(8,128)S(1)}, f32[4,64,64]{2,1,0:T(8,128)S(1)}, u32[]{:S(2)}, u32[]{:S(2)}) collective-permute-start(f32[4,64,64]{2,1,0:T(8,128)S(1)} %add.239), channel_id=1, source_target_pairs={{0,128},{16,144},{32,160},{48,176},{64,192},{80,208},{96,224},{112... | collective-permute-start | bytes 196616 | tf_op jit(solution)/shard_map/ppermute | solution.py:35
  135.6 3.8 %collective-permute-done.25 = f32[4,64,64]{2,1,0:T(8,128)S(1)} collective-permute-done((f32[4,64,64]{2,1,0:T(8,128)S(1)}, f32[4,64,64]{2,1,0:T(8,128)S(1)}, u32[]{:S(2)}, u32[]{:S(2)}) %collective-permute-start.25) | collective-permute-done | bytes 65568 | tf_op jit(solution)/shard_map/ppermute | solution.py:35
  139.5 5.0 %collective-permute-done.26 = f32[4,64,64]{2,1,0:T(8,128)S(1)} collective-permute-done((f32[4,64,64]{2,1,0:T(8,128)S(1)}, f32[4,64,64]{2,1,0:T(8,128)S(1)}, u32[]{:S(2)}, u32[]{:S(2)}) %collective-permute-start.26) | collective-permute-done | bytes 65568 | tf_op jit(solution)/shard_map/ppermute | solution.py:35
  145.3 5.6 %collective-permute-done.27 = f32[4,64,64]{2,1,0:T(8,128)S(1)} collective-permute-done((f32[4,64,64]{2,1,0:T(8,128)S(1)}, f32[4,64,64]{2,1,0:T(8,128)S(1)}, u32[]{:S(2)}, u32[]{:S(2)}) %collective-permute-start.27) | collective-permute-done | bytes 65568 | tf_op jit(solution)/shard_map/ppermute | solution.py:35
  150.9 2.6 %update.1 = bf16[256,1024]{1,0:T(8,128)(2,1)} custom-call(f32[4,64,64]{2,1,0:T(8,128)S(1)} %add.242.refs_0_, f32[64,256]{1,0:T(8,128)S(1)} %copy-done.17), custom_call_target="tpu_custom_call" | custom-call | tf_op jit(solution)/shard_map/update/pallas_call | solution.py:221
  (118 shorter events, 40.5 us)
Async XLA Ops:
  10.3 41.4 %collective-permute-start.20 = (bf16[2,4,128,256]{3,2,1,0:T(8,128)(2,1)}, bf16[2,4,128,256]{3,2,1,0:T(8,128)(2,1)}, u32[]{:S(2)}, u32[]{:S(2)}) collective-permute-start(bf16[2,4,128,256]{3,2,1,0:T(8,128)(2,1)} %get-tuple-element.37), channel_id=1, source_target_pairs={{0,3},{1,2},{2,1},{3,0},{4,7},{5,6},{6,5},{7,4},{8,11},{9,10},{10,... | collective-permute-start | bytes 1572872 | tf_op jit(solution)/shard_map/ppermute | solution.py:35
  16.6 37.5 %collective-permute-start.16 = (bf16[2,4,128,256]{3,2,1,0:T(8,128)(2,1)}, bf16[2,4,128,256]{3,2,1,0:T(8,128)(2,1)}, u32[]{:S(2)}, u32[]{:S(2)}) collective-permute-start(bf16[2,4,128,256]{3,2,1,0:T(8,128)(2,1)} %get-tuple-element.35), channel_id=1, source_target_pairs={{0,1},{1,0},{2,3},{3,2},{4,5},{5,4},{6,7},{7,6},{8,9},{9,8},{10,11... | collective-permute-start | bytes 1572872 | tf_op jit(solution)/shard_map/ppermute | solution.py:35
  24.3 53.0 %collective-permute-start.12 = (bf16[2,4,256,256]{3,2,1,0:T(8,128)(2,1)}, bf16[2,4,256,256]{3,2,1,0:T(8,128)(2,1)S(1)}, u32[]{:S(2)}, u32[]{:S(2)}) collective-permute-start(bf16[2,4,256,256]{3,2,1,0:T(8,128)(2,1)} %get-tuple-element.33), channel_id=1, source_target_pairs={{0,12},{1,13},{2,14},{3,15},{4,8},{5,9},{6,10},{7,11},{8,4},{9,5},... | collective-permute-start | bytes 3145736 | tf_op jit(solution)/shard_map/ppermute | solution.py:35
  24.7 57.5 %collective-permute-start.8 = (bf16[2,4,256,256]{3,2,1,0:T(8,128)(2,1)}, bf16[2,4,256,256]{3,2,1,0:T(8,128)(2,1)S(1)}, u32[]{:S(2)}, u32[]{:S(2)}) collective-permute-start(bf16[2,4,256,256]{3,2,1,0:T(8,128)(2,1)} %get-tuple-element.31), channel_id=1, source_target_pairs={{0,4},{1,5},{2,6},{3,7},{4,0},{5,1},{6,2},{7,3},{8,12},{9,13},{10,... | collective-permute-start | bytes 3145736 | tf_op jit(solution)/shard_map/ppermute | solution.py:35
  30.8 30.6 %collective-permute-start.4 = (bf16[2,4,128,256]{3,2,1,0:T(8,128)(2,1)}, bf16[2,4,128,256]{3,2,1,0:T(8,128)(2,1)}, u32[]{:S(2)}, u32[]{:S(2)}) collective-permute-start(bf16[2,4,128,256]{3,2,1,0:T(8,128)(2,1)} %get-tuple-element.29), channel_id=1, source_target_pairs={{0,12},{1,13},{2,14},{3,15},{4,8},{5,9},{6,10},{7,11},{8,4},{9,5},... | collective-permute-start | bytes 1572872 | tf_op jit(solution)/shard_map/ppermute | solution.py:35
  50.9 70.6 %copy-start.4 = (f32[1,256,1024]{2,1,0:T(8,128)S(1)}, f32[1,256,1024]{2,1,0:T(8,128)}, u32[]{:S(2)}) copy-start(f32[1,256,1024]{2,1,0:T(8,128)} %refs_10_.5) | copy-start | bytes 3145732
  50.9 70.6 %copy-start.17 = (f32[64,256]{1,0:T(8,128)S(1)}, f32[64,256]{1,0:T(8,128)}, u32[]{:S(2)}) copy-start(f32[64,256]{1,0:T(8,128)} %constant.51.clone.refs_12_.refs_1_) | copy-start | bytes 196612
  51.7 51.4 %copy-start.12 = (bf16[2,4,128,256]{3,2,1,0:T(8,128)(2,1)S(1)}, bf16[2,4,128,256]{3,2,1,0:T(8,128)(2,1)}, u32[]{:S(2)}) copy-start(bf16[2,4,128,256]{3,2,1,0:T(8,128)(2,1)} %copy-done.11) | copy-start | bytes 1572868
  51.7 67.8 %copy-start.10 = (bf16[2,4,128,256]{3,2,1,0:T(8,128)(2,1)S(1)}, bf16[2,4,128,256]{3,2,1,0:T(8,128)(2,1)}, u32[]{:S(2)}) copy-start(bf16[2,4,128,256]{3,2,1,0:T(8,128)(2,1)} %copy-done.9) | copy-start | bytes 1572868
  51.7 12.6 %collective-permute-start = (bf16[2,4,128,256]{3,2,1,0:T(8,128)(2,1)}, bf16[2,4,128,256]{3,2,1,0:T(8,128)(2,1)S(1)}, u32[]{:S(2)}, u32[]{:S(2)}) collective-permute-start(bf16[2,4,128,256]{3,2,1,0:T(8,128)(2,1)} %copy-done.20), channel_id=1, source_target_pairs={{0,4},{1,5},{2,6},{3,7},{4,0},{5,1},{6,2},{7,3},{8,12},{9,13},{10,... | collective-permute-start | bytes 1572872 | tf_op jit(solution)/shard_map/ppermute | solution.py:35
  54.1 13.3 %collective-permute-start.21 = (bf16[4,128,256]{2,1,0:T(8,128)(2,1)S(1)}, bf16[4,128,256]{2,1,0:T(8,128)(2,1)S(1)}, u32[]{:S(2)}, u32[]{:S(2)}) collective-permute-start(bf16[4,128,256]{2,1,0:T(8,128)(2,1)S(1)} %fusion.7), channel_id=1, source_target_pairs={{0,1},{1,0},{2,3},{3,2},{4,5},{5,4},{6,7},{7,6},{8,9},{9,8},{10,11... | collective-permute-start | bytes 786440 | tf_op jit(solution)/shard_map/ppermute | solution.py:35
  61.4 11.2 %collective-permute-start.17 = (bf16[4,128,256]{2,1,0:T(8,128)(2,1)S(1)}, bf16[4,128,256]{2,1,0:T(8,128)(2,1)S(1)}, u32[]{:S(2)}, u32[]{:S(2)}) collective-permute-start(bf16[4,128,256]{2,1,0:T(8,128)(2,1)S(1)} %fusion.6), channel_id=1, source_target_pairs={{0,3},{1,2},{2,1},{3,0},{4,7},{5,6},{6,5},{7,4},{8,11},{9,10},{10,... | collective-permute-start | bytes 786440 | tf_op jit(solution)/shard_map/ppermute | solution.py:35
  64.3 10.3 %collective-permute-start.5 = (bf16[4,128,256]{2,1,0:T(8,128)(2,1)S(1)}, bf16[4,128,256]{2,1,0:T(8,128)(2,1)S(1)}, u32[]{:S(2)}, u32[]{:S(2)}) collective-permute-start(bf16[4,128,256]{2,1,0:T(8,128)(2,1)S(1)} %fusion.5), channel_id=1, source_target_pairs={{0,4},{1,5},{2,6},{3,7},{4,0},{5,1},{6,2},{7,3},{8,12},{9,13},{10,... | collective-permute-start | bytes 786440 | tf_op jit(solution)/shard_map/ppermute | solution.py:35
  67.4 8.9 %collective-permute-start.1 = (bf16[4,128,256]{2,1,0:T(8,128)(2,1)S(1)}, bf16[4,128,256]{2,1,0:T(8,128)(2,1)S(1)}, u32[]{:S(2)}, u32[]{:S(2)}) collective-permute-start(bf16[4,128,256]{2,1,0:T(8,128)(2,1)S(1)} %fusion.4), channel_id=1, source_target_pairs={{0,12},{1,13},{2,14},{3,15},{4,8},{5,9},{6,10},{7,11},{8,4},{9,5},... | collective-permute-start | bytes 786440 | tf_op jit(solution)/shard_map/ppermute | solution.py:35
  72.6 12.9 %collective-permute-start.22 = (bf16[2,128,256]{2,1,0:T(8,128)(2,1)S(1)}, bf16[2,128,256]{2,1,0:T(8,128)(2,1)S(1)}, u32[]{:S(2)}, u32[]{:S(2)}) collective-permute-start(bf16[2,128,256]{2,1,0:T(8,128)(2,1)S(1)} %fusion.10), channel_id=1, source_target_pairs={{0,12},{1,13},{2,14},{3,15},{4,8},{5,9},{6,10},{7,11},{8,4},{9,5},... | collective-permute-start | bytes 393224 | tf_op jit(solution)/shard_map/ppermute | solution.py:35
  74.7 14.6 %collective-permute-start.18 = (bf16[2,128,256]{2,1,0:T(8,128)(2,1)S(1)}, bf16[2,128,256]{2,1,0:T(8,128)(2,1)S(1)}, u32[]{:S(2)}, u32[]{:S(2)}) collective-permute-start(bf16[2,128,256]{2,1,0:T(8,128)(2,1)S(1)} %fusion.11), channel_id=1, source_target_pairs={{0,4},{1,5},{2,6},{3,7},{4,0},{5,1},{6,2},{7,3},{8,12},{9,13},{10,... | collective-permute-start | bytes 393224 | tf_op jit(solution)/shard_map/ppermute | solution.py:35
  76.3 25.2 %collective-permute-start.6 = (bf16[2,128,256]{2,1,0:T(8,128)(2,1)S(1)}, bf16[2,128,256]{2,1,0:T(8,128)(2,1)S(1)}, u32[]{:S(2)}, u32[]{:S(2)}) collective-permute-start(bf16[2,128,256]{2,1,0:T(8,128)(2,1)S(1)} %fusion.12), channel_id=1, source_target_pairs={{0,3},{1,2},{2,1},{3,0},{4,7},{5,6},{6,5},{7,4},{8,11},{9,10},{10,... | collective-permute-start | bytes 393224 | tf_op jit(solution)/shard_map/ppermute | solution.py:35
  77.2 39.9 %collective-permute-start.2 = (bf16[2,128,256]{2,1,0:T(8,128)(2,1)S(1)}, bf16[2,128,256]{2,1,0:T(8,128)(2,1)S(1)}, u32[]{:S(2)}, u32[]{:S(2)}) collective-permute-start(bf16[2,128,256]{2,1,0:T(8,128)(2,1)S(1)} %fusion.13), channel_id=1, source_target_pairs={{0,1},{1,0},{2,3},{3,2},{4,5},{5,4},{6,7},{7,6},{8,9},{9,8},{10,11... | collective-permute-start | bytes 393224 | tf_op jit(solution)/shard_map/ppermute | solution.py:35
  82.2 13.1 %collective-permute-start.13 = (bf16[4,256,256]{2,1,0:T(8,128)(2,1)S(1)}, bf16[4,256,256]{2,1,0:T(8,128)(2,1)S(1)}, u32[]{:S(2)}, u32[]{:S(2)}) collective-permute-start(bf16[4,256,256]{2,1,0:T(8,128)(2,1)S(1)} %fusion.1), channel_id=1, source_target_pairs={{0,4},{1,5},{2,6},{3,7},{4,0},{5,1},{6,2},{7,3},{8,12},{9,13},{10,... | collective-permute-start | bytes 1572872 | tf_op jit(solution)/shard_map/ppermute | solution.py:35
  85.5 13.8 %collective-permute-start.9 = (bf16[4,256,256]{2,1,0:T(8,128)(2,1)S(1)}, bf16[4,256,256]{2,1,0:T(8,128)(2,1)S(1)}, u32[]{:S(2)}, u32[]{:S(2)}) collective-permute-start(bf16[4,256,256]{2,1,0:T(8,128)(2,1)S(1)} %fusion), channel_id=1, source_target_pairs={{0,12},{1,13},{2,14},{3,15},{4,8},{5,9},{6,10},{7,11},{8,4},{9,5},... | collective-permute-start | bytes 1572872 | tf_op jit(solution)/shard_map/ppermute | solution.py:35
  89.2 30.3 %collective-permute-start.23 = (bf16[128,256]{1,0:T(8,128)(2,1)S(1)}, bf16[128,256]{1,0:T(8,128)(2,1)S(1)}, u32[]{:S(2)}, u32[]{:S(2)}) collective-permute-start(bf16[128,256]{1,0:T(8,128)(2,1)S(1)} %fusion.14), channel_id=1, source_target_pairs={{0,4},{1,5},{2,6},{3,7},{4,0},{5,1},{6,2},{7,3},{8,12},{9,13},{10,... | collective-permute-start | bytes 196616 | tf_op jit(solution)/shard_map/ppermute | solution.py:35
  95.3 26.2 %collective-permute-start.19 = (bf16[128,256]{1,0:T(8,128)(2,1)S(1)}, bf16[128,256]{1,0:T(8,128)(2,1)S(1)}, u32[]{:S(2)}, u32[]{:S(2)}) collective-permute-start(bf16[128,256]{1,0:T(8,128)(2,1)S(1)} %fusion.15), channel_id=1, source_target_pairs={{0,12},{1,13},{2,14},{3,15},{4,8},{5,9},{6,10},{7,11},{8,4},{9,5},... | collective-permute-start | bytes 196616 | tf_op jit(solution)/shard_map/ppermute | solution.py:35
  99.2 10.5 %collective-permute-start.14 = (bf16[2,256,256]{2,1,0:T(8,128)(2,1)S(1)}, bf16[2,256,256]{2,1,0:T(8,128)(2,1)S(1)}, u32[]{:S(2)}, u32[]{:S(2)}) collective-permute-start(bf16[2,256,256]{2,1,0:T(8,128)(2,1)S(1)} %fusion.2), channel_id=1, source_target_pairs={{0,3},{1,2},{2,1},{3,0},{4,7},{5,6},{6,5},{7,4},{8,11},{9,10},{10,... | collective-permute-start | bytes 786440 | tf_op jit(solution)/shard_map/ppermute | solution.py:35
  101.4 15.6 %collective-permute-start.10 = (bf16[2,256,256]{2,1,0:T(8,128)(2,1)S(1)}, bf16[2,256,256]{2,1,0:T(8,128)(2,1)S(1)}, u32[]{:S(2)}, u32[]{:S(2)}) collective-permute-start(bf16[2,256,256]{2,1,0:T(8,128)(2,1)S(1)} %fusion.3), channel_id=1, source_target_pairs={{0,1},{1,0},{2,3},{3,2},{4,5},{5,4},{6,7},{7,6},{8,9},{9,8},{10,11... | collective-permute-start | bytes 786440 | tf_op jit(solution)/shard_map/ppermute | solution.py:35
  109.7 18.0 %collective-permute-start.7 = (bf16[128,256]{1,0:T(8,128)(2,1)S(1)}, bf16[128,256]{1,0:T(8,128)(2,1)S(1)}, u32[]{:S(2)}, u32[]{:S(2)}) collective-permute-start(bf16[128,256]{1,0:T(8,128)(2,1)S(1)} %fusion.16), channel_id=1, source_target_pairs={{0,1},{1,0},{2,3},{3,2},{4,5},{5,4},{6,7},{7,6},{8,9},{9,8},{10,11... | collective-permute-start | bytes 196616 | tf_op jit(solution)/shard_map/ppermute | solution.py:35
  117.1 7.4 %collective-permute-start.15 = (bf16[256,256]{1,0:T(8,128)(2,1)S(1)}, bf16[256,256]{1,0:T(8,128)(2,1)S(1)}, u32[]{:S(2)}, u32[]{:S(2)}) collective-permute-start(bf16[256,256]{1,0:T(8,128)(2,1)S(1)} %fusion.8), channel_id=1, source_target_pairs={{0,1},{1,0},{2,3},{3,2},{4,5},{5,4},{6,7},{7,6},{8,9},{9,8},{10,11... | collective-permute-start | bytes 393224 | tf_op jit(solution)/shard_map/ppermute | solution.py:35
  117.1 7.3 %collective-permute-start.11 = (bf16[256,256]{1,0:T(8,128)(2,1)S(1)}, bf16[256,256]{1,0:T(8,128)(2,1)S(1)}, u32[]{:S(2)}, u32[]{:S(2)}) collective-permute-start(bf16[256,256]{1,0:T(8,128)(2,1)S(1)} %fusion.9), channel_id=1, source_target_pairs={{0,3},{1,2},{2,1},{3,0},{4,7},{5,6},{6,5},{7,4},{8,11},{9,10},{10,... | collective-permute-start | bytes 393224 | tf_op jit(solution)/shard_map/ppermute | solution.py:35
  119.5 8.2 %collective-permute-start.3 = (bf16[128,256]{1,0:T(8,128)(2,1)S(1)}, bf16[128,256]{1,0:T(8,128)(2,1)S(1)}, u32[]{:S(2)}, u32[]{:S(2)}) collective-permute-start(bf16[128,256]{1,0:T(8,128)(2,1)S(1)} %fusion.17), channel_id=1, source_target_pairs={{0,3},{1,2},{2,1},{3,0},{4,7},{5,6},{6,5},{7,4},{8,11},{9,10},{10,... | collective-permute-start | bytes 196616 | tf_op jit(solution)/shard_map/ppermute | solution.py:35
  130.7 1.4 collective-permute-start.24
  132.1 7.3 %collective-permute-start.25 = (f32[4,64,64]{2,1,0:T(8,128)S(1)}, f32[4,64,64]{2,1,0:T(8,128)S(1)}, u32[]{:S(2)}, u32[]{:S(2)}) collective-permute-start(f32[4,64,64]{2,1,0:T(8,128)S(1)} %add.239), channel_id=1, source_target_pairs={{0,128},{16,144},{32,160},{48,176},{64,192},{80,208},{96,224},{112... | collective-permute-start | bytes 196616 | tf_op jit(solution)/shard_map/ppermute | solution.py:35
  139.4 5.1 %collective-permute-start.26 = (f32[4,64,64]{2,1,0:T(8,128)S(1)}, f32[4,64,64]{2,1,0:T(8,128)S(1)}, u32[]{:S(2)}, u32[]{:S(2)}) collective-permute-start(f32[4,64,64]{2,1,0:T(8,128)S(1)} %add.240), channel_id=1, source_target_pairs={{0,32},{16,48},{32,0},{48,16},{64,96},{80,112},{96,64},{112,80},{1... | collective-permute-start | bytes 196616 | tf_op jit(solution)/shard_map/ppermute | solution.py:35
  144.6 6.3 %collective-permute-start.27 = (f32[4,64,64]{2,1,0:T(8,128)S(1)}, f32[4,64,64]{2,1,0:T(8,128)S(1)}, u32[]{:S(2)}, u32[]{:S(2)}) collective-permute-start(f32[4,64,64]{2,1,0:T(8,128)S(1)} %add.241), channel_id=1, source_target_pairs={{0,96},{16,112},{32,64},{48,80},{64,32},{80,48},{96,0},{112,16},{1... | collective-permute-start | bytes 196616 | tf_op jit(solution)/shard_map/ppermute | solution.py:35
  (22 other events, 223.4 us)

commit v2 on v0

v2 whole, which is shorter than its diff:
```python
import functools
import math

import jax
import jax.numpy as jnp
import numpy as np
from jax import lax
from jax.experimental import pallas as pl
from jax.experimental.pallas import tpu as pltpu
from jax.sharding import PartitionSpec as P

BLOCK = 64
BAND = 32
LOW = 16
DECAY = 0.9
ROWS = 256
CHAINS = (
    (192, (3, 4, 12, 1)),
    (256, (12, 4, 1, 3)),
    (256, (4, 12, 3, 1)),
    (192, (1, 12, 3, 4)),
    (128, (4, 1, 12, 3)),
)
SCHEDULE = (
    (2, 0), (1, 0), (3, 0), (0, 0), (4, 0), (2, 1), (1, 1), (4, 1), (3, 1), (2, 2),
    (0, 1), (1, 2), (3, 2), (4, 2), (0, 2), (2, 3), (4, 3), (1, 3), (0, 3), (3, 3),
)
VMEM = 40 * 1024 * 1024
TERMS_VMEM = 40 * 1024 * 1024
IN_VMEM = pl.BlockSpec(memory_space=pltpu.VMEM)


def low_table():
    freq = np.arange(LOW, dtype=np.float64)[:, None]
    place = np.arange(BLOCK, dtype=np.float64)[None, :]
    factor = np.where(freq == 0, math.sqrt(1.0 / BLOCK), math.sqrt(2.0 / BLOCK))
    table = factor * np.cos(math.pi * (2.0 * place + 1.0) * freq / (2.0 * BLOCK))
    whole = np.kron(np.eye(ROWS // BLOCK), table).astype(np.float32)
    first = whole.astype(jnp.bfloat16)
    second = (whole - first.astype(np.float32)).astype(jnp.bfloat16)
    return np.concatenate([first, second], axis=0)


def swap(value, axis, mask):
    n = lax.axis_size(axis)
    return lax.ppermute(value, axis, [(i, i ^ mask) for i in range(n)])


def digits(offset, masks):
    for index in range(16):
        bits = [(index >> (3 - i)) & 1 for i in range(4)]
        if functools.reduce(lambda a, b: a ^ b, [m * b for m, b in zip(masks, bits)]) == offset:
            return index
    raise ValueError(offset)


def terms_kernel(pos_ref, act_ref, cot_ref, *refs):
    outs = refs[: 2 * len(CHAINS)]
    gt_ref, buf_ref, cot_buf, sem_ref = refs[2 * len(CHAINS) :]
    a, b = pos_ref[0], pos_ref[1]
    width = buf_ref.shape[2]

    def load(ka):
        start = pl.multiple_of((a ^ ka) * width, width)
        return pltpu.make_async_copy(act_ref.at[:, pl.ds(start, width)], buf_ref.at[ka], sem_ref.at[ka])

    cot_copy = pltpu.make_async_copy(cot_ref, cot_buf, sem_ref.at[4])
    cot_copy.start()
    for ka in range(4):
        load(ka).start()
    cot_copy.wait()
    gt_ref[...] = cot_buf[...].T
    for ka in range(4):
        load(ka).wait()
        for kb in range(4):
            offset = pl.multiple_of((b ^ kb) * ROWS, ROWS)
            product = jnp.dot(
                gt_ref[...], buf_ref[ka, :, pl.ds(offset, ROWS)], preferred_element_type=jnp.float32
            ).astype(jnp.bfloat16)
            row = 0
            for c, (ncol, masks) in enumerate(CHAINS):
                index = digits(4 * ka + kb, masks)
                outs[2 * c + (0 if index >= 8 else 1)][index % 8] = product[row : row + ncol]
                row += ncol


def terms(activations, cotangent, pos):
    tokens, width = activations.shape
    shapes = [jax.ShapeDtypeStruct((8, n, ROWS), jnp.bfloat16) for n, _ in CHAINS for _ in range(2)]
    return pl.pallas_call(
        terms_kernel,
        in_specs=[
            pl.BlockSpec(memory_space=pltpu.SMEM),
            pl.BlockSpec(memory_space=pltpu.HBM),
            pl.BlockSpec(memory_space=pltpu.HBM),
        ],
        out_specs=[IN_VMEM] * len(shapes),
        out_shape=shapes,
        scratch_shapes=[
            pltpu.VMEM((cotangent.shape[1], tokens), jnp.bfloat16),
            pltpu.VMEM((4, tokens, width // 4), jnp.bfloat16),
            pltpu.VMEM(cotangent.shape, jnp.bfloat16),
            pltpu.SemaphoreType.DMA((5,)),
        ],
        compiler_params=pltpu.CompilerParams(vmem_limit_bytes=TERMS_VMEM),
        cost_estimate=pl.CostEstimate(
            flops=2 * tokens * width * cotangent.shape[1], bytes_accessed=tokens * width * 2, transcendentals=0
        ),
        name="terms",
    )(pos, activations, cotangent)


def f32(x):
    return x.astype(jnp.float32)


def dot(a, b, dims=((1,), (0,))):
    return lax.dot_general(a, b, (dims, ((), ())), preferred_element_type=jnp.float32)


def split(x):
    first = x.astype(jnp.bfloat16)
    return first, (x - f32(first)).astype(jnp.bfloat16)


def forward(matrix, low):
    first, second = split(matrix)
    both = dot(low, first)
    left = both[:64] + both[64:] + dot(low[:64], second)
    stacked = jnp.concatenate([left[:, c : c + ROWS] for c in range(0, left.shape[1], ROWS)], axis=0)
    first, second = split(stacked)
    both = dot(first, low, ((1,), (1,)))
    return both[:, :64] + both[:, 64:] + dot(second, low[:64], ((1,), (1,)))


def backward(coeff, low):
    first, second = split(coeff)
    right = dot(first, low[:64]) + dot(first, low[64:]) + dot(second, low[:64])
    beside = jnp.concatenate([right[r : r + 64] for r in range(0, right.shape[0], 64)], axis=1)
    first, second = split(beside)
    three = jnp.concatenate([low, low[:64]], axis=0)
    return dot(three, jnp.concatenate([first, first, second], axis=0), ((0,), (0,)))


def add_kernel(size, *refs):
    for i in range(size):
        parts = [f32(ref[size + i]) for ref in refs[:-1]]
        refs[-1][i] = functools.reduce(jnp.add, parts).astype(jnp.bfloat16)


def add(held, size, name):
    _, rows, cols = held[0].shape
    return pl.pallas_call(
        functools.partial(add_kernel, size),
        in_specs=[IN_VMEM] * len(held),
        out_specs=IN_VMEM,
        out_shape=jax.ShapeDtypeStruct((size, rows, cols), jnp.bfloat16),
        compiler_params=pltpu.CompilerParams(vmem_limit_bytes=VMEM),
        cost_estimate=pl.CostEstimate(flops=size * 100000, bytes_accessed=size * rows * 512 * 3, transcendentals=0),
        name=name,
    )(*held)


def coeff_kernel(counts, *refs):
    n = sum(counts)
    mom_ref, band_ref, low_ref, updated_ref, coeff_ref = refs[n:]
    row = lax.broadcasted_iota(jnp.int32, (64, 64), 0) % LOW
    spot = row * BLOCK + lax.broadcasted_iota(jnp.int32, (64, 64), 1) % LOW
    chosen = functools.reduce(jnp.logical_or, [spot == band_ref[i] for i in range(BAND)])
    mask = chosen.astype(jnp.float32)
    rows, at = [], 0
    for count in counts:
        parts = [f32(ref[0]) for ref in refs[at : at + count]]
        rows.append(functools.reduce(jnp.add, parts))
        at += count
    gradient = jnp.concatenate(rows, axis=0)
    turned = [gradient[c : c + ROWS].T for c in range(0, gradient.shape[0], ROWS)]
    updated = DECAY * mom_ref[0] + jnp.concatenate(turned, axis=1)
    updated_ref[...] = updated
    coeff_ref[...] = forward(updated, low_ref[...]) * jnp.concatenate([mask] * len(turned), axis=0)


def coefficients(held, momentum, band, low):
    _, rows, ncol = momentum.shape
    arrays = [a for chain in held for a in chain]
    return pl.pallas_call(
        functools.partial(coeff_kernel, [len(chain) for chain in held]),
        in_specs=[IN_VMEM] * (len(arrays) + 1) + [pl.BlockSpec(memory_space=pltpu.SMEM), IN_VMEM],
        out_specs=[IN_VMEM] * 2,
        out_shape=[
            jax.ShapeDtypeStruct((rows, ncol), jnp.float32),
            jax.ShapeDtypeStruct((ncol // 4, 64), jnp.float32),
        ],
        compiler_params=pltpu.CompilerParams(vmem_limit_bytes=VMEM),
        cost_estimate=pl.CostEstimate(flops=ncol * 1000000, bytes_accessed=ncol * 256 * 8, transcendentals=0),
        name="coefficients",
    )(*arrays, momentum, band, low)


def fresh_kernel(updated_ref, coeff_ref, low_ref, out_ref):
    out_ref[0] = updated_ref[...] - backward(coeff_ref[...], low_ref[...])


def new_momentum(updated, coeffs, low, shape):
    return pl.pallas_call(
        fresh_kernel,
        in_specs=[IN_VMEM] * 3,
        out_shape=jax.ShapeDtypeStruct(shape, jnp.float32),
        compiler_params=pltpu.CompilerParams(vmem_limit_bytes=VMEM),
        cost_estimate=pl.CostEstimate(flops=2000000000, bytes_accessed=2000000, transcendentals=0),
        name="new_momentum",
    )(updated, coeffs, low)


def update_kernel(scale, a_ref, b_ref, c_ref, d_ref, low_ref, out_ref):
    total = (a_ref[...] + b_ref[...]) + (c_ref[...] + d_ref[...])
    out_ref[...] = (backward(total, low_ref[...]) * scale).astype(jnp.bfloat16)


def make_update(parts, low, ncols, scale):
    return pl.pallas_call(
        functools.partial(update_kernel, scale),
        in_specs=[IN_VMEM] * 5,
        out_shape=jax.ShapeDtypeStruct((ROWS, ncols), jnp.bfloat16),
        compiler_params=pltpu.CompilerParams(vmem_limit_bytes=VMEM),
        name="update",
    )(*parts, low)


def per_device(activations, cotangent, momentum, band):
    low = jnp.asarray(low_table())
    me = lax.axis_index("fsdp")
    blocks = terms(activations, cotangent, jnp.stack([me >> 2, me & 3]).astype(jnp.int32))

    held = [[blocks[2 * c + 1]] for c in range(len(CHAINS))]
    before = blocks[0]
    for c, stage in SCHEDULE:
        if stage:
            held[c][-1], before = lax.optimization_barrier((held[c][-1], before))
            send = add(held[c], 8 >> stage, "add%d_%d" % (c, stage))
        else:
            send, before = lax.optimization_barrier((blocks[2 * c], before))
        held[c].append(swap(send, "fsdp", CHAINS[c][1][stage]))
        before = send

    updated, coeffs = coefficients(held, momentum, band, low)
    fresh = new_momentum(updated, coeffs, low, momentum.shape)
    summed = coeffs
    for m in (1, 8):
        summed = summed + swap(summed, "rep", m)
    parts = [summed] + [swap(summed, "rep", m) for m in (2, 4, 6)]
    scale = BLOCK / math.sqrt(BAND * lax.axis_size("rep"))
    update = make_update(parts, low, momentum.shape[2], scale)
    return (fresh, update)


def solution(mesh):
    in_specs = (P(("rep", "fsdp"), None), P(("rep", "fsdp"), None), P("rep", "fsdp", None), P())
    out_specs = (P("rep", "fsdp", None), P("fsdp", None))
    return jax.shard_map(
        per_device, mesh=mesh, in_specs=in_specs, out_specs=out_specs, check_vma=False
    )
```

time: 254 us -> 121 us (0.48)
  waiting for transfers between devices: 124 us -> 53.8 us
  blocking collectives: 54.8 us -> 0 us
  starting transfers between devices: 0.04 us -> 47.3 us
  matrix products: 37.2 us -> 0 us
  local copies, waits for them, and re-layouts: 19 us -> 1.52 us
  Pallas kernels: 0 us -> 17.2 us
  between operations: 14.1 us -> 0.8 us
  other arithmetic: 3.87 us -> 0.11 us
    reduce_scatter x1 -> x0, waiting for transfers between devices: 124 us -> none  [per_device(): lax.psum_scatter(lax.dot_general(activations, cotangent, (((0,), (0,)), (...]
    psum x1 -> x0, blocking collectives: 54.8 us -> none  [per_device(): summed = lax.psum(values, 'rep')]
    ppermute x0 -> x25, waiting for transfers between devices: none -> 53.8 us  [swap(): return lax.ppermute(value, axis, [(i, i ^ mask) for i in range(n)])]
    ppermute x0 -> x25, starting transfers between devices: none -> 47.3 us  [swap(): return lax.ppermute(value, axis, [(i, i ^ mask) for i in range(n)])]
    dot_general x10 -> x0, matrix products: 37.2 us -> none  [the longest x1 14.3 us: per_device(): lax.dot_general(activations, cotangent, (((0,), (0,)), ((), ())), preferr...]
    pallas_call x0 -> x19, Pallas kernels: none -> 17.2 us  [the longest x1 11.6 us: terms(): pl.pallas_call(terms_kernel, in_specs=[pl.BlockSpec(memory_space=pltpu.SM...]
    reshape x5 -> x0, local copies, waits for them, and re-layouts: 12.8 us -> none  [the longest x2 5.3 us: inverse(): grid = grid.reshape(nrows // side, ncols // side, side, side)]
    transpose x1 -> x0, local copies, waits for them, and re-layouts: 2.56 us -> none  [inverse(): back = jnp.einsum('ui,abuv,vj->aibj', table, grid, table, precision=highest)]
  transfers between devices with their start and end apart: 1 -> 25, of which waited for: 1 -> 14; matrix products, arithmetic and copies ran while one was open for 0% -> 0% of each run, Pallas kernels for 0% -> 2%
where the time goes in v2:
time: 121 us
  waiting for transfers between devices  53.8 us (44%)
  starting transfers between devices  47.3 us (39%)
  Pallas kernels  17.2 us (14%)
  local copies, waits for them, and re-layouts  1.52 us (1%)
    ppermute x25, waiting for transfers between devices, swap(): return lax.ppermute(value, axis, [(i, i ^ mask) for i in range(n)])  53.8 us
    ppermute x25, starting transfers between devices, swap(): return lax.ppermute(value, axis, [(i, i ^ mask) for i in range(n)])  47.3 us
    pallas_call x1, Pallas kernels, terms(): pl.pallas_call(terms_kernel, in_specs=[pl.BlockSpec(memory_space=pltpu.SM...  11.6 us
  transfers between devices with their start and end apart: 25, of which 14 were waited for; matrix products, arithmetic and copies ran while one was open for 0% of the time, Pallas kernels for 2%

profile of v2, /device:TPU:6, one launch (start us, length us, event | category | flops | bytes accessed | tf_op | source)
XLA Modules:
  0.0 120.7 jit_solution(13520379568007643518)
XLA Ops:
  0.7 1.5 %copy-done.3 = bf16[896,1024]{1,0:T(8,128)(2,1)S(1)} copy-done((bf16[896,1024]{1,0:T(8,128)(2,1)S(1)}, bf16[896,1024]{1,0:T(8,128)(2,1)}, u32[]{:S(2)}) %copy-start.3) | copy-done | bytes 1835032
  2.2 11.6 %terms.1 = (bf16[8,192,256]{2,1,0:T(8,128)(2,1)S(1)}, bf16[8,192,256]{2,1,0:T(8,128)(2,1)S(1)}, bf16[8,256,256]{2,1,0:T(8,128)(2,1)S(1)}, bf16[8,256,256]{2,1,0:...) custom-call(s32[2]{0:T(128)S(1)} %pad_add_fusion.pos_ref, ...), custom_call_target="tpu_custom_call" | custom-call | flops 7516192768 | bytes 7340032 | tf_op jit(solution)/shard_map/terms/pallas_call | solution.py:90
  14.7 1.5 %collective-permute-start.5 = (bf16[8,256,256]{2,1,0:T(8,128)(2,1)S(1)}, bf16[8,256,256]{2,1,0:T(8,128)(2,1)S(1)}, u32[]{:S(2)}, u32[]{:S(2)}) collective-permute-start(bf16[8,256,256]{2,1,0:T(8,128)(2,1)S(1)} %get-tuple-element.40), channel_id=1, source_target_pairs={{0,12},{1,13},{2,14},{3,15},{4,8},{5,9},{6,10},{7,11},{8,4},{9,5},... | collective-permute-start | bytes 3145736 | tf_op jit(solution)/shard_map/ppermute | solution.py:46
  16.2 2.9 %collective-permute-start.3 = (bf16[8,192,256]{2,1,0:T(8,128)(2,1)S(1)}, bf16[8,192,256]{2,1,0:T(8,128)(2,1)S(1)}, u32[]{:S(2)}, u32[]{:S(2)}) collective-permute-start(bf16[8,192,256]{2,1,0:T(8,128)(2,1)S(1)} %get-tuple-element.41), channel_id=1, source_target_pairs={{0,1},{1,0},{2,3},{3,2},{4,5},{5,4},{6,7},{7,6},{8,9},{9,8},{10,11... | collective-permute-start | bytes 2359304 | tf_op jit(solution)/shard_map/ppermute | solution.py:46
  19.2 4.5 %collective-permute-start = (bf16[8,192,256]{2,1,0:T(8,128)(2,1)S(1)}, bf16[8,192,256]{2,1,0:T(8,128)(2,1)S(1)}, u32[]{:S(2)}, u32[]{:S(2)}) collective-permute-start(bf16[8,192,256]{2,1,0:T(8,128)(2,1)S(1)} %get-tuple-element.42), channel_id=1, source_target_pairs={{0,3},{1,2},{2,1},{3,0},{4,7},{5,6},{6,5},{7,4},{8,11},{9,10},{10,... | collective-permute-start | bytes 2359304 | tf_op jit(solution)/shard_map/ppermute | solution.py:46
  23.7 16.3 %collective-permute-done.1.refs_1_.refs_11_ = bf16[8,256,256]{2,1,0:T(8,128)(2,1)S(1)} collective-permute-done((bf16[8,256,256]{2,1,0:T(8,128)(2,1)S(1)}, bf16[8,256,256]{2,1,0:T(8,128)(2,1)S(1)}, u32[]{:S(2)}, u32[]{:S(2)}) %collective-permute-start.1) | collective-permute-done | bytes 1048608 | tf_op jit(solution)/shard_map/ppermute | solution.py:46
  40.1 2.4 %collective-permute-start.2 = (bf16[4,256,256]{2,1,0:T(8,128)(2,1)S(1)}, bf16[4,256,256]{2,1,0:T(8,128)(2,1)S(1)}, u32[]{:S(2)}, u32[]{:S(2)}) collective-permute-start(bf16[4,256,256]{2,1,0:T(8,128)(2,1)S(1)} %add2_1.1), channel_id=1, source_target_pairs={{0,12},{1,13},{2,14},{3,15},{4,8},{5,9},{6,10},{7,11},{8,4},{9,5},... | collective-permute-start | bytes 1572872 | tf_op jit(solution)/shard_map/ppermute | solution.py:46
  42.7 8.5 %collective-permute-done.4.refs_1_.refs_21_ = bf16[8,128,256]{2,1,0:T(8,128)(2,1)S(1)} collective-permute-done((bf16[8,128,256]{2,1,0:T(8,128)(2,1)S(1)}, bf16[8,128,256]{2,1,0:T(8,128)(2,1)S(1)}, u32[]{:S(2)}, u32[]{:S(2)}) %collective-permute-start.4) | collective-permute-done | bytes 524320 | tf_op jit(solution)/shard_map/ppermute | solution.py:46
  51.3 1.8 %collective-permute-done.3.refs_1_.refs_16_ = bf16[8,192,256]{2,1,0:T(8,128)(2,1)S(1)} collective-permute-done((bf16[8,192,256]{2,1,0:T(8,128)(2,1)S(1)}, bf16[8,192,256]{2,1,0:T(8,128)(2,1)S(1)}, u32[]{:S(2)}, u32[]{:S(2)}) %collective-permute-start.3) | collective-permute-done | bytes 786464 | tf_op jit(solution)/shard_map/ppermute | solution.py:46
  53.2 2.2 %collective-permute-start.8 = (bf16[4,192,256]{2,1,0:T(8,128)(2,1)S(1)}, bf16[4,192,256]{2,1,0:T(8,128)(2,1)S(1)}, u32[]{:S(2)}, u32[]{:S(2)}) collective-permute-start(bf16[4,192,256]{2,1,0:T(8,128)(2,1)S(1)} %add3_1.1), channel_id=1, source_target_pairs={{0,12},{1,13},{2,14},{3,15},{4,8},{5,9},{6,10},{7,11},{8,4},{9,5},... | collective-permute-start | bytes 1179656 | tf_op jit(solution)/shard_map/ppermute | solution.py:46
  57.0 2.0 %collective-permute-start.7 = (bf16[4,128,256]{2,1,0:T(8,128)(2,1)S(1)}, bf16[4,128,256]{2,1,0:T(8,128)(2,1)S(1)}, u32[]{:S(2)}, u32[]{:S(2)}) collective-permute-start(bf16[4,128,256]{2,1,0:T(8,128)(2,1)S(1)} %add4_1.1), channel_id=1, source_target_pairs={{0,1},{1,0},{2,3},{3,2},{4,5},{5,4},{6,7},{7,6},{8,9},{9,8},{10,11... | collective-permute-start | bytes 786440 | tf_op jit(solution)/shard_map/ppermute | solution.py:46
  59.0 3.9 %collective-permute-start.13 = (bf16[2,256,256]{2,1,0:T(8,128)(2,1)S(1)}, bf16[2,256,256]{2,1,0:T(8,128)(2,1)S(1)}, u32[]{:S(2)}, u32[]{:S(2)}) collective-permute-start(bf16[2,256,256]{2,1,0:T(8,128)(2,1)S(1)} %add2_2.1), channel_id=1, source_target_pairs={{0,3},{1,2},{2,1},{3,0},{4,7},{5,6},{6,5},{7,4},{8,11},{9,10},{10,... | collective-permute-start | bytes 786440 | tf_op jit(solution)/shard_map/ppermute | solution.py:46
  63.1 2.8 %collective-permute-start.11 = (bf16[2,256,256]{2,1,0:T(8,128)(2,1)S(1)}, bf16[2,256,256]{2,1,0:T(8,128)(2,1)S(1)}, u32[]{:S(2)}, u32[]{:S(2)}) collective-permute-start(bf16[2,256,256]{2,1,0:T(8,128)(2,1)S(1)} %add1_2.1), channel_id=1, source_target_pairs={{0,1},{1,0},{2,3},{3,2},{4,5},{5,4},{6,7},{7,6},{8,9},{9,8},{10,11... | collective-permute-start | bytes 786440 | tf_op jit(solution)/shard_map/ppermute | solution.py:46
  66.0 3.5 %collective-permute-done.7.refs_2_.refs_22_ = bf16[4,128,256]{2,1,0:T(8,128)(2,1)S(1)} collective-permute-done((bf16[4,128,256]{2,1,0:T(8,128)(2,1)S(1)}, bf16[4,128,256]{2,1,0:T(8,128)(2,1)S(1)}, u32[]{:S(2)}, u32[]{:S(2)}) %collective-permute-start.7) | collective-permute-done | bytes 262176 | tf_op jit(solution)/shard_map/ppermute | solution.py:46
  69.8 2.3 %collective-permute-start.10 = (bf16[2,192,256]{2,1,0:T(8,128)(2,1)S(1)}, bf16[2,192,256]{2,1,0:T(8,128)(2,1)S(1)}, u32[]{:S(2)}, u32[]{:S(2)}) collective-permute-start(bf16[2,192,256]{2,1,0:T(8,128)(2,1)S(1)} %add0_2.1), channel_id=1, source_target_pairs={{0,12},{1,13},{2,14},{3,15},{4,8},{5,9},{6,10},{7,11},{8,4},{9,5},... | collective-permute-start | bytes 589832 | tf_op jit(solution)/shard_map/ppermute | solution.py:46
  72.0 5.7 %collective-permute-start.17 = (bf16[2,192,256]{2,1,0:T(8,128)(2,1)S(1)}, bf16[2,192,256]{2,1,0:T(8,128)(2,1)S(1)}, u32[]{:S(2)}, u32[]{:S(2)}) collective-permute-start(bf16[2,192,256]{2,1,0:T(8,128)(2,1)S(1)} %add3_2.1), channel_id=1, source_target_pairs={{0,3},{1,2},{2,1},{3,0},{4,7},{5,6},{6,5},{7,4},{8,11},{9,10},{10,... | collective-permute-start | bytes 589832 | tf_op jit(solution)/shard_map/ppermute | solution.py:46
  77.7 1.9 %collective-permute-start.12 = (bf16[2,128,256]{2,1,0:T(8,128)(2,1)S(1)}, bf16[2,128,256]{2,1,0:T(8,128)(2,1)S(1)}, u32[]{:S(2)}, u32[]{:S(2)}) collective-permute-start(bf16[2,128,256]{2,1,0:T(8,128)(2,1)S(1)} %add4_2.1), channel_id=1, source_target_pairs={{0,12},{1,13},{2,14},{3,15},{4,8},{5,9},{6,10},{7,11},{8,4},{9,5},... | collective-permute-start | bytes 393224 | tf_op jit(solution)/shard_map/ppermute | solution.py:46
  79.7 4.2 %collective-permute-done.12.refs_3_.refs_23_ = bf16[2,128,256]{2,1,0:T(8,128)(2,1)S(1)} collective-permute-done((bf16[2,128,256]{2,1,0:T(8,128)(2,1)S(1)}, bf16[2,128,256]{2,1,0:T(8,128)(2,1)S(1)}, u32[]{:S(2)}, u32[]{:S(2)}) %collective-permute-start.12) | collective-permute-done | bytes 131104 | tf_op jit(solution)/shard_map/ppermute | solution.py:46
  84.0 3.2 %collective-permute-start.15 = (bf16[1,256,256]{2,1,0:T(8,128)(2,1)S(1)}, bf16[1,256,256]{2,1,0:T(8,128)(2,1)S(1)}, u32[]{:S(2)}, u32[]{:S(2)}) collective-permute-start(bf16[1,256,256]{2,1,0:T(8,128)(2,1)S(1)} %add1_3.1), channel_id=1, source_target_pairs={{0,3},{1,2},{2,1},{3,0},{4,7},{5,6},{6,5},{7,4},{8,11},{9,10},{10,... | collective-permute-start | bytes 393224 | tf_op jit(solution)/shard_map/ppermute | solution.py:46
  87.2 3.5 %collective-permute-start.16 = (bf16[1,256,256]{2,1,0:T(8,128)(2,1)S(1)}, bf16[1,256,256]{2,1,0:T(8,128)(2,1)S(1)}, u32[]{:S(2)}, u32[]{:S(2)}) collective-permute-start(bf16[1,256,256]{2,1,0:T(8,128)(2,1)S(1)} %add2_3.1), channel_id=1, source_target_pairs={{0,1},{1,0},{2,3},{3,2},{4,5},{5,4},{6,7},{7,6},{8,9},{9,8},{10,11... | collective-permute-start | bytes 393224 | tf_op jit(solution)/shard_map/ppermute | solution.py:46
  91.2 2.3 %collective-permute-start.19 = (bf16[1,128,256]{2,1,0:T(8,128)(2,1)S(1)}, bf16[1,128,256]{2,1,0:T(8,128)(2,1)S(1)}, u32[]{:S(2)}, u32[]{:S(2)}) collective-permute-start(bf16[1,128,256]{2,1,0:T(8,128)(2,1)S(1)} %add4_3.1), channel_id=1, source_target_pairs={{0,3},{1,2},{2,1},{3,0},{4,7},{5,6},{6,5},{7,4},{8,11},{9,10},{10,... | collective-permute-start | bytes 196616 | tf_op jit(solution)/shard_map/ppermute | solution.py:46
  93.5 4.3 %collective-permute-done.19.refs_24_ = bf16[1,128,256]{2,1,0:T(8,128)(2,1)S(1)} collective-permute-done((bf16[1,128,256]{2,1,0:T(8,128)(2,1)S(1)}, bf16[1,128,256]{2,1,0:T(8,128)(2,1)S(1)}, u32[]{:S(2)}, u32[]{:S(2)}) %collective-permute-start.19) | collective-permute-done | bytes 65568 | tf_op jit(solution)/shard_map/ppermute | solution.py:46
  97.8 1.4 %collective-permute-done.16.refs_14_ = bf16[1,256,256]{2,1,0:T(8,128)(2,1)S(1)} collective-permute-done((bf16[1,256,256]{2,1,0:T(8,128)(2,1)S(1)}, bf16[1,256,256]{2,1,0:T(8,128)(2,1)S(1)}, u32[]{:S(2)}, u32[]{:S(2)}) %collective-permute-start.16) | collective-permute-done | bytes 131104 | tf_op jit(solution)/shard_map/ppermute | solution.py:46
  99.2 1.1 collective-permute-done.14.refs_4_
  100.2 1.5 %coefficients.1 = (f32[256,1024]{1,0:T(8,128)S(1)}, f32[256,64]{1,0:T(8,128)S(1)}) custom-call(bf16[8,192,256]{2,1,0:T(8,128)(2,1)S(1)} %get-tuple-element.34.refs_0_, bf16[8,192,256]{2,1,0:T(8,128)(2,1)S(1)} %collective-permute-done.refs_1_, bf16[4,192,256]{2,1,0:T(8,128)(2,1)S(1)} %collective-permute-done.6.refs_2_, ...), custom_call_target="tpu_custom_call" | custom-call | flops 1024000000 | bytes 2097152 | tf_op jit(solution)/shard_map/coefficients/pallas_call | solution.py:186
  101.8 1.3 %collective-permute-done.20 = f32[256,64]{1,0:T(8,128)S(1)} collective-permute-done((f32[256,64]{1,0:T(8,128)S(1)}, f32[256,64]{1,0:T(8,128)S(1)}, u32[]{:S(2)}, u32[]{:S(2)}) %collective-permute-start.20) | collective-permute-done | bytes 65568 | tf_op jit(solution)/shard_map/ppermute | solution.py:46
  103.3 5.5 %collective-permute-done.21 = f32[256,64]{1,0:T(8,128)S(1)} collective-permute-done((f32[256,64]{1,0:T(8,128)S(1)}, f32[256,64]{1,0:T(8,128)S(1)}, u32[]{:S(2)}, u32[]{:S(2)}) %collective-permute-start.21) | collective-permute-done | bytes 65568 | tf_op jit(solution)/shard_map/ppermute | solution.py:46
  108.9 3.1 %collective-permute-start.24 = (f32[256,64]{1,0:T(8,128)S(1)}, f32[256,64]{1,0:T(8,128)S(1)}, u32[]{:S(2)}, u32[]{:S(2)}) collective-permute-start(f32[256,64]{1,0:T(8,128)S(1)} %add.7.a_ref), channel_id=1, source_target_pairs={{0,96},{16,112},{32,64},{48,80},{64,32},{80,48},{96,0},{112,16},{1... | collective-permute-start | bytes 196616 | tf_op jit(solution)/shard_map/ppermute | solution.py:46
  113.0 1.6 %new_momentum.1 = f32[1,256,1024]{2,1,0:T(8,128)} custom-call(f32[256,1024]{1,0:T(8,128)S(1)} %get-tuple-element.64.updated_ref, f32[256,64]{1,0:T(8,128)S(1)} %get-tuple-element.65.coeff_ref, bf16[128,256]{1,0:T(8,128)(2,1)S(1)} %copy-done.1), custom_call_target="tpu_custom_call" | custom-call | flops 2000000000 | bytes 2000000 | tf_op jit(solution)/shard_map/new_momentum/pallas_call | solution.py:205
  114.6 2.4 %collective-permute-done.24.d_ref = f32[256,64]{1,0:T(8,128)S(1)} collective-permute-done((f32[256,64]{1,0:T(8,128)S(1)}, f32[256,64]{1,0:T(8,128)S(1)}, u32[]{:S(2)}, u32[]{:S(2)}) %collective-permute-start.24) | collective-permute-done | bytes 65568 | tf_op jit(solution)/shard_map/ppermute | solution.py:46
  117.0 2.3 %collective-permute-done.23.c_ref = f32[256,64]{1,0:T(8,128)S(1)} collective-permute-done((f32[256,64]{1,0:T(8,128)S(1)}, f32[256,64]{1,0:T(8,128)S(1)}, u32[]{:S(2)}, u32[]{:S(2)}) %collective-permute-start.23) | collective-permute-done | bytes 65568 | tf_op jit(solution)/shard_map/ppermute | solution.py:46
  119.3 1.4 %update.1 = bf16[256,1024]{1,0:T(8,128)(2,1)} custom-call(f32[256,64]{1,0:T(8,128)S(1)} %add.7.a_ref, f32[256,64]{1,0:T(8,128)S(1)} %collective-permute-done.22.b_ref, f32[256,64]{1,0:T(8,128)S(1)} %collective-permute-done.23.c_ref, f32[256,64]{1,0:T(8,128)S(1)} %collective-permute-done.24.d_ref, bf16[128,256]{1,0:T(8,128)(2,1)S(1)} %copy-done.1), custom_call_target="tpu_custom_call" | custom-call | tf_op jit(solution)/shard_map/update/pallas_call | solution.py:221
  (48 shorter events, 5.6 us)
Async XLA Ops:
  0.7 1.5 %copy-start.3 = (bf16[896,1024]{1,0:T(8,128)(2,1)S(1)}, bf16[896,1024]{1,0:T(8,128)(2,1)}, u32[]{:S(2)}) copy-start(bf16[896,1024]{1,0:T(8,128)(2,1)} %cot_ref.1) | copy-start | bytes 5505028
  13.8 26.1 %collective-permute-start.1 = (bf16[8,256,256]{2,1,0:T(8,128)(2,1)S(1)}, bf16[8,256,256]{2,1,0:T(8,128)(2,1)S(1)}, u32[]{:S(2)}, u32[]{:S(2)}) collective-permute-start(bf16[8,256,256]{2,1,0:T(8,128)(2,1)S(1)} %get-tuple-element.39), channel_id=1, source_target_pairs={{0,4},{1,5},{2,6},{3,7},{4,0},{5,1},{6,2},{7,3},{8,12},{9,13},{10,... | collective-permute-start | bytes 3145736 | tf_op jit(solution)/shard_map/ppermute | solution.py:46
  14.7 27.7 %collective-permute-start.5 = (bf16[8,256,256]{2,1,0:T(8,128)(2,1)S(1)}, bf16[8,256,256]{2,1,0:T(8,128)(2,1)S(1)}, u32[]{:S(2)}, u32[]{:S(2)}) collective-permute-start(bf16[8,256,256]{2,1,0:T(8,128)(2,1)S(1)} %get-tuple-element.40), channel_id=1, source_target_pairs={{0,12},{1,13},{2,14},{3,15},{4,8},{5,9},{6,10},{7,11},{8,4},{9,5},... | collective-permute-start | bytes 3145736 | tf_op jit(solution)/shard_map/ppermute | solution.py:46
  16.2 36.9 %collective-permute-start.3 = (bf16[8,192,256]{2,1,0:T(8,128)(2,1)S(1)}, bf16[8,192,256]{2,1,0:T(8,128)(2,1)S(1)}, u32[]{:S(2)}, u32[]{:S(2)}) collective-permute-start(bf16[8,192,256]{2,1,0:T(8,128)(2,1)S(1)} %get-tuple-element.41), channel_id=1, source_target_pairs={{0,1},{1,0},{2,3},{3,2},{4,5},{5,4},{6,7},{7,6},{8,9},{9,8},{10,11... | collective-permute-start | bytes 2359304 | tf_op jit(solution)/shard_map/ppermute | solution.py:46
  19.2 37.3 %collective-permute-start = (bf16[8,192,256]{2,1,0:T(8,128)(2,1)S(1)}, bf16[8,192,256]{2,1,0:T(8,128)(2,1)S(1)}, u32[]{:S(2)}, u32[]{:S(2)}) collective-permute-start(bf16[8,192,256]{2,1,0:T(8,128)(2,1)S(1)} %get-tuple-element.42), channel_id=1, source_target_pairs={{0,3},{1,2},{2,1},{3,0},{4,7},{5,6},{6,5},{7,4},{8,11},{9,10},{10,... | collective-permute-start | bytes 2359304 | tf_op jit(solution)/shard_map/ppermute | solution.py:46
  23.6 27.6 %collective-permute-start.4 = (bf16[8,128,256]{2,1,0:T(8,128)(2,1)S(1)}, bf16[8,128,256]{2,1,0:T(8,128)(2,1)S(1)}, u32[]{:S(2)}, u32[]{:S(2)}) collective-permute-start(bf16[8,128,256]{2,1,0:T(8,128)(2,1)S(1)} %get-tuple-element.45), channel_id=1, source_target_pairs={{0,4},{1,5},{2,6},{3,7},{4,0},{5,1},{6,2},{7,3},{8,12},{9,13},{10,... | collective-permute-start | bytes 1572872 | tf_op jit(solution)/shard_map/ppermute | solution.py:46
  40.1 15.3 %collective-permute-start.2 = (bf16[4,256,256]{2,1,0:T(8,128)(2,1)S(1)}, bf16[4,256,256]{2,1,0:T(8,128)(2,1)S(1)}, u32[]{:S(2)}, u32[]{:S(2)}) collective-permute-start(bf16[4,256,256]{2,1,0:T(8,128)(2,1)S(1)} %add2_1.1), channel_id=1, source_target_pairs={{0,12},{1,13},{2,14},{3,15},{4,8},{5,9},{6,10},{7,11},{8,4},{9,5},... | collective-permute-start | bytes 1572872 | tf_op jit(solution)/shard_map/ppermute | solution.py:46
  42.6 20.4 %collective-permute-start.9 = (bf16[4,256,256]{2,1,0:T(8,128)(2,1)S(1)}, bf16[4,256,256]{2,1,0:T(8,128)(2,1)S(1)}, u32[]{:S(2)}, u32[]{:S(2)}) collective-permute-start(bf16[4,256,256]{2,1,0:T(8,128)(2,1)S(1)} %add1_1.1), channel_id=1, source_target_pairs={{0,4},{1,5},{2,6},{3,7},{4,0},{5,1},{6,2},{7,3},{8,12},{9,13},{10,... | collective-permute-start | bytes 1572872 | tf_op jit(solution)/shard_map/ppermute | solution.py:46
  53.2 12.7 %collective-permute-start.8 = (bf16[4,192,256]{2,1,0:T(8,128)(2,1)S(1)}, bf16[4,192,256]{2,1,0:T(8,128)(2,1)S(1)}, u32[]{:S(2)}, u32[]{:S(2)}) collective-permute-start(bf16[4,192,256]{2,1,0:T(8,128)(2,1)S(1)} %add3_1.1), channel_id=1, source_target_pairs={{0,12},{1,13},{2,14},{3,15},{4,8},{5,9},{6,10},{7,11},{8,4},{9,5},... | collective-permute-start | bytes 1179656 | tf_op jit(solution)/shard_map/ppermute | solution.py:46
  56.6 13.1 %collective-permute-start.6 = (bf16[4,192,256]{2,1,0:T(8,128)(2,1)S(1)}, bf16[4,192,256]{2,1,0:T(8,128)(2,1)S(1)}, u32[]{:S(2)}, u32[]{:S(2)}) collective-permute-start(bf16[4,192,256]{2,1,0:T(8,128)(2,1)S(1)} %add0_1.1), channel_id=1, source_target_pairs={{0,4},{1,5},{2,6},{3,7},{4,0},{5,1},{6,2},{7,3},{8,12},{9,13},{10,... | collective-permute-start | bytes 1179656 | tf_op jit(solution)/shard_map/ppermute | solution.py:46
  57.0 12.4 %collective-permute-start.7 = (bf16[4,128,256]{2,1,0:T(8,128)(2,1)S(1)}, bf16[4,128,256]{2,1,0:T(8,128)(2,1)S(1)}, u32[]{:S(2)}, u32[]{:S(2)}) collective-permute-start(bf16[4,128,256]{2,1,0:T(8,128)(2,1)S(1)} %add4_1.1), channel_id=1, source_target_pairs={{0,1},{1,0},{2,3},{3,2},{4,5},{5,4},{6,7},{7,6},{8,9},{9,8},{10,11... | collective-permute-start | bytes 786440 | tf_op jit(solution)/shard_map/ppermute | solution.py:46
  59.0 20.6 %collective-permute-start.13 = (bf16[2,256,256]{2,1,0:T(8,128)(2,1)S(1)}, bf16[2,256,256]{2,1,0:T(8,128)(2,1)S(1)}, u32[]{:S(2)}, u32[]{:S(2)}) collective-permute-start(bf16[2,256,256]{2,1,0:T(8,128)(2,1)S(1)} %add2_2.1), channel_id=1, source_target_pairs={{0,3},{1,2},{2,1},{3,0},{4,7},{5,6},{6,5},{7,4},{8,11},{9,10},{10,... | collective-permute-start | bytes 786440 | tf_op jit(solution)/shard_map/ppermute | solution.py:46
  63.1 20.8 %collective-permute-start.11 = (bf16[2,256,256]{2,1,0:T(8,128)(2,1)S(1)}, bf16[2,256,256]{2,1,0:T(8,128)(2,1)S(1)}, u32[]{:S(2)}, u32[]{:S(2)}) collective-permute-start(bf16[2,256,256]{2,1,0:T(8,128)(2,1)S(1)} %add1_2.1), channel_id=1, source_target_pairs={{0,1},{1,0},{2,3},{3,2},{4,5},{5,4},{6,7},{7,6},{8,9},{9,8},{10,11... | collective-permute-start | bytes 786440 | tf_op jit(solution)/shard_map/ppermute | solution.py:46
  69.5 30.7 %copy-start = (f32[1,256,1024]{2,1,0:T(8,128)S(1)}, f32[1,256,1024]{2,1,0:T(8,128)}, u32[]{:S(2)}) copy-start(f32[1,256,1024]{2,1,0:T(8,128)} %refs_25_.1) | copy-start | bytes 3145732
  69.5 30.7 %copy-start.1 = (bf16[128,256]{1,0:T(8,128)(2,1)S(1)}, bf16[128,256]{1,0:T(8,128)(2,1)}, u32[]{:S(2)}) copy-start(bf16[128,256]{1,0:T(8,128)(2,1)} %constant.10.clone.refs_27_.low_ref) | copy-start | bytes 196612
  69.5 30.7 %copy-start.2 = (s32[32]{0:T(128)S(1)}, s32[32]{0:T(128)}, u32[]{:S(2)}) copy-start(s32[32]{0:T(128)} %refs_26_.1) | copy-start | bytes 388
  69.8 20.9 %collective-permute-start.10 = (bf16[2,192,256]{2,1,0:T(8,128)(2,1)S(1)}, bf16[2,192,256]{2,1,0:T(8,128)(2,1)S(1)}, u32[]{:S(2)}, u32[]{:S(2)}) collective-permute-start(bf16[2,192,256]{2,1,0:T(8,128)(2,1)S(1)} %add0_2.1), channel_id=1, source_target_pairs={{0,12},{1,13},{2,14},{3,15},{4,8},{5,9},{6,10},{7,11},{8,4},{9,5},... | collective-permute-start | bytes 589832 | tf_op jit(solution)/shard_map/ppermute | solution.py:46
  72.0 18.8 %collective-permute-start.17 = (bf16[2,192,256]{2,1,0:T(8,128)(2,1)S(1)}, bf16[2,192,256]{2,1,0:T(8,128)(2,1)S(1)}, u32[]{:S(2)}, u32[]{:S(2)}) collective-permute-start(bf16[2,192,256]{2,1,0:T(8,128)(2,1)S(1)} %add3_2.1), channel_id=1, source_target_pairs={{0,3},{1,2},{2,1},{3,0},{4,7},{5,6},{6,5},{7,4},{8,11},{9,10},{10,... | collective-permute-start | bytes 589832 | tf_op jit(solution)/shard_map/ppermute | solution.py:46
  77.7 6.2 %collective-permute-start.12 = (bf16[2,128,256]{2,1,0:T(8,128)(2,1)S(1)}, bf16[2,128,256]{2,1,0:T(8,128)(2,1)S(1)}, u32[]{:S(2)}, u32[]{:S(2)}) collective-permute-start(bf16[2,128,256]{2,1,0:T(8,128)(2,1)S(1)} %add4_2.1), channel_id=1, source_target_pairs={{0,12},{1,13},{2,14},{3,15},{4,8},{5,9},{6,10},{7,11},{8,4},{9,5},... | collective-permute-start | bytes 393224 | tf_op jit(solution)/shard_map/ppermute | solution.py:46
  84.0 13.8 %collective-permute-start.15 = (bf16[1,256,256]{2,1,0:T(8,128)(2,1)S(1)}, bf16[1,256,256]{2,1,0:T(8,128)(2,1)S(1)}, u32[]{:S(2)}, u32[]{:S(2)}) collective-permute-start(bf16[1,256,256]{2,1,0:T(8,128)(2,1)S(1)} %add1_3.1), channel_id=1, source_target_pairs={{0,3},{1,2},{2,1},{3,0},{4,7},{5,6},{6,5},{7,4},{8,11},{9,10},{10,... | collective-permute-start | bytes 393224 | tf_op jit(solution)/shard_map/ppermute | solution.py:46
  87.2 12.0 %collective-permute-start.16 = (bf16[1,256,256]{2,1,0:T(8,128)(2,1)S(1)}, bf16[1,256,256]{2,1,0:T(8,128)(2,1)S(1)}, u32[]{:S(2)}, u32[]{:S(2)}) collective-permute-start(bf16[1,256,256]{2,1,0:T(8,128)(2,1)S(1)} %add2_3.1), channel_id=1, source_target_pairs={{0,1},{1,0},{2,3},{3,2},{4,5},{5,4},{6,7},{7,6},{8,9},{9,8},{10,11... | collective-permute-start | bytes 393224 | tf_op jit(solution)/shard_map/ppermute | solution.py:46
  90.9 8.3 %collective-permute-start.18 = (bf16[1,192,256]{2,1,0:T(8,128)(2,1)S(1)}, bf16[1,192,256]{2,1,0:T(8,128)(2,1)S(1)}, u32[]{:S(2)}, u32[]{:S(2)}) collective-permute-start(bf16[1,192,256]{2,1,0:T(8,128)(2,1)S(1)} %add3_3.1), channel_id=1, source_target_pairs={{0,4},{1,5},{2,6},{3,7},{4,0},{5,1},{6,2},{7,3},{8,12},{9,13},{10,... | collective-permute-start | bytes 294920 | tf_op jit(solution)/shard_map/ppermute | solution.py:46
  91.2 9.1 %collective-permute-start.14 = (bf16[1,192,256]{2,1,0:T(8,128)(2,1)S(1)}, bf16[1,192,256]{2,1,0:T(8,128)(2,1)S(1)}, u32[]{:S(2)}, u32[]{:S(2)}) collective-permute-start(bf16[1,192,256]{2,1,0:T(8,128)(2,1)S(1)} %add0_3.1), channel_id=1, source_target_pairs={{0,1},{1,0},{2,3},{3,2},{4,5},{5,4},{6,7},{7,6},{8,9},{9,8},{10,11... | collective-permute-start | bytes 294920 | tf_op jit(solution)/shard_map/ppermute | solution.py:46
  91.2 6.6 %collective-permute-start.19 = (bf16[1,128,256]{2,1,0:T(8,128)(2,1)S(1)}, bf16[1,128,256]{2,1,0:T(8,128)(2,1)S(1)}, u32[]{:S(2)}, u32[]{:S(2)}) collective-permute-start(bf16[1,128,256]{2,1,0:T(8,128)(2,1)S(1)} %add4_3.1), channel_id=1, source_target_pairs={{0,3},{1,2},{2,1},{3,0},{4,7},{5,6},{6,5},{7,4},{8,11},{9,10},{10,... | collective-permute-start | bytes 196616 | tf_op jit(solution)/shard_map/ppermute | solution.py:46
  101.7 1.4 %collective-permute-start.20 = (f32[256,64]{1,0:T(8,128)S(1)}, f32[256,64]{1,0:T(8,128)S(1)}, u32[]{:S(2)}, u32[]{:S(2)}) collective-permute-start(f32[256,64]{1,0:T(8,128)S(1)} %get-tuple-element.65.coeff_ref), channel_id=1, source_target_pairs={{0,16},{16,0},{32,48},{48,32},{64,80},{80,64},{96,112},{112,96},{1... | collective-permute-start | bytes 196616 | tf_op jit(solution)/shard_map/ppermute | solution.py:46
  103.2 5.6 %collective-permute-start.21 = (f32[256,64]{1,0:T(8,128)S(1)}, f32[256,64]{1,0:T(8,128)S(1)}, u32[]{:S(2)}, u32[]{:S(2)}) collective-permute-start(f32[256,64]{1,0:T(8,128)S(1)} %add.6), channel_id=1, source_target_pairs={{0,128},{16,144},{32,160},{48,176},{64,192},{80,208},{96,224},{112... | collective-permute-start | bytes 196616 | tf_op jit(solution)/shard_map/ppermute | solution.py:46
  108.9 8.2 %collective-permute-start.24 = (f32[256,64]{1,0:T(8,128)S(1)}, f32[256,64]{1,0:T(8,128)S(1)}, u32[]{:S(2)}, u32[]{:S(2)}) collective-permute-start(f32[256,64]{1,0:T(8,128)S(1)} %add.7.a_ref), channel_id=1, source_target_pairs={{0,96},{16,112},{32,64},{48,80},{64,32},{80,48},{96,0},{112,16},{1... | collective-permute-start | bytes 196616 | tf_op jit(solution)/shard_map/ppermute | solution.py:46
  112.0 7.4 %collective-permute-start.23 = (f32[256,64]{1,0:T(8,128)S(1)}, f32[256,64]{1,0:T(8,128)S(1)}, u32[]{:S(2)}, u32[]{:S(2)}) collective-permute-start(f32[256,64]{1,0:T(8,128)S(1)} %add.7.a_ref), channel_id=1, source_target_pairs={{0,64},{16,80},{32,96},{48,112},{64,0},{80,16},{96,32},{112,48},{1... | collective-permute-start | bytes 196616 | tf_op jit(solution)/shard_map/ppermute | solution.py:46
  112.6 6.7 %collective-permute-start.22 = (f32[256,64]{1,0:T(8,128)S(1)}, f32[256,64]{1,0:T(8,128)S(1)}, u32[]{:S(2)}, u32[]{:S(2)}) collective-permute-start(f32[256,64]{1,0:T(8,128)S(1)} %add.7.a_ref), channel_id=1, source_target_pairs={{0,32},{16,48},{32,0},{48,16},{64,96},{80,112},{96,64},{112,80},{1... | collective-permute-start | bytes 196616 | tf_op jit(solution)/shard_map/ppermute | solution.py:46

commit v3 on v2

--- a/solution.py
+++ b/solution.py
@@ -15,18 +15,18 @@
 DECAY = 0.9
 ROWS = 256
 CHAINS = (
-    (192, (3, 4, 12, 1)),
     (256, (12, 4, 1, 3)),
+    (128, (4, 12, 1, 3)),
+    (192, (3, 12, 4, 1)),
+    (192, (1, 4, 3, 12)),
     (256, (4, 12, 3, 1)),
-    (192, (1, 12, 3, 4)),
-    (128, (4, 1, 12, 3)),
 )
 SCHEDULE = (
-    (2, 0), (1, 0), (3, 0), (0, 0), (4, 0), (2, 1), (1, 1), (4, 1), (3, 1), (2, 2),
-    (0, 1), (1, 2), (3, 2), (4, 2), (0, 2), (2, 3), (4, 3), (1, 3), (0, 3), (3, 3),
+    (4, 0), (2, 0), (3, 0), (0, 0), (4, 1), (0, 1), (2, 1), (1, 0), (1, 1), (3, 1),
+    (4, 2), (0, 2), (2, 2), (3, 2), (4, 3), (1, 2), (2, 3), (0, 3), (1, 3), (3, 3),
 )
 VMEM = 40 * 1024 * 1024
-TERMS_VMEM = 40 * 1024 * 1024
+TERMS_VMEM = 50 * 1024 * 1024
 IN_VMEM = pl.BlockSpec(memory_space=pltpu.VMEM)
 
 
@@ -54,11 +54,12 @@
     raise ValueError(offset)
 
 
-def terms_kernel(pos_ref, act_ref, cot_ref, *refs):
-    outs = refs[: 2 * len(CHAINS)]
-    gt_ref, buf_ref, cot_buf, sem_ref = refs[2 * len(CHAINS) :]
+def terms_kernel(kept, pos_ref, act_ref, cot_ref, *refs):
+    outs = refs[: len(CHAINS)]
+    gt_ref, buf_ref, cot_buf, sem_ref = refs[len(CHAINS) :]
     a, b = pos_ref[0], pos_ref[1]
     width = buf_ref.shape[2]
+    order = (0, 3, 1, 2) if kept else (2, 1, 3, 0)
 
     def load(ka):
         start = pl.multiple_of((a ^ ka) * width, width)
@@ -66,29 +67,39 @@
 
     cot_copy = pltpu.make_async_copy(cot_ref, cot_buf, sem_ref.at[4])
     cot_copy.start()
-    for ka in range(4):
+    for ka in order:
         load(ka).start()
     cot_copy.wait()
     gt_ref[...] = cot_buf[...].T
-    for ka in range(4):
+    for ka in order:
         load(ka).wait()
         for kb in range(4):
             offset = pl.multiple_of((b ^ kb) * ROWS, ROWS)
-            product = jnp.dot(
-                gt_ref[...], buf_ref[ka, :, pl.ds(offset, ROWS)], preferred_element_type=jnp.float32
-            ).astype(jnp.bfloat16)
-            row = 0
+            runs, row = [], 0
             for c, (ncol, masks) in enumerate(CHAINS):
                 index = digits(4 * ka + kb, masks)
-                outs[2 * c + (0 if index >= 8 else 1)][index % 8] = product[row : row + ncol]
+                if (index < 8) == kept:
+                    if runs and runs[-1][1] == row:
+                        runs[-1][1] += ncol
+                    else:
+                        runs.append([row, row + ncol, []])
+                    runs[-1][2].append((c, index % 8, ncol))
                 row += ncol
-
-
-def terms(activations, cotangent, pos):
+            for first, last, members in runs:
+                product = jnp.dot(
+                    gt_ref[first:last, :], buf_ref[ka, :, pl.ds(offset, ROWS)], preferred_element_type=jnp.float32
+                ).astype(jnp.bfloat16)
+                at = 0
+                for c, index, ncol in members:
+                    outs[c][index] = product[at : at + ncol]
+                    at += ncol
+
+
+def terms(activations, cotangent, pos, kept):
     tokens, width = activations.shape
-    shapes = [jax.ShapeDtypeStruct((8, n, ROWS), jnp.bfloat16) for n, _ in CHAINS for _ in range(2)]
-    return pl.pallas_call(
-        terms_kernel,
+    shapes = [jax.ShapeDtypeStruct((8, n, ROWS), jnp.bfloat16) for n, _ in CHAINS]
+    return pl.pallas_call(
+        functools.partial(terms_kernel, kept),
         in_specs=[
             pl.BlockSpec(memory_space=pltpu.SMEM),
             pl.BlockSpec(memory_space=pltpu.HBM),
@@ -102,11 +113,11 @@
             pltpu.VMEM(cotangent.shape, jnp.bfloat16),
             pltpu.SemaphoreType.DMA((5,)),
         ],
-        compiler_params=pltpu.CompilerParams(vmem_limit_bytes=TERMS_VMEM),
+        compiler_params=pltpu.CompilerParams(vmem_limit_bytes=(46 if kept else 50) * 2**20),
         cost_estimate=pl.CostEstimate(
-            flops=2 * tokens * width * cotangent.shape[1], bytes_accessed=tokens * width * 2, transcendentals=0
+            flops=tokens * width * cotangent.shape[1], bytes_accessed=tokens * width * 2, transcendentals=0
         ),
-        name="terms",
+        name="terms_kept" if kept else "terms_sent",
     )(pos, activations, cotangent)
 
 
@@ -130,11 +141,13 @@
     stacked = jnp.concatenate([left[:, c : c + ROWS] for c in range(0, left.shape[1], ROWS)], axis=0)
     first, second = split(stacked)
     both = dot(first, low, ((1,), (1,)))
-    return both[:, :64] + both[:, 64:] + dot(second, low[:64], ((1,), (1,)))
+    coeff = both[:, :64] + both[:, 64:] + dot(second, low[:64], ((1,), (1,)))
+    half = coeff.shape[0] // 2
+    return jnp.concatenate([coeff[:half], coeff[half:]], axis=1)
 
 
 def backward(coeff, low):
-    first, second = split(coeff)
+    first, second = split(jnp.concatenate([coeff[:, :64], coeff[:, 64:]], axis=0))
     right = dot(first, low[:64]) + dot(first, low[64:]) + dot(second, low[:64])
     beside = jnp.concatenate([right[r : r + 64] for r in range(0, right.shape[0], 64)], axis=1)
     first, second = split(beside)
@@ -156,7 +169,7 @@
         out_specs=IN_VMEM,
         out_shape=jax.ShapeDtypeStruct((size, rows, cols), jnp.bfloat16),
         compiler_params=pltpu.CompilerParams(vmem_limit_bytes=VMEM),
-        cost_estimate=pl.CostEstimate(flops=size * 100000, bytes_accessed=size * rows * 512 * 3, transcendentals=0),
+        cost_estimate=pl.CostEstimate(flops=size, bytes_accessed=size, transcendentals=0),
         name=name,
     )(*held)
 
@@ -164,8 +177,8 @@
 def coeff_kernel(counts, *refs):
     n = sum(counts)
     mom_ref, band_ref, low_ref, updated_ref, coeff_ref = refs[n:]
-    row = lax.broadcasted_iota(jnp.int32, (64, 64), 0) % LOW
-    spot = row * BLOCK + lax.broadcasted_iota(jnp.int32, (64, 64), 1) % LOW
+    row = lax.broadcasted_iota(jnp.int32, coeff_ref.shape, 0) % LOW
+    spot = row * BLOCK + lax.broadcasted_iota(jnp.int32, coeff_ref.shape, 1) % LOW
     chosen = functools.reduce(jnp.logical_or, [spot == band_ref[i] for i in range(BAND)])
     mask = chosen.astype(jnp.float32)
     rows, at = [], 0
@@ -177,7 +190,7 @@
     turned = [gradient[c : c + ROWS].T for c in range(0, gradient.shape[0], ROWS)]
     updated = DECAY * mom_ref[0] + jnp.concatenate(turned, axis=1)
     updated_ref[...] = updated
-    coeff_ref[...] = forward(updated, low_ref[...]) * jnp.concatenate([mask] * len(turned), axis=0)
+    coeff_ref[...] = forward(updated, low_ref[...]) * mask
 
 
 def coefficients(held, momentum, band, low):
@@ -189,7 +202,7 @@
         out_specs=[IN_VMEM] * 2,
         out_shape=[
             jax.ShapeDtypeStruct((rows, ncol), jnp.float32),
-            jax.ShapeDtypeStruct((ncol // 4, 64), jnp.float32),
+            jax.ShapeDtypeStruct((ncol // 8, 128), jnp.float32),
         ],
         compiler_params=pltpu.CompilerParams(vmem_limit_bytes=VMEM),
         cost_estimate=pl.CostEstimate(flops=ncol * 1000000, bytes_accessed=ncol * 256 * 8, transcendentals=0),
@@ -230,18 +243,21 @@
 def per_device(activations, cotangent, momentum, band):
     low = jnp.asarray(low_table())
     me = lax.axis_index("fsdp")
-    blocks = terms(activations, cotangent, jnp.stack([me >> 2, me & 3]).astype(jnp.int32))
-
-    held = [[blocks[2 * c + 1]] for c in range(len(CHAINS))]
-    before = blocks[0]
+    pos = jnp.stack([me >> 2, me & 3]).astype(jnp.int32)
+    sent = terms(activations, cotangent, pos, False)
+    pos, _ = lax.optimization_barrier((pos, sent[0]))
+    kept = terms(activations, cotangent, pos, True)
+
+    held = [[k] for k in kept]
+    before = sent[0]
     for c, stage in SCHEDULE:
         if stage:
             held[c][-1], before = lax.optimization_barrier((held[c][-1], before))
             send = add(held[c], 8 >> stage, "add%d_%d" % (c, stage))
         else:
-            send, before = lax.optimization_barrier((blocks[2 * c], before))
+            send = sent[c]
         held[c].append(swap(send, "fsdp", CHAINS[c][1][stage]))
-        before = send
+        before = send if stage else before
 
     updated, coeffs = coefficients(held, momentum, band, low)
     fresh = new_momentum(updated, coeffs, low, momentum.shape)

time: 121 us -> 110 us (0.909)
  waiting for transfers between devices: 53.8 us -> 41 us
  Pallas kernels: 17.2 us -> 22.1 us
  starting transfers between devices: 47.3 us -> 45.4 us
  local copies, waits for them, and re-layouts: 1.52 us -> 0.03 us
    ppermute x25, waiting for transfers between devices: 53.8 us -> 41 us  [swap(): return lax.ppermute(value, axis, [(i, i ^ mask) for i in range(n)])]
    pallas_call x1 -> x2, Pallas kernels: 11.6 us -> 16.3 us  [terms(): pl.pallas_call(functools.partial(terms_kernel, kept), in_specs=[pl.BlockS...]
    ppermute x25, starting transfers between devices: 47.3 us -> 45.4 us  [swap(): return lax.ppermute(value, axis, [(i, i ^ mask) for i in range(n)])]
    unnamed x8, local copies, waits for them, and re-layouts: 1.52 us -> 0.03 us
  transfers between devices with their start and end apart: 25 -> 25, of which waited for: 14 -> 12; matrix products, arithmetic and copies ran while one was open for 0% -> 0% of each run, Pallas kernels for 2% -> 10%
where the time goes in v3:
time: 110 us; the launch traced here: 109 us
  starting transfers between devices  45.4 us (41%)
  waiting for transfers between devices  41 us (37%)
  Pallas kernels  22.1 us (20%)
    ppermute x25, starting transfers between devices, swap(): return lax.ppermute(value, axis, [(i, i ^ mask) for i in range(n)])  45.4 us
    ppermute x25, waiting for transfers between devices, swap(): return lax.ppermute(value, axis, [(i, i ^ mask) for i in range(n)])  41 us
    pallas_call x2, Pallas kernels, terms(): pl.pallas_call(functools.partial(terms_kernel, kept), in_specs=[pl.BlockS...  16.3 us
  transfers between devices with their start and end apart: 25, of which 12 were waited for; matrix products, arithmetic and copies ran while one was open for 0% of the time, Pallas kernels for 10%

profile of v3, /device:TPU:6, one launch (start us, length us, event | category | flops | bytes accessed | tf_op | source)
XLA Modules:
  0.0 109.4 jit_solution(6589204903770264868)
XLA Ops:
  0.7 8.5 %terms_sent.1 = (bf16[8,256,256]{2,1,0:T(8,128)(2,1)S(1)}, bf16[8,128,256]{2,1,0:T(8,128)(2,1)S(1)}, bf16[8,192,256]{2,1,0:T(8,128)(2,1)S(1)}, bf16[8,192,256]{2,1,0:T(8,128)(2,1)S(1)}, bf16[8,256,256]{2,1,0:T(8,128)(2,1)}) custom-call(s32[2]{0:T(128)S(1)} %pad_add_fusion.pos_ref, bf16[896,4096]{1,0:T(8,128)(2,1)} %act_ref.3, bf16[896,1024]{1,0:T(8,128)(2,1)} %cot_ref.3), custom_call_target="tpu_custom_call" | custom-call | flops 3758096384 | bytes 7340032 | tf_op jit(solution)/shard_map/terms_sent/pallas_call | solution.py:101
  9.3 0.9 collective-permute-start.1
  10.2 1.5 %collective-permute-start = (bf16[8,256,256]{2,1,0:T(8,128)(2,1)S(1)}, bf16[8,256,256]{2,1,0:T(8,128)(2,1)S(1)}, u32[]{:S(2)}, u32[]{:S(2)}) collective-permute-start(bf16[8,256,256]{2,1,0:T(8,128)(2,1)S(1)} %get-tuple-element.30), channel_id=1, source_target_pairs={{0,12},{1,13},{2,14},{3,15},{4,8},{5,9},{6,10},{7,11},{8,4},{9,5},... | collective-permute-start | bytes 3145736 | tf_op jit(solution)/shard_map/ppermute | solution.py:46
  11.7 6.0 %collective-permute-start.6 = (bf16[8,192,256]{2,1,0:T(8,128)(2,1)S(1)}, bf16[8,192,256]{2,1,0:T(8,128)(2,1)S(1)}, u32[]{:S(2)}, u32[]{:S(2)}) collective-permute-start(bf16[8,192,256]{2,1,0:T(8,128)(2,1)S(1)} %get-tuple-element.42), channel_id=1, source_target_pairs={{0,3},{1,2},{2,1},{3,0},{4,7},{5,6},{6,5},{7,4},{8,11},{9,10},{10,... | collective-permute-start | bytes 2359304 | tf_op jit(solution)/shard_map/ppermute | solution.py:46
  17.6 1.4 %collective-permute-start.4 = (bf16[8,192,256]{2,1,0:T(8,128)(2,1)S(1)}, bf16[8,192,256]{2,1,0:T(8,128)(2,1)S(1)}, u32[]{:S(2)}, u32[]{:S(2)}) collective-permute-start(bf16[8,192,256]{2,1,0:T(8,128)(2,1)S(1)} %get-tuple-element.38), channel_id=1, source_target_pairs={{0,1},{1,0},{2,3},{3,2},{4,5},{5,4},{6,7},{7,6},{8,9},{9,8},{10,11... | collective-permute-start | bytes 2359304 | tf_op jit(solution)/shard_map/ppermute | solution.py:46
  19.1 7.7 %terms_kept.1 = (bf16[8,256,256]{2,1,0:T(8,128)(2,1)S(1)}, bf16[8,128,256]{2,1,0:T(8,128)(2,1)S(1)}, bf16[8,192,256]{2,1,0:T(8,128)(2,1)S(1)}, bf16[8,192,256]{2,1,0:T(8,128)(2,1)S(1)}, bf16[8,256,256]{2,1,0:T(8,128)(2,1)S(1)}) custom-call(s32[2]{0:T(128)S(1)} %pad_add_fusion.pos_ref, bf16[896,4096]{1,0:T(8,128)(2,1)} %act_ref.3, bf16[896,1024]{1,0:T(8,128)(2,1)S(1)} %copy-done.3), custom_call_target="tpu_custom_call" | custom-call | flops 3758096384 | bytes 7340032 | tf_op jit(solution)/shard_map/terms_kept/pallas_call | solution.py:101
  26.9 8.8 %collective-permute-done.1.refs_1_.refs_21_ = bf16[8,256,256]{2,1,0:T(8,128)(2,1)S(1)} collective-permute-done((bf16[8,256,256]{2,1,0:T(8,128)(2,1)}, bf16[8,256,256]{2,1,0:T(8,128)(2,1)S(1)}, u32[]{:S(2)}, u32[]{:S(2)}) %collective-permute-start.1) | collective-permute-done | bytes 1048608 | tf_op jit(solution)/shard_map/ppermute | solution.py:46
  35.7 2.5 %collective-permute-start.3 = (bf16[4,256,256]{2,1,0:T(8,128)(2,1)S(1)}, bf16[4,256,256]{2,1,0:T(8,128)(2,1)S(1)}, u32[]{:S(2)}, u32[]{:S(2)}) collective-permute-start(bf16[4,256,256]{2,1,0:T(8,128)(2,1)S(1)} %add4_1.1), channel_id=1, source_target_pairs={{0,12},{1,13},{2,14},{3,15},{4,8},{5,9},{6,10},{7,11},{8,4},{9,5},... | collective-permute-start | bytes 1572872 | tf_op jit(solution)/shard_map/ppermute | solution.py:46
  38.5 12.2 %collective-permute-done.6.refs_1_.refs_11_ = bf16[8,192,256]{2,1,0:T(8,128)(2,1)S(1)} collective-permute-done((bf16[8,192,256]{2,1,0:T(8,128)(2,1)S(1)}, bf16[8,192,256]{2,1,0:T(8,128)(2,1)S(1)}, u32[]{:S(2)}, u32[]{:S(2)}) %collective-permute-start.6) | collective-permute-done | bytes 786464 | tf_op jit(solution)/shard_map/ppermute | solution.py:46
  50.8 2.2 %collective-permute-start.8 = (bf16[4,192,256]{2,1,0:T(8,128)(2,1)S(1)}, bf16[4,192,256]{2,1,0:T(8,128)(2,1)S(1)}, u32[]{:S(2)}, u32[]{:S(2)}) collective-permute-start(bf16[4,192,256]{2,1,0:T(8,128)(2,1)S(1)} %add2_1.1), channel_id=1, source_target_pairs={{0,12},{1,13},{2,14},{3,15},{4,8},{5,9},{6,10},{7,11},{8,4},{9,5},... | collective-permute-start | bytes 1179656 | tf_op jit(solution)/shard_map/ppermute | solution.py:46
  53.1 0.8 collective-permute-done.4.refs_1_.refs_16_
  54.5 3.6 %collective-permute-start.11 = (bf16[2,256,256]{2,1,0:T(8,128)(2,1)S(1)}, bf16[2,256,256]{2,1,0:T(8,128)(2,1)S(1)}, u32[]{:S(2)}, u32[]{:S(2)}) collective-permute-start(bf16[2,256,256]{2,1,0:T(8,128)(2,1)S(1)} %add4_2.1), channel_id=1, source_target_pairs={{0,3},{1,2},{2,1},{3,0},{4,7},{5,6},{6,5},{7,4},{8,11},{9,10},{10,... | collective-permute-start | bytes 786440 | tf_op jit(solution)/shard_map/ppermute | solution.py:46
  58.1 1.1 %collective-permute-start.10 = (bf16[4,128,256]{2,1,0:T(8,128)(2,1)S(1)}, bf16[4,128,256]{2,1,0:T(8,128)(2,1)S(1)}, u32[]{:S(2)}, u32[]{:S(2)}) collective-permute-start(bf16[4,128,256]{2,1,0:T(8,128)(2,1)S(1)} %add1_1.1), channel_id=1, source_target_pairs={{0,12},{1,13},{2,14},{3,15},{4,8},{5,9},{6,10},{7,11},{8,4},{9,5},... | collective-permute-start | bytes 786440 | tf_op jit(solution)/shard_map/ppermute | solution.py:46
  59.3 2.2 %collective-permute-start.7 = (bf16[2,256,256]{2,1,0:T(8,128)(2,1)S(1)}, bf16[2,256,256]{2,1,0:T(8,128)(2,1)S(1)}, u32[]{:S(2)}, u32[]{:S(2)}) collective-permute-start(bf16[2,256,256]{2,1,0:T(8,128)(2,1)S(1)} %add0_2.1), channel_id=1, source_target_pairs={{0,1},{1,0},{2,3},{3,2},{4,5},{5,4},{6,7},{7,6},{8,9},{9,8},{10,11... | collective-permute-start | bytes 786440 | tf_op jit(solution)/shard_map/ppermute | solution.py:46
  61.5 2.6 %collective-permute-done.8.refs_2_.refs_12_ = bf16[4,192,256]{2,1,0:T(8,128)(2,1)S(1)} collective-permute-done((bf16[4,192,256]{2,1,0:T(8,128)(2,1)S(1)}, bf16[4,192,256]{2,1,0:T(8,128)(2,1)S(1)}, u32[]{:S(2)}, u32[]{:S(2)}) %collective-permute-start.8) | collective-permute-done | bytes 393248 | tf_op jit(solution)/shard_map/ppermute | solution.py:46
  64.4 2.1 %collective-permute-done.12.refs_2_.refs_17_ = bf16[4,192,256]{2,1,0:T(8,128)(2,1)S(1)} collective-permute-done((bf16[4,192,256]{2,1,0:T(8,128)(2,1)S(1)}, bf16[4,192,256]{2,1,0:T(8,128)(2,1)S(1)}, u32[]{:S(2)}, u32[]{:S(2)}) %collective-permute-start.12) | collective-permute-done | bytes 393248 | tf_op jit(solution)/shard_map/ppermute | solution.py:46
  66.6 6.4 %collective-permute-start.17 = (bf16[2,192,256]{2,1,0:T(8,128)(2,1)S(1)}, bf16[2,192,256]{2,1,0:T(8,128)(2,1)S(1)}, u32[]{:S(2)}, u32[]{:S(2)}) collective-permute-start(bf16[2,192,256]{2,1,0:T(8,128)(2,1)S(1)} %add3_2.1), channel_id=1, source_target_pairs={{0,3},{1,2},{2,1},{3,0},{4,7},{5,6},{6,5},{7,4},{8,11},{9,10},{10,... | collective-permute-start | bytes 589832 | tf_op jit(solution)/shard_map/ppermute | solution.py:46
  73.1 1.5 %collective-permute-start.14 = (bf16[2,128,256]{2,1,0:T(8,128)(2,1)S(1)}, bf16[2,128,256]{2,1,0:T(8,128)(2,1)S(1)}, u32[]{:S(2)}, u32[]{:S(2)}) collective-permute-start(bf16[2,128,256]{2,1,0:T(8,128)(2,1)S(1)} %add1_2.1), channel_id=1, source_target_pairs={{0,1},{1,0},{2,3},{3,2},{4,5},{5,4},{6,7},{7,6},{8,9},{9,8},{10,11... | collective-permute-start | bytes 393224 | tf_op jit(solution)/shard_map/ppermute | solution.py:46
  74.8 2.7 %collective-permute-start.13 = (bf16[1,256,256]{2,1,0:T(8,128)(2,1)S(1)}, bf16[1,256,256]{2,1,0:T(8,128)(2,1)S(1)}, u32[]{:S(2)}, u32[]{:S(2)}) collective-permute-start(bf16[1,256,256]{2,1,0:T(8,128)(2,1)S(1)} %add0_3.1), channel_id=1, source_target_pairs={{0,3},{1,2},{2,1},{3,0},{4,7},{5,6},{6,5},{7,4},{8,11},{9,10},{10,... | collective-permute-start | bytes 393224 | tf_op jit(solution)/shard_map/ppermute | solution.py:46
  77.5 1.3 %collective-permute-start.19 = (bf16[1,256,256]{2,1,0:T(8,128)(2,1)S(1)}, bf16[1,256,256]{2,1,0:T(8,128)(2,1)S(1)}, u32[]{:S(2)}, u32[]{:S(2)}) collective-permute-start(bf16[1,256,256]{2,1,0:T(8,128)(2,1)S(1)} %add4_3.1), channel_id=1, source_target_pairs={{0,1},{1,0},{2,3},{3,2},{4,5},{5,4},{6,7},{7,6},{8,9},{9,8},{10,11... | collective-permute-start | bytes 393224 | tf_op jit(solution)/shard_map/ppermute | solution.py:46
  78.8 1.6 %collective-permute-start.16 = (bf16[1,192,256]{2,1,0:T(8,128)(2,1)S(1)}, bf16[1,192,256]{2,1,0:T(8,128)(2,1)S(1)}, u32[]{:S(2)}, u32[]{:S(2)}) collective-permute-start(bf16[1,192,256]{2,1,0:T(8,128)(2,1)S(1)} %add2_3.1), channel_id=1, source_target_pairs={{0,1},{1,0},{2,3},{3,2},{4,5},{5,4},{6,7},{7,6},{8,9},{9,8},{10,11... | collective-permute-start | bytes 294920 | tf_op jit(solution)/shard_map/ppermute | solution.py:46
  81.2 2.2 %collective-permute-done.17.refs_3_.refs_18_ = bf16[2,192,256]{2,1,0:T(8,128)(2,1)S(1)} collective-permute-done((bf16[2,192,256]{2,1,0:T(8,128)(2,1)S(1)}, bf16[2,192,256]{2,1,0:T(8,128)(2,1)S(1)}, u32[]{:S(2)}, u32[]{:S(2)}) %collective-permute-start.17) | collective-permute-done | bytes 196640 | tf_op jit(solution)/shard_map/ppermute | solution.py:46
  83.5 5.2 %collective-permute-start.15 = (bf16[1,128,256]{2,1,0:T(8,128)(2,1)S(1)}, bf16[1,128,256]{2,1,0:T(8,128)(2,1)S(1)}, u32[]{:S(2)}, u32[]{:S(2)}) collective-permute-start(bf16[1,128,256]{2,1,0:T(8,128)(2,1)S(1)} %add1_3.1), channel_id=1, source_target_pairs={{0,3},{1,2},{2,1},{3,0},{4,7},{5,6},{6,5},{7,4},{8,11},{9,10},{10,... | collective-permute-start | bytes 196616 | tf_op jit(solution)/shard_map/ppermute | solution.py:46
  88.8 1.6 %collective-permute-done.16.refs_14_ = bf16[1,192,256]{2,1,0:T(8,128)(2,1)S(1)} collective-permute-done((bf16[1,192,256]{2,1,0:T(8,128)(2,1)S(1)}, bf16[1,192,256]{2,1,0:T(8,128)(2,1)S(1)}, u32[]{:S(2)}, u32[]{:S(2)}) %collective-permute-start.16) | collective-permute-done | bytes 98336 | tf_op jit(solution)/shard_map/ppermute | solution.py:46
  90.4 1.2 %collective-permute-done.15.refs_9_ = bf16[1,128,256]{2,1,0:T(8,128)(2,1)S(1)} collective-permute-done((bf16[1,128,256]{2,1,0:T(8,128)(2,1)S(1)}, bf16[1,128,256]{2,1,0:T(8,128)(2,1)S(1)}, u32[]{:S(2)}, u32[]{:S(2)}) %collective-permute-start.15) | collective-permute-done | bytes 65568 | tf_op jit(solution)/shard_map/ppermute | solution.py:46
  91.6 1.7 %coefficients.1 = (f32[256,1024]{1,0:T(8,128)S(1)}, f32[128,128]{1,0:T(8,128)S(1)}) custom-call(bf16[8,256,256]{2,1,0:T(8,128)(2,1)S(1)} %get-tuple-element.32.refs_0_, bf16[8,256,256]{2,1,0:T(8,128)(2,1)S(1)} %collective-permute-done.refs_1_, bf16[4,256,256]{2,1,0:T(8,128)(2,1)S(1)} %collective-permute-done.2.refs_2_, ...), custom_call_target="tpu_custom_call" | custom-call | flops 1024000000 | bytes 2097152 | tf_op jit(solution)/shard_map/coefficients/pallas_call | solution.py:199
  93.5 1.2 %collective-permute-done.20 = f32[128,128]{1,0:T(8,128)S(1)} collective-permute-done((f32[128,128]{1,0:T(8,128)S(1)}, f32[128,128]{1,0:T(8,128)S(1)}, u32[]{:S(2)}, u32[]{:S(2)}) %collective-permute-start.20) | collective-permute-done | bytes 65568 | tf_op jit(solution)/shard_map/ppermute | solution.py:46
  94.8 4.3 %collective-permute-done.21 = f32[128,128]{1,0:T(8,128)S(1)} collective-permute-done((f32[128,128]{1,0:T(8,128)S(1)}, f32[128,128]{1,0:T(8,128)S(1)}, u32[]{:S(2)}, u32[]{:S(2)}) %collective-permute-start.21) | collective-permute-done | bytes 65568 | tf_op jit(solution)/shard_map/ppermute | solution.py:46
  99.1 3.2 %collective-permute-start.24 = (f32[128,128]{1,0:T(8,128)S(1)}, f32[128,128]{1,0:T(8,128)S(1)}, u32[]{:S(2)}, u32[]{:S(2)}) collective-permute-start(f32[128,128]{1,0:T(8,128)S(1)} %add.7.a_ref), channel_id=1, source_target_pairs={{0,96},{16,112},{32,64},{48,80},{64,32},{80,48},{96,0},{112,16},{1... | collective-permute-start | bytes 196616 | tf_op jit(solution)/shard_map/ppermute | solution.py:46
  103.3 1.6 %new_momentum.1 = f32[1,256,1024]{2,1,0:T(8,128)} custom-call(f32[256,1024]{1,0:T(8,128)S(1)} %get-tuple-element.56.updated_ref, f32[128,128]{1,0:T(8,128)S(1)} %get-tuple-element.57.coeff_ref, bf16[128,256]{1,0:T(8,128)(2,1)S(1)} %copy-done.1), custom_call_target="tpu_custom_call" | custom-call | flops 2000000000 | bytes 2000000 | tf_op jit(solution)/shard_map/new_momentum/pallas_call | solution.py:218
  104.8 3.2 %collective-permute-done.23.c_ref = f32[128,128]{1,0:T(8,128)S(1)} collective-permute-done((f32[128,128]{1,0:T(8,128)S(1)}, f32[128,128]{1,0:T(8,128)S(1)}, u32[]{:S(2)}, u32[]{:S(2)}) %collective-permute-start.23) | collective-permute-done | bytes 65568 | tf_op jit(solution)/shard_map/ppermute | solution.py:46
  108.0 1.4 %update.1 = bf16[256,1024]{1,0:T(8,128)(2,1)} custom-call(f32[128,128]{1,0:T(8,128)S(1)} %add.7.a_ref, f32[128,128]{1,0:T(8,128)S(1)} %collective-permute-done.22.b_ref, f32[128,128]{1,0:T(8,128)S(1)} %collective-permute-done.23.c_ref, f32[128,128]{1,0:T(8,128)S(1)} %collective-permute-done.24.d_ref, bf16[128,256]{1,0:T(8,128)(2,1)S(1)} %copy-done.1), custom_call_target="tpu_custom_call" | custom-call | tf_op jit(solution)/shard_map/update/pallas_call | solution.py:234
  (49 shorter events, 4.1 us)
Async XLA Ops:
  0.6 18.5 %copy-start.3 = (bf16[896,1024]{1,0:T(8,128)(2,1)S(1)}, bf16[896,1024]{1,0:T(8,128)(2,1)}, u32[]{:S(2)}) copy-start(bf16[896,1024]{1,0:T(8,128)(2,1)} %cot_ref.3) | copy-start | bytes 5505028
  9.3 26.3 %collective-permute-start.1 = (bf16[8,256,256]{2,1,0:T(8,128)(2,1)}, bf16[8,256,256]{2,1,0:T(8,128)(2,1)S(1)}, u32[]{:S(2)}, u32[]{:S(2)}) collective-permute-start(bf16[8,256,256]{2,1,0:T(8,128)(2,1)} %get-tuple-element.34), channel_id=1, source_target_pairs={{0,4},{1,5},{2,6},{3,7},{4,0},{5,1},{6,2},{7,3},{8,12},{9,13},{10,... | collective-permute-start | bytes 3145736 | tf_op jit(solution)/shard_map/ppermute | solution.py:46
  10.2 28.1 %collective-permute-start = (bf16[8,256,256]{2,1,0:T(8,128)(2,1)S(1)}, bf16[8,256,256]{2,1,0:T(8,128)(2,1)S(1)}, u32[]{:S(2)}, u32[]{:S(2)}) collective-permute-start(bf16[8,256,256]{2,1,0:T(8,128)(2,1)S(1)} %get-tuple-element.30), channel_id=1, source_target_pairs={{0,12},{1,13},{2,14},{3,15},{4,8},{5,9},{6,10},{7,11},{8,4},{9,5},... | collective-permute-start | bytes 3145736 | tf_op jit(solution)/shard_map/ppermute | solution.py:46
  11.7 39.0 %collective-permute-start.6 = (bf16[8,192,256]{2,1,0:T(8,128)(2,1)S(1)}, bf16[8,192,256]{2,1,0:T(8,128)(2,1)S(1)}, u32[]{:S(2)}, u32[]{:S(2)}) collective-permute-start(bf16[8,192,256]{2,1,0:T(8,128)(2,1)S(1)} %get-tuple-element.42), channel_id=1, source_target_pairs={{0,3},{1,2},{2,1},{3,0},{4,7},{5,6},{6,5},{7,4},{8,11},{9,10},{10,... | collective-permute-start | bytes 2359304 | tf_op jit(solution)/shard_map/ppermute | solution.py:46
  17.6 36.2 %collective-permute-start.4 = (bf16[8,192,256]{2,1,0:T(8,128)(2,1)S(1)}, bf16[8,192,256]{2,1,0:T(8,128)(2,1)S(1)}, u32[]{:S(2)}, u32[]{:S(2)}) collective-permute-start(bf16[8,192,256]{2,1,0:T(8,128)(2,1)S(1)} %get-tuple-element.38), channel_id=1, source_target_pairs={{0,1},{1,0},{2,3},{3,2},{4,5},{5,4},{6,7},{7,6},{8,9},{9,8},{10,11... | collective-permute-start | bytes 2359304 | tf_op jit(solution)/shard_map/ppermute | solution.py:46
  19.1 33.9 %collective-permute-start.5 = (bf16[8,128,256]{2,1,0:T(8,128)(2,1)S(1)}, bf16[8,128,256]{2,1,0:T(8,128)(2,1)S(1)}, u32[]{:S(2)}, u32[]{:S(2)}) collective-permute-start(bf16[8,128,256]{2,1,0:T(8,128)(2,1)S(1)} %get-tuple-element.40), channel_id=1, source_target_pairs={{0,4},{1,5},{2,6},{3,7},{4,0},{5,1},{6,2},{7,3},{8,12},{9,13},{10,... | collective-permute-start | bytes 1572872 | tf_op jit(solution)/shard_map/ppermute | solution.py:46
  35.7 18.6 %collective-permute-start.3 = (bf16[4,256,256]{2,1,0:T(8,128)(2,1)S(1)}, bf16[4,256,256]{2,1,0:T(8,128)(2,1)S(1)}, u32[]{:S(2)}, u32[]{:S(2)}) collective-permute-start(bf16[4,256,256]{2,1,0:T(8,128)(2,1)S(1)} %add4_1.1), channel_id=1, source_target_pairs={{0,12},{1,13},{2,14},{3,15},{4,8},{5,9},{6,10},{7,11},{8,4},{9,5},... | collective-permute-start | bytes 1572872 | tf_op jit(solution)/shard_map/ppermute | solution.py:46
  38.4 20.8 %collective-permute-start.2 = (bf16[4,256,256]{2,1,0:T(8,128)(2,1)S(1)}, bf16[4,256,256]{2,1,0:T(8,128)(2,1)S(1)}, u32[]{:S(2)}, u32[]{:S(2)}) collective-permute-start(bf16[4,256,256]{2,1,0:T(8,128)(2,1)S(1)} %add0_1.1), channel_id=1, source_target_pairs={{0,4},{1,5},{2,6},{3,7},{4,0},{5,1},{6,2},{7,3},{8,12},{9,13},{10,... | collective-permute-start | bytes 1572872 | tf_op jit(solution)/shard_map/ppermute | solution.py:46
  50.8 13.3 %collective-permute-start.8 = (bf16[4,192,256]{2,1,0:T(8,128)(2,1)S(1)}, bf16[4,192,256]{2,1,0:T(8,128)(2,1)S(1)}, u32[]{:S(2)}, u32[]{:S(2)}) collective-permute-start(bf16[4,192,256]{2,1,0:T(8,128)(2,1)S(1)} %add2_1.1), channel_id=1, source_target_pairs={{0,12},{1,13},{2,14},{3,15},{4,8},{5,9},{6,10},{7,11},{8,4},{9,5},... | collective-permute-start | bytes 1179656 | tf_op jit(solution)/shard_map/ppermute | solution.py:46
  54.0 12.6 %collective-permute-start.12 = (bf16[4,192,256]{2,1,0:T(8,128)(2,1)S(1)}, bf16[4,192,256]{2,1,0:T(8,128)(2,1)S(1)}, u32[]{:S(2)}, u32[]{:S(2)}) collective-permute-start(bf16[4,192,256]{2,1,0:T(8,128)(2,1)S(1)} %add3_1.1), channel_id=1, source_target_pairs={{0,4},{1,5},{2,6},{3,7},{4,0},{5,1},{6,2},{7,3},{8,12},{9,13},{10,... | collective-permute-start | bytes 1179656 | tf_op jit(solution)/shard_map/ppermute | solution.py:46
  54.5 18.5 %collective-permute-start.11 = (bf16[2,256,256]{2,1,0:T(8,128)(2,1)S(1)}, bf16[2,256,256]{2,1,0:T(8,128)(2,1)S(1)}, u32[]{:S(2)}, u32[]{:S(2)}) collective-permute-start(bf16[2,256,256]{2,1,0:T(8,128)(2,1)S(1)} %add4_2.1), channel_id=1, source_target_pairs={{0,3},{1,2},{2,1},{3,0},{4,7},{5,6},{6,5},{7,4},{8,11},{9,10},{10,... | collective-permute-start | bytes 786440 | tf_op jit(solution)/shard_map/ppermute | solution.py:46
  58.1 15.0 %collective-permute-start.10 = (bf16[4,128,256]{2,1,0:T(8,128)(2,1)S(1)}, bf16[4,128,256]{2,1,0:T(8,128)(2,1)S(1)}, u32[]{:S(2)}, u32[]{:S(2)}) collective-permute-start(bf16[4,128,256]{2,1,0:T(8,128)(2,1)S(1)} %add1_1.1), channel_id=1, source_target_pairs={{0,12},{1,13},{2,14},{3,15},{4,8},{5,9},{6,10},{7,11},{8,4},{9,5},... | collective-permute-start | bytes 786440 | tf_op jit(solution)/shard_map/ppermute | solution.py:46
  59.3 15.4 %collective-permute-start.7 = (bf16[2,256,256]{2,1,0:T(8,128)(2,1)S(1)}, bf16[2,256,256]{2,1,0:T(8,128)(2,1)S(1)}, u32[]{:S(2)}, u32[]{:S(2)}) collective-permute-start(bf16[2,256,256]{2,1,0:T(8,128)(2,1)S(1)} %add0_2.1), channel_id=1, source_target_pairs={{0,1},{1,0},{2,3},{3,2},{4,5},{5,4},{6,7},{7,6},{8,9},{9,8},{10,11... | collective-permute-start | bytes 786440 | tf_op jit(solution)/shard_map/ppermute | solution.py:46
  64.3 27.4 %copy-start = (f32[1,256,1024]{2,1,0:T(8,128)S(1)}, f32[1,256,1024]{2,1,0:T(8,128)}, u32[]{:S(2)}) copy-start(f32[1,256,1024]{2,1,0:T(8,128)} %refs_25_.1) | copy-start | bytes 3145732
  64.3 27.3 %copy-start.1 = (bf16[128,256]{1,0:T(8,128)(2,1)S(1)}, bf16[128,256]{1,0:T(8,128)(2,1)}, u32[]{:S(2)}) copy-start(bf16[128,256]{1,0:T(8,128)(2,1)} %constant.10.clone.refs_27_.low_ref) | copy-start | bytes 196612
  64.3 27.3 %copy-start.2 = (s32[32]{0:T(128)S(1)}, s32[32]{0:T(128)}, u32[]{:S(2)}) copy-start(s32[32]{0:T(128)} %refs_26_.1) | copy-start | bytes 388
  64.3 10.4 %collective-permute-start.9 = (bf16[2,192,256]{2,1,0:T(8,128)(2,1)S(1)}, bf16[2,192,256]{2,1,0:T(8,128)(2,1)S(1)}, u32[]{:S(2)}, u32[]{:S(2)}) collective-permute-start(bf16[2,192,256]{2,1,0:T(8,128)(2,1)S(1)} %add2_2.1), channel_id=1, source_target_pairs={{0,4},{1,5},{2,6},{3,7},{4,0},{5,1},{6,2},{7,3},{8,12},{9,13},{10,... | collective-permute-start | bytes 589832 | tf_op jit(solution)/shard_map/ppermute | solution.py:46
  66.6 16.8 %collective-permute-start.17 = (bf16[2,192,256]{2,1,0:T(8,128)(2,1)S(1)}, bf16[2,192,256]{2,1,0:T(8,128)(2,1)S(1)}, u32[]{:S(2)}, u32[]{:S(2)}) collective-permute-start(bf16[2,192,256]{2,1,0:T(8,128)(2,1)S(1)} %add3_2.1), channel_id=1, source_target_pairs={{0,3},{1,2},{2,1},{3,0},{4,7},{5,6},{6,5},{7,4},{8,11},{9,10},{10,... | collective-permute-start | bytes 589832 | tf_op jit(solution)/shard_map/ppermute | solution.py:46
  73.1 8.0 %collective-permute-start.14 = (bf16[2,128,256]{2,1,0:T(8,128)(2,1)S(1)}, bf16[2,128,256]{2,1,0:T(8,128)(2,1)S(1)}, u32[]{:S(2)}, u32[]{:S(2)}) collective-permute-start(bf16[2,128,256]{2,1,0:T(8,128)(2,1)S(1)} %add1_2.1), channel_id=1, source_target_pairs={{0,1},{1,0},{2,3},{3,2},{4,5},{5,4},{6,7},{7,6},{8,9},{9,8},{10,11... | collective-permute-start | bytes 393224 | tf_op jit(solution)/shard_map/ppermute | solution.py:46
  74.8 15.6 %collective-permute-start.13 = (bf16[1,256,256]{2,1,0:T(8,128)(2,1)S(1)}, bf16[1,256,256]{2,1,0:T(8,128)(2,1)S(1)}, u32[]{:S(2)}, u32[]{:S(2)}) collective-permute-start(bf16[1,256,256]{2,1,0:T(8,128)(2,1)S(1)} %add0_3.1), channel_id=1, source_target_pairs={{0,3},{1,2},{2,1},{3,0},{4,7},{5,6},{6,5},{7,4},{8,11},{9,10},{10,... | collective-permute-start | bytes 393224 | tf_op jit(solution)/shard_map/ppermute | solution.py:46
  77.5 12.9 %collective-permute-start.19 = (bf16[1,256,256]{2,1,0:T(8,128)(2,1)S(1)}, bf16[1,256,256]{2,1,0:T(8,128)(2,1)S(1)}, u32[]{:S(2)}, u32[]{:S(2)}) collective-permute-start(bf16[1,256,256]{2,1,0:T(8,128)(2,1)S(1)} %add4_3.1), channel_id=1, source_target_pairs={{0,1},{1,0},{2,3},{3,2},{4,5},{5,4},{6,7},{7,6},{8,9},{9,8},{10,11... | collective-permute-start | bytes 393224 | tf_op jit(solution)/shard_map/ppermute | solution.py:46
  78.8 11.6 %collective-permute-start.16 = (bf16[1,192,256]{2,1,0:T(8,128)(2,1)S(1)}, bf16[1,192,256]{2,1,0:T(8,128)(2,1)S(1)}, u32[]{:S(2)}, u32[]{:S(2)}) collective-permute-start(bf16[1,192,256]{2,1,0:T(8,128)(2,1)S(1)} %add2_3.1), channel_id=1, source_target_pairs={{0,1},{1,0},{2,3},{3,2},{4,5},{5,4},{6,7},{7,6},{8,9},{9,8},{10,11... | collective-permute-start | bytes 294920 | tf_op jit(solution)/shard_map/ppermute | solution.py:46
  83.4 8.2 %collective-permute-start.18 = (bf16[1,192,256]{2,1,0:T(8,128)(2,1)S(1)}, bf16[1,192,256]{2,1,0:T(8,128)(2,1)S(1)}, u32[]{:S(2)}, u32[]{:S(2)}) collective-permute-start(bf16[1,192,256]{2,1,0:T(8,128)(2,1)S(1)} %add3_3.1), channel_id=1, source_target_pairs={{0,12},{1,13},{2,14},{3,15},{4,8},{5,9},{6,10},{7,11},{8,4},{9,5},... | collective-permute-start | bytes 294920 | tf_op jit(solution)/shard_map/ppermute | solution.py:46
  83.5 8.1 %collective-permute-start.15 = (bf16[1,128,256]{2,1,0:T(8,128)(2,1)S(1)}, bf16[1,128,256]{2,1,0:T(8,128)(2,1)S(1)}, u32[]{:S(2)}, u32[]{:S(2)}) collective-permute-start(bf16[1,128,256]{2,1,0:T(8,128)(2,1)S(1)} %add1_3.1), channel_id=1, source_target_pairs={{0,3},{1,2},{2,1},{3,0},{4,7},{5,6},{6,5},{7,4},{8,11},{9,10},{10,... | collective-permute-start | bytes 196616 | tf_op jit(solution)/shard_map/ppermute | solution.py:46
  93.4 1.3 %collective-permute-start.20 = (f32[128,128]{1,0:T(8,128)S(1)}, f32[128,128]{1,0:T(8,128)S(1)}, u32[]{:S(2)}, u32[]{:S(2)}) collective-permute-start(f32[128,128]{1,0:T(8,128)S(1)} %get-tuple-element.57.coeff_ref), channel_id=1, source_target_pairs={{0,16},{16,0},{32,48},{48,32},{64,80},{80,64},{96,112},{112,96},{1... | collective-permute-start | bytes 196616 | tf_op jit(solution)/shard_map/ppermute | solution.py:46
  94.7 4.4 %collective-permute-start.21 = (f32[128,128]{1,0:T(8,128)S(1)}, f32[128,128]{1,0:T(8,128)S(1)}, u32[]{:S(2)}, u32[]{:S(2)}) collective-permute-start(f32[128,128]{1,0:T(8,128)S(1)} %add.6), channel_id=1, source_target_pairs={{0,128},{16,144},{32,160},{48,176},{64,192},{80,208},{96,224},{112... | collective-permute-start | bytes 196616 | tf_op jit(solution)/shard_map/ppermute | solution.py:46
  99.1 5.7 %collective-permute-start.24 = (f32[128,128]{1,0:T(8,128)S(1)}, f32[128,128]{1,0:T(8,128)S(1)}, u32[]{:S(2)}, u32[]{:S(2)}) collective-permute-start(f32[128,128]{1,0:T(8,128)S(1)} %add.7.a_ref), channel_id=1, source_target_pairs={{0,96},{16,112},{32,64},{48,80},{64,32},{80,48},{96,0},{112,16},{1... | collective-permute-start | bytes 196616 | tf_op jit(solution)/shard_map/ppermute | solution.py:46
  102.2 5.8 %collective-permute-start.23 = (f32[128,128]{1,0:T(8,128)S(1)}, f32[128,128]{1,0:T(8,128)S(1)}, u32[]{:S(2)}, u32[]{:S(2)}) collective-permute-start(f32[128,128]{1,0:T(8,128)S(1)} %add.7.a_ref), channel_id=1, source_target_pairs={{0,64},{16,80},{32,96},{48,112},{64,0},{80,16},{96,32},{112,48},{1... | collective-permute-start | bytes 196616 | tf_op jit(solution)/shard_map/ppermute | solution.py:46
  102.8 5.2 %collective-permute-start.22 = (f32[128,128]{1,0:T(8,128)S(1)}, f32[128,128]{1,0:T(8,128)S(1)}, u32[]{:S(2)}, u32[]{:S(2)}) collective-permute-start(f32[128,128]{1,0:T(8,128)S(1)} %add.7.a_ref), channel_id=1, source_target_pairs={{0,32},{16,48},{32,0},{48,16},{64,96},{80,112},{96,64},{112,80},{1... | collective-permute-start | bytes 196616 | tf_op jit(solution)/shard_map/ppermute | solution.py:46

commit v4 on v3

--- a/solution.py
+++ b/solution.py
@@ -16,16 +16,16 @@
 ROWS = 256
 CHAINS = (
     (256, (12, 4, 1, 3)),
+    (256, (4, 12, 3, 1)),
     (128, (4, 12, 1, 3)),
     (192, (3, 12, 4, 1)),
     (192, (1, 4, 3, 12)),
-    (256, (4, 12, 3, 1)),
 )
 SCHEDULE = (
-    (4, 0), (2, 0), (3, 0), (0, 0), (4, 1), (0, 1), (2, 1), (1, 0), (1, 1), (3, 1),
-    (4, 2), (0, 2), (2, 2), (3, 2), (4, 3), (1, 2), (2, 3), (0, 3), (1, 3), (3, 3),
+    (1, 0), (3, 0), (4, 0), (0, 0), (1, 1), (0, 1), (3, 1), (2, 0), (2, 1), (4, 1),
+    (1, 2), (0, 2), (3, 2), (4, 2), (1, 3), (2, 2), (3, 3), (0, 3), (2, 3), (4, 3),
 )
-VMEM = 40 * 1024 * 1024
+VMEM = 16 * 1024 * 1024
 TERMS_VMEM = 50 * 1024 * 1024
 IN_VMEM = pl.BlockSpec(memory_space=pltpu.VMEM)
 
@@ -54,10 +54,11 @@
     raise ValueError(offset)
 
 
-def terms_kernel(kept, pos_ref, act_ref, cot_ref, *refs):
+def terms_kernel(kept, act_ref, cot_ref, *refs):
     outs = refs[: len(CHAINS)]
     gt_ref, buf_ref, cot_buf, sem_ref = refs[len(CHAINS) :]
-    a, b = pos_ref[0], pos_ref[1]
+    me = lax.axis_index("fsdp")
+    a, b = me >> 2, me & 3
     width = buf_ref.shape[2]
     order = (0, 3, 1, 2) if kept else (2, 1, 3, 0)
 
@@ -67,9 +68,10 @@
 
     cot_copy = pltpu.make_async_copy(cot_ref, cot_buf, sem_ref.at[4])
     cot_copy.start()
-    for ka in order:
+    load(order[0]).start()
+    cot_copy.wait()
+    for ka in order[1:]:
         load(ka).start()
-    cot_copy.wait()
     gt_ref[...] = cot_buf[...].T
     for ka in order:
         load(ka).wait()
@@ -95,13 +97,12 @@
                     at += ncol
 
 
-def terms(activations, cotangent, pos, kept):
+def terms(activations, cotangent, kept):
     tokens, width = activations.shape
     shapes = [jax.ShapeDtypeStruct((8, n, ROWS), jnp.bfloat16) for n, _ in CHAINS]
     return pl.pallas_call(
         functools.partial(terms_kernel, kept),
         in_specs=[
-            pl.BlockSpec(memory_space=pltpu.SMEM),
             pl.BlockSpec(memory_space=pltpu.HBM),
             pl.BlockSpec(memory_space=pltpu.HBM),
         ],
@@ -118,7 +119,7 @@
             flops=tokens * width * cotangent.shape[1], bytes_accessed=tokens * width * 2, transcendentals=0
         ),
         name="terms_kept" if kept else "terms_sent",
-    )(pos, activations, cotangent)
+    )(activations, cotangent)
 
 
 def f32(x):
@@ -141,13 +142,11 @@
     stacked = jnp.concatenate([left[:, c : c + ROWS] for c in range(0, left.shape[1], ROWS)], axis=0)
     first, second = split(stacked)
     both = dot(first, low, ((1,), (1,)))
-    coeff = both[:, :64] + both[:, 64:] + dot(second, low[:64], ((1,), (1,)))
-    half = coeff.shape[0] // 2
-    return jnp.concatenate([coeff[:half], coeff[half:]], axis=1)
+    return both[:, :64] + both[:, 64:] + dot(second, low[:64], ((1,), (1,)))
 
 
 def backward(coeff, low):
-    first, second = split(jnp.concatenate([coeff[:, :64], coeff[:, 64:]], axis=0))
+    first, second = split(coeff)
     right = dot(first, low[:64]) + dot(first, low[64:]) + dot(second, low[:64])
     beside = jnp.concatenate([right[r : r + 64] for r in range(0, right.shape[0], 64)], axis=1)
     first, second = split(beside)
@@ -174,13 +173,24 @@
     )(*held)
 
 
+def band_tables(band, rows):
+    width = band.shape[1]
+    column = lax.broadcasted_iota(jnp.int32, (64, width), 1) % 4 * LOW + band % BLOCK
+    pick = (lax.broadcasted_iota(jnp.int32, (64, width), 0) == column).astype(jnp.bfloat16)
+    keep = (lax.broadcasted_iota(jnp.int32, (rows, width), 0) % LOW == band // BLOCK).astype(jnp.float32)
+    own = lax.broadcasted_iota(jnp.int32, (rows // LOW, rows), 1) // LOW
+    gather = (own == lax.broadcasted_iota(jnp.int32, (rows // LOW, rows), 0)).astype(jnp.bfloat16)
+    return pick, keep, gather
+
+
+def both_of(x, table, dims=((1,), (0,))):
+    first, second = split(x)
+    return dot(first, table, dims) + dot(second, table, dims)
+
+
 def coeff_kernel(counts, *refs):
     n = sum(counts)
-    mom_ref, band_ref, low_ref, updated_ref, coeff_ref = refs[n:]
-    row = lax.broadcasted_iota(jnp.int32, coeff_ref.shape, 0) % LOW
-    spot = row * BLOCK + lax.broadcasted_iota(jnp.int32, coeff_ref.shape, 1) % LOW
-    chosen = functools.reduce(jnp.logical_or, [spot == band_ref[i] for i in range(BAND)])
-    mask = chosen.astype(jnp.float32)
+    mom_ref, band_ref, low_ref, updated_ref, coeff_ref, chosen_ref = refs[n:]
     rows, at = [], 0
     for count in counts:
         parts = [f32(ref[0]) for ref in refs[at : at + count]]
@@ -190,7 +200,12 @@
     turned = [gradient[c : c + ROWS].T for c in range(0, gradient.shape[0], ROWS)]
     updated = DECAY * mom_ref[0] + jnp.concatenate(turned, axis=1)
     updated_ref[...] = updated
-    coeff_ref[...] = forward(updated, low_ref[...]) * mask
+    coeff = forward(updated, low_ref[...])
+    pick, keep, gather = band_tables(band_ref[...], coeff.shape[0])
+    picked = both_of(coeff, pick) * keep
+    first, second = split(picked)
+    chosen_ref[...] = dot(gather, first) + dot(gather, second)
+    coeff_ref[...] = both_of(picked, pick, ((1,), (1,)))
 
 
 def coefficients(held, momentum, band, low):
@@ -198,11 +213,12 @@
     arrays = [a for chain in held for a in chain]
     return pl.pallas_call(
         functools.partial(coeff_kernel, [len(chain) for chain in held]),
-        in_specs=[IN_VMEM] * (len(arrays) + 1) + [pl.BlockSpec(memory_space=pltpu.SMEM), IN_VMEM],
-        out_specs=[IN_VMEM] * 2,
+        in_specs=[IN_VMEM] * (len(arrays) + 3),
+        out_specs=[IN_VMEM] * 3,
         out_shape=[
             jax.ShapeDtypeStruct((rows, ncol), jnp.float32),
-            jax.ShapeDtypeStruct((ncol // 8, 128), jnp.float32),
+            jax.ShapeDtypeStruct((ncol // 4, 64), jnp.float32),
+            jax.ShapeDtypeStruct((ncol // 64, 4 * BAND), jnp.float32),
         ],
         compiler_params=pltpu.CompilerParams(vmem_limit_bytes=VMEM),
         cost_estimate=pl.CostEstimate(flops=ncol * 1000000, bytes_accessed=ncol * 256 * 8, transcendentals=0),
@@ -225,29 +241,30 @@
     )(updated, coeffs, low)
 
 
-def update_kernel(scale, a_ref, b_ref, c_ref, d_ref, low_ref, out_ref):
+def update_kernel(scale, a_ref, b_ref, c_ref, d_ref, band_ref, low_ref, out_ref):
     total = (a_ref[...] + b_ref[...]) + (c_ref[...] + d_ref[...])
-    out_ref[...] = (backward(total, low_ref[...]) * scale).astype(jnp.bfloat16)
-
-
-def make_update(parts, low, ncols, scale):
+    pick, keep, gather = band_tables(band_ref[...], LOW * total.shape[0])
+    first, second = split(total)
+    spread = (dot(gather, first, ((0,), (0,))) + dot(gather, second, ((0,), (0,)))) * keep
+    coeff = both_of(spread, pick, ((1,), (1,)))
+    out_ref[...] = (backward(coeff, low_ref[...]) * scale).astype(jnp.bfloat16)
+
+
+def make_update(parts, band, low, ncols, scale):
     return pl.pallas_call(
         functools.partial(update_kernel, scale),
-        in_specs=[IN_VMEM] * 5,
+        in_specs=[IN_VMEM] * 6,
         out_shape=jax.ShapeDtypeStruct((ROWS, ncols), jnp.bfloat16),
         compiler_params=pltpu.CompilerParams(vmem_limit_bytes=VMEM),
         name="update",
-    )(*parts, low)
+    )(*parts, band, low)
 
 
 def per_device(activations, cotangent, momentum, band):
     low = jnp.asarray(low_table())
-    me = lax.axis_index("fsdp")
-    pos = jnp.stack([me >> 2, me & 3]).astype(jnp.int32)
-    sent = terms(activations, cotangent, pos, False)
-    pos, _ = lax.optimization_barrier((pos, sent[0]))
-    kept = terms(activations, cotangent, pos, True)
-
+    sent = terms(activations, cotangent, False)
+    cotangent, _ = lax.optimization_barrier((cotangent, sent[0]))
+    kept = terms(activations, cotangent, True)
     held = [[k] for k in kept]
     before = sent[0]
     for c, stage in SCHEDULE:
@@ -259,14 +276,14 @@
         held[c].append(swap(send, "fsdp", CHAINS[c][1][stage]))
         before = send if stage else before
 
-    updated, coeffs = coefficients(held, momentum, band, low)
+    band = jnp.repeat(band, 4)[None]
+    updated, coeffs, chosen = coefficients(held, momentum, band, low)
     fresh = new_momentum(updated, coeffs, low, momentum.shape)
-    summed = coeffs
-    for m in (1, 8):
-        summed = summed + swap(summed, "rep", m)
+    a, b, c, d = [chosen] + [swap(chosen, "rep", m) for m in (1, 8, 9)]
+    summed = (a + b) + (c + d)
     parts = [summed] + [swap(summed, "rep", m) for m in (2, 4, 6)]
     scale = BLOCK / math.sqrt(BAND * lax.axis_size("rep"))
-    update = make_update(parts, low, momentum.shape[2], scale)
+    update = make_update(parts, band, low, momentum.shape[2], scale)
     return (fresh, update)
 
 

time: 110 us -> 130 us (1.18)
  the two profiles are of different devices: /device:TPU:6 before, /device:TPU:64 now
where the time goes in v4:
time: 130 us; the launch traced here: 129 us
  waiting for transfers between devices  43.1 us (33%)
  starting transfers between devices  39.8 us (31%)
  Pallas kernels  25.3 us (19%)
  local copies, waits for them, and re-layouts  20.1 us (15%)
    ppermute x26, waiting for transfers between devices, swap(): return lax.ppermute(value, axis, [(i, i ^ mask) for i in range(n)])  43.1 us
    ppermute x26, starting transfers between devices, swap(): return lax.ppermute(value, axis, [(i, i ^ mask) for i in range(n)])  39.8 us
    unnamed x72, local copies, waits for them, and re-layouts  18.7 us
    pallas_call x2, Pallas kernels, terms(): pl.pallas_call(functools.partial(terms_kernel, kept), in_specs=[pl.BlockS...  15.1 us
    pallas_call x15, Pallas kernels, add(): pl.pallas_call(functools.partial(add_kernel, size), in_specs=[IN_VMEM] *...  4.52 us
  transfers between devices with their start and end apart: 26, of which 11 were waited for; matrix products, arithmetic and copies ran while one was open for 1% of the time, Pallas kernels for 10%

profile of v4, /device:TPU:64, one launch (start us, length us, event | category | flops | bytes accessed | tf_op | source)
XLA Modules:
  0.0 129.3 jit_solution(17821828724028496659)
XLA Ops:
  0.6 8.2 %terms_sent.1 = (bf16[8,256,256]{2,1,0:T(8,128)(2,1)S(1)}, bf16[8,256,256]{2,1,0:T(8,128)(2,1)}, bf16[8,128,256]{2,1,0:T(8,128)(2,1)S(1)}, bf16[8,192,256]{2,1,0:T(8,128)(2,1)S(1)}, bf16[8,192,256]{2,1,0:T(8,128)(2,1)S(1)}) custom-call(bf16[896,4096]{1,0:T(8,128)(2,1)} %act_ref.3, bf16[896,1024]{1,0:T(8,128)(2,1)} %cot_ref.2), custom_call_target="tpu_custom_call" | custom-call | flops 3758096384 | bytes 7340032 | tf_op jit(solution)/shard_map/terms_sent/pallas_call | solution.py:103
  8.9 1.6 %collective-permute-start.1 = (bf16[8,256,256]{2,1,0:T(8,128)(2,1)}, bf16[8,256,256]{2,1,0:T(8,128)(2,1)S(1)}, u32[]{:S(2)}, u32[]{:S(2)}) collective-permute-start(bf16[8,256,256]{2,1,0:T(8,128)(2,1)} %get-tuple-element.35), channel_id=1, source_target_pairs={{0,4},{1,5},{2,6},{3,7},{4,0},{5,1},{6,2},{7,3},{8,12},{9,13},{10,... | collective-permute-start | bytes 3145736 | tf_op jit(solution)/shard_map/ppermute | solution.py:46
  10.5 2.1 %collective-permute-start = (bf16[8,256,256]{2,1,0:T(8,128)(2,1)S(1)}, bf16[8,256,256]{2,1,0:T(8,128)(2,1)S(1)}, u32[]{:S(2)}, u32[]{:S(2)}) collective-permute-start(bf16[8,256,256]{2,1,0:T(8,128)(2,1)S(1)} %get-tuple-element.31), channel_id=1, source_target_pairs={{0,12},{1,13},{2,14},{3,15},{4,8},{5,9},{6,10},{7,11},{8,4},{9,5},... | collective-permute-start | bytes 3145736 | tf_op jit(solution)/shard_map/ppermute | solution.py:46
  12.6 4.5 %collective-permute-start.6 = (bf16[8,192,256]{2,1,0:T(8,128)(2,1)S(1)}, bf16[8,192,256]{2,1,0:T(8,128)(2,1)S(1)}, u32[]{:S(2)}, u32[]{:S(2)}) collective-permute-start(bf16[8,192,256]{2,1,0:T(8,128)(2,1)S(1)} %get-tuple-element.43), channel_id=1, source_target_pairs={{0,3},{1,2},{2,1},{3,0},{4,7},{5,6},{6,5},{7,4},{8,11},{9,10},{10,... | collective-permute-start | bytes 2359304 | tf_op jit(solution)/shard_map/ppermute | solution.py:46
  17.0 1.5 %collective-permute-start.4 = (bf16[8,192,256]{2,1,0:T(8,128)(2,1)S(1)}, bf16[8,192,256]{2,1,0:T(8,128)(2,1)S(1)}, u32[]{:S(2)}, u32[]{:S(2)}) collective-permute-start(bf16[8,192,256]{2,1,0:T(8,128)(2,1)S(1)} %get-tuple-element.39), channel_id=1, source_target_pairs={{0,1},{1,0},{2,3},{3,2},{4,5},{5,4},{6,7},{7,6},{8,9},{9,8},{10,11... | collective-permute-start | bytes 2359304 | tf_op jit(solution)/shard_map/ppermute | solution.py:46
  19.1 6.9 %terms_kept.1 = (bf16[8,256,256]{2,1,0:T(8,128)(2,1)S(1)}, bf16[8,256,256]{2,1,0:T(8,128)(2,1)S(1)}, bf16[8,128,256]{2,1,0:T(8,128)(2,1)S(1)}, bf16[8,192,256]{2,1,0:T(8,128)(2,1)S(1)}, bf16[8,192,256]{2,1,0:T(8,128)(2,1)S(1)}) custom-call(bf16[896,4096]{1,0:T(8,128)(2,1)} %act_ref.3, bf16[896,1024]{1,0:T(8,128)(2,1)S(1)} %copy-done.34), custom_call_target="tpu_custom_call" | custom-call | flops 3758096384 | bytes 7340032 | tf_op jit(solution)/shard_map/terms_kept/pallas_call | solution.py:103
  26.0 9.2 %collective-permute-done.1.refs_1_.refs_6_ = bf16[8,256,256]{2,1,0:T(8,128)(2,1)S(1)} collective-permute-done((bf16[8,256,256]{2,1,0:T(8,128)(2,1)}, bf16[8,256,256]{2,1,0:T(8,128)(2,1)S(1)}, u32[]{:S(2)}, u32[]{:S(2)}) %collective-permute-start.1) | collective-permute-done | bytes 1048608 | tf_op jit(solution)/shard_map/ppermute | solution.py:46
  35.3 3.0 %collective-permute-start.3 = (bf16[4,256,256]{2,1,0:T(8,128)(2,1)S(1)}, bf16[4,256,256]{2,1,0:T(8,128)(2,1)S(1)}, u32[]{:S(2)}, u32[]{:S(2)}) collective-permute-start(bf16[4,256,256]{2,1,0:T(8,128)(2,1)S(1)} %add1_1.1), channel_id=1, source_target_pairs={{0,12},{1,13},{2,14},{3,15},{4,8},{5,9},{6,10},{7,11},{8,4},{9,5},... | collective-permute-start | bytes 1572872 | tf_op jit(solution)/shard_map/ppermute | solution.py:46
  38.8 12.1 %collective-permute-done.6.refs_1_.refs_16_ = bf16[8,192,256]{2,1,0:T(8,128)(2,1)S(1)} collective-permute-done((bf16[8,192,256]{2,1,0:T(8,128)(2,1)S(1)}, bf16[8,192,256]{2,1,0:T(8,128)(2,1)S(1)}, u32[]{:S(2)}, u32[]{:S(2)}) %collective-permute-start.6) | collective-permute-done | bytes 786464 | tf_op jit(solution)/shard_map/ppermute | solution.py:46
  51.0 1.2 collective-permute-start.8
  54.6 2.2 %collective-permute-start.10 = (bf16[4,128,256]{2,1,0:T(8,128)(2,1)S(1)}, bf16[4,128,256]{2,1,0:T(8,128)(2,1)S(1)}, u32[]{:S(2)}, u32[]{:S(2)}) collective-permute-start(bf16[4,128,256]{2,1,0:T(8,128)(2,1)S(1)} %add2_1.1), channel_id=1, source_target_pairs={{0,12},{1,13},{2,14},{3,15},{4,8},{5,9},{6,10},{7,11},{8,4},{9,5},... | collective-permute-start | bytes 786440 | tf_op jit(solution)/shard_map/ppermute | solution.py:46
  57.8 2.5 %collective-permute-start.7 = (bf16[2,256,256]{2,1,0:T(8,128)(2,1)S(1)}, bf16[2,256,256]{2,1,0:T(8,128)(2,1)S(1)}, u32[]{:S(2)}, u32[]{:S(2)}) collective-permute-start(bf16[2,256,256]{2,1,0:T(8,128)(2,1)S(1)} %add0_2.1), channel_id=1, source_target_pairs={{0,1},{1,0},{2,3},{3,2},{4,5},{5,4},{6,7},{7,6},{8,9},{9,8},{10,11... | collective-permute-start | bytes 786440 | tf_op jit(solution)/shard_map/ppermute | solution.py:46
  60.3 4.0 %collective-permute-done.8.refs_2_.refs_17_ = bf16[4,192,256]{2,1,0:T(8,128)(2,1)S(1)} collective-permute-done((bf16[4,192,256]{2,1,0:T(8,128)(2,1)S(1)}, bf16[4,192,256]{2,1,0:T(8,128)(2,1)S(1)}, u32[]{:S(2)}, u32[]{:S(2)}) %collective-permute-start.8) | collective-permute-done | bytes 393248 | tf_op jit(solution)/shard_map/ppermute | solution.py:46
  64.5 1.6 %collective-permute-done.12.refs_2_.refs_22_ = bf16[4,192,256]{2,1,0:T(8,128)(2,1)S(1)} collective-permute-done((bf16[4,192,256]{2,1,0:T(8,128)(2,1)S(1)}, bf16[4,192,256]{2,1,0:T(8,128)(2,1)S(1)}, u32[]{:S(2)}, u32[]{:S(2)}) %collective-permute-start.12) | collective-permute-done | bytes 393248 | tf_op jit(solution)/shard_map/ppermute | solution.py:46
  66.2 4.6 %collective-permute-start.18 = (bf16[2,192,256]{2,1,0:T(8,128)(2,1)S(1)}, bf16[2,192,256]{2,1,0:T(8,128)(2,1)S(1)}, u32[]{:S(2)}, u32[]{:S(2)}) collective-permute-start(bf16[2,192,256]{2,1,0:T(8,128)(2,1)S(1)} %add4_2.1), channel_id=1, source_target_pairs={{0,3},{1,2},{2,1},{3,0},{4,7},{5,6},{6,5},{7,4},{8,11},{9,10},{10,... | collective-permute-start | bytes 589832 | tf_op jit(solution)/shard_map/ppermute | solution.py:46
  71.6 1.6 %collective-permute-start.15 = (bf16[2,128,256]{2,1,0:T(8,128)(2,1)S(1)}, bf16[2,128,256]{2,1,0:T(8,128)(2,1)S(1)}, u32[]{:S(2)}, u32[]{:S(2)}) collective-permute-start(bf16[2,128,256]{2,1,0:T(8,128)(2,1)S(1)} %add2_2.1), channel_id=1, source_target_pairs={{0,1},{1,0},{2,3},{3,2},{4,5},{5,4},{6,7},{7,6},{8,9},{9,8},{10,11... | collective-permute-start | bytes 393224 | tf_op jit(solution)/shard_map/ppermute | solution.py:46
  75.4 3.2 %collective-permute-start.14 = (bf16[1,256,256]{2,1,0:T(8,128)(2,1)}, bf16[1,256,256]{2,1,0:T(8,128)(2,1)}, u32[]{:S(2)}, u32[]{:S(2)}) collective-permute-start(bf16[1,256,256]{2,1,0:T(8,128)(2,1)} %add1_3.1), channel_id=1, source_target_pairs={{0,1},{1,0},{2,3},{3,2},{4,5},{5,4},{6,7},{7,6},{8,9},{9,8},{10,11... | collective-permute-start | bytes 393224 | tf_op jit(solution)/shard_map/ppermute | solution.py:46
  78.7 5.3 %collective-permute-done.15.refs_3_.refs_13_ = bf16[2,128,256]{2,1,0:T(8,128)(2,1)S(1)} collective-permute-done((bf16[2,128,256]{2,1,0:T(8,128)(2,1)S(1)}, bf16[2,128,256]{2,1,0:T(8,128)(2,1)S(1)}, u32[]{:S(2)}, u32[]{:S(2)}) %collective-permute-start.15) | collective-permute-done | bytes 131104 | tf_op jit(solution)/shard_map/ppermute | solution.py:46
  85.4 2.4 %collective-permute-start.19 = (bf16[1,192,256]{2,1,0:T(8,128)(2,1)}, bf16[1,192,256]{2,1,0:T(8,128)(2,1)}, u32[]{:S(2)}, u32[]{:S(2)}) collective-permute-start(bf16[1,192,256]{2,1,0:T(8,128)(2,1)} %add4_3.1), channel_id=1, source_target_pairs={{0,12},{1,13},{2,14},{3,15},{4,8},{5,9},{6,10},{7,11},{8,4},{9,5},... | collective-permute-start | bytes 294920 | tf_op jit(solution)/shard_map/ppermute | solution.py:46
  89.3 5.1 %collective-permute-done.16.refs_14_ = bf16[1,128,256]{2,1,0:T(8,128)(2,1)} collective-permute-done((bf16[1,128,256]{2,1,0:T(8,128)(2,1)}, bf16[1,128,256]{2,1,0:T(8,128)(2,1)}, u32[]{:S(2)}, u32[]{:S(2)}) %collective-permute-start.16) | collective-permute-done | bytes 65568 | tf_op jit(solution)/shard_map/ppermute | solution.py:46
  94.4 1.2 copy-done.1
  96.8 1.1 copy-done.5
  97.9 1.1 copy-done.7
  99.1 1.1 copy-done.9
  106.3 1.2 copy-done.22
  113.0 2.4 %coefficients.1 = (f32[256,1024]{1,0:T(8,128)S(1)}, f32[256,64]{1,0:T(8,128)S(1)}, f32[16,128]{1,0:T(8,128)S(1)}) custom-call(bf16[8,256,256]{2,1,0:T(8,128)(2,1)S(1)} %get-tuple-element.33.refs_0_, bf16[8,256,256]{2,1,0:T(8,128)(2,1)S(1)} %collective-permute-done.refs_1_, bf16[4,256,256]{2,1,0:T(8,128)(2,1)S(1)} %copy-done.17, ...), custom_call_target="tpu_custom_call" | custom-call | flops 1024000000 | bytes 2097152 | tf_op jit(solution)/shard_map/coefficients/pallas_call | solution.py:214
  115.6 1.7 %collective-permute-start.20 = (f32[16,128]{1,0:T(8,128)S(1)}, f32[16,128]{1,0:T(8,128)S(1)}, u32[]{:S(2)}, u32[]{:S(2)}) collective-permute-start(f32[16,128]{1,0:T(8,128)S(1)} %get-tuple-element.59), channel_id=1, source_target_pairs={{0,16},{16,0},{32,48},{48,32},{64,80},{80,64},{96,112},{112,96},{1... | collective-permute-start | bytes 24584 | tf_op jit(solution)/shard_map/ppermute | solution.py:46
  117.4 1.2 collective-permute-done.22
  119.3 3.1 %collective-permute-start.25 = (f32[16,128]{1,0:T(8,128)S(1)}, f32[16,128]{1,0:T(8,128)S(1)}, u32[]{:S(2)}, u32[]{:S(2)}) collective-permute-start(f32[16,128]{1,0:T(8,128)S(1)} %add_add_fusion.a_ref), channel_id=1, source_target_pairs={{0,96},{16,112},{32,64},{48,80},{64,32},{80,48},{96,0},{112,16},{1... | collective-permute-start | bytes 24584 | tf_op jit(solution)/shard_map/ppermute | solution.py:46
  123.4 1.6 %new_momentum.1 = f32[1,256,1024]{2,1,0:T(8,128)} custom-call(f32[256,1024]{1,0:T(8,128)S(1)} %get-tuple-element.57.updated_ref, f32[256,64]{1,0:T(8,128)S(1)} %get-tuple-element.58.coeff_ref, bf16[128,256]{1,0:T(8,128)(2,1)S(1)} %copy-done.33), custom_call_target="tpu_custom_call" | custom-call | flops 2000000000 | bytes 2000000 | tf_op jit(solution)/shard_map/new_momentum/pallas_call | solution.py:234
  125.0 2.5 %collective-permute-done.24.c_ref = f32[16,128]{1,0:T(8,128)S(1)} collective-permute-done((f32[16,128]{1,0:T(8,128)S(1)}, f32[16,128]{1,0:T(8,128)S(1)}, u32[]{:S(2)}, u32[]{:S(2)}) %collective-permute-start.24) | collective-permute-done | bytes 8224 | tf_op jit(solution)/shard_map/ppermute | solution.py:46
  127.5 1.8 %update.1 = bf16[256,1024]{1,0:T(8,128)(2,1)} custom-call(f32[16,128]{1,0:T(8,128)S(1)} %add_add_fusion.a_ref, f32[16,128]{1,0:T(8,128)S(1)} %collective-permute-done.23.b_ref, f32[16,128]{1,0:T(8,128)S(1)} %collective-permute-done.24.c_ref, f32[16,128]{1,0:T(8,128)S(1)} %collective-permute-done.25.d_ref, ...), custom_call_target="tpu_custom_call" | custom-call | tf_op jit(solution)/shard_map/update/pallas_call | solution.py:254
  (115 shorter events, 25.5 us)
Async XLA Ops:
  8.9 26.3 %collective-permute-start.1 = (bf16[8,256,256]{2,1,0:T(8,128)(2,1)}, bf16[8,256,256]{2,1,0:T(8,128)(2,1)S(1)}, u32[]{:S(2)}, u32[]{:S(2)}) collective-permute-start(bf16[8,256,256]{2,1,0:T(8,128)(2,1)} %get-tuple-element.35), channel_id=1, source_target_pairs={{0,4},{1,5},{2,6},{3,7},{4,0},{5,1},{6,2},{7,3},{8,12},{9,13},{10,... | collective-permute-start | bytes 3145736 | tf_op jit(solution)/shard_map/ppermute | solution.py:46
  10.5 27.9 %collective-permute-start = (bf16[8,256,256]{2,1,0:T(8,128)(2,1)S(1)}, bf16[8,256,256]{2,1,0:T(8,128)(2,1)S(1)}, u32[]{:S(2)}, u32[]{:S(2)}) collective-permute-start(bf16[8,256,256]{2,1,0:T(8,128)(2,1)S(1)} %get-tuple-element.31), channel_id=1, source_target_pairs={{0,12},{1,13},{2,14},{3,15},{4,8},{5,9},{6,10},{7,11},{8,4},{9,5},... | collective-permute-start | bytes 3145736 | tf_op jit(solution)/shard_map/ppermute | solution.py:46
  12.6 38.3 %collective-permute-start.6 = (bf16[8,192,256]{2,1,0:T(8,128)(2,1)S(1)}, bf16[8,192,256]{2,1,0:T(8,128)(2,1)S(1)}, u32[]{:S(2)}, u32[]{:S(2)}) collective-permute-start(bf16[8,192,256]{2,1,0:T(8,128)(2,1)S(1)} %get-tuple-element.43), channel_id=1, source_target_pairs={{0,3},{1,2},{2,1},{3,0},{4,7},{5,6},{6,5},{7,4},{8,11},{9,10},{10,... | collective-permute-start | bytes 2359304 | tf_op jit(solution)/shard_map/ppermute | solution.py:46
  17.0 35.7 %collective-permute-start.4 = (bf16[8,192,256]{2,1,0:T(8,128)(2,1)S(1)}, bf16[8,192,256]{2,1,0:T(8,128)(2,1)S(1)}, u32[]{:S(2)}, u32[]{:S(2)}) collective-permute-start(bf16[8,192,256]{2,1,0:T(8,128)(2,1)S(1)} %get-tuple-element.39), channel_id=1, source_target_pairs={{0,1},{1,0},{2,3},{3,2},{4,5},{5,4},{6,7},{7,6},{8,9},{9,8},{10,11... | collective-permute-start | bytes 2359304 | tf_op jit(solution)/shard_map/ppermute | solution.py:46
  18.5 33.7 %collective-permute-start.5 = (bf16[8,128,256]{2,1,0:T(8,128)(2,1)S(1)}, bf16[8,128,256]{2,1,0:T(8,128)(2,1)S(1)}, u32[]{:S(2)}, u32[]{:S(2)}) collective-permute-start(bf16[8,128,256]{2,1,0:T(8,128)(2,1)S(1)} %get-tuple-element.41), channel_id=1, source_target_pairs={{0,4},{1,5},{2,6},{3,7},{4,0},{5,1},{6,2},{7,3},{8,12},{9,13},{10,... | collective-permute-start | bytes 1572872 | tf_op jit(solution)/shard_map/ppermute | solution.py:46
  26.0 44.8 %copy-start = (bf16[8,256,256]{2,1,0:T(8,128)(2,1)}, bf16[8,256,256]{2,1,0:T(8,128)(2,1)S(1)}, u32[]{:S(2)}) copy-start(bf16[8,256,256]{2,1,0:T(8,128)(2,1)S(1)} %get-tuple-element.34.refs_0_.refs_5_) | copy-start | bytes 3145732
  26.0 47.2 %copy-start.6 = (bf16[8,192,256]{2,1,0:T(8,128)(2,1)}, bf16[8,192,256]{2,1,0:T(8,128)(2,1)S(1)}, u32[]{:S(2)}) copy-start(bf16[8,192,256]{2,1,0:T(8,128)(2,1)S(1)} %get-tuple-element.42.refs_0_.refs_15_) | copy-start | bytes 2359300
  26.0 57.9 %copy-start.12 = (bf16[8,128,256]{2,1,0:T(8,128)(2,1)}, bf16[8,128,256]{2,1,0:T(8,128)(2,1)S(1)}, u32[]{:S(2)}) copy-start(bf16[8,128,256]{2,1,0:T(8,128)(2,1)S(1)} %get-tuple-element.40.refs_0_.refs_10_) | copy-start | bytes 1572868
  26.0 58.6 %copy-start.8 = (bf16[8,192,256]{2,1,0:T(8,128)(2,1)}, bf16[8,192,256]{2,1,0:T(8,128)(2,1)S(1)}, u32[]{:S(2)}) copy-start(bf16[8,192,256]{2,1,0:T(8,128)(2,1)S(1)} %get-tuple-element.38.refs_0_.refs_20_) | copy-start | bytes 2359300
  35.3 18.2 %collective-permute-start.3 = (bf16[4,256,256]{2,1,0:T(8,128)(2,1)S(1)}, bf16[4,256,256]{2,1,0:T(8,128)(2,1)S(1)}, u32[]{:S(2)}, u32[]{:S(2)}) collective-permute-start(bf16[4,256,256]{2,1,0:T(8,128)(2,1)S(1)} %add1_1.1), channel_id=1, source_target_pairs={{0,12},{1,13},{2,14},{3,15},{4,8},{5,9},{6,10},{7,11},{8,4},{9,5},... | collective-permute-start | bytes 1572872 | tf_op jit(solution)/shard_map/ppermute | solution.py:46
  38.5 19.2 %collective-permute-start.2 = (bf16[4,256,256]{2,1,0:T(8,128)(2,1)S(1)}, bf16[4,256,256]{2,1,0:T(8,128)(2,1)S(1)}, u32[]{:S(2)}, u32[]{:S(2)}) collective-permute-start(bf16[4,256,256]{2,1,0:T(8,128)(2,1)S(1)} %add0_1.1), channel_id=1, source_target_pairs={{0,4},{1,5},{2,6},{3,7},{4,0},{5,1},{6,2},{7,3},{8,12},{9,13},{10,... | collective-permute-start | bytes 1572872 | tf_op jit(solution)/shard_map/ppermute | solution.py:46
  51.0 13.4 %collective-permute-start.8 = (bf16[4,192,256]{2,1,0:T(8,128)(2,1)S(1)}, bf16[4,192,256]{2,1,0:T(8,128)(2,1)S(1)}, u32[]{:S(2)}, u32[]{:S(2)}) collective-permute-start(bf16[4,192,256]{2,1,0:T(8,128)(2,1)S(1)} %add3_1.1), channel_id=1, source_target_pairs={{0,12},{1,13},{2,14},{3,15},{4,8},{5,9},{6,10},{7,11},{8,4},{9,5},... | collective-permute-start | bytes 1179656 | tf_op jit(solution)/shard_map/ppermute | solution.py:46
  52.2 31.8 %copy-start.10 = (bf16[8,128,256]{2,1,0:T(8,128)(2,1)}, bf16[8,128,256]{2,1,0:T(8,128)(2,1)S(1)}, u32[]{:S(2)}) copy-start(bf16[8,128,256]{2,1,0:T(8,128)(2,1)S(1)} %collective-permute-done.5.refs_1_.refs_11_) | copy-start | bytes 1572868
  52.8 31.9 %copy-start.4 = (bf16[8,192,256]{2,1,0:T(8,128)(2,1)}, bf16[8,192,256]{2,1,0:T(8,128)(2,1)S(1)}, u32[]{:S(2)}) copy-start(bf16[8,192,256]{2,1,0:T(8,128)(2,1)S(1)} %collective-permute-done.4.refs_1_.refs_21_) | copy-start | bytes 2359300
  52.9 13.2 %collective-permute-start.12 = (bf16[4,192,256]{2,1,0:T(8,128)(2,1)S(1)}, bf16[4,192,256]{2,1,0:T(8,128)(2,1)S(1)}, u32[]{:S(2)}, u32[]{:S(2)}) collective-permute-start(bf16[4,192,256]{2,1,0:T(8,128)(2,1)S(1)} %add4_1.1), channel_id=1, source_target_pairs={{0,4},{1,5},{2,6},{3,7},{4,0},{5,1},{6,2},{7,3},{8,12},{9,13},{10,... | collective-permute-start | bytes 1179656 | tf_op jit(solution)/shard_map/ppermute | solution.py:46
  53.7 17.1 %collective-permute-start.11 = (bf16[2,256,256]{2,1,0:T(8,128)(2,1)S(1)}, bf16[2,256,256]{2,1,0:T(8,128)(2,1)S(1)}, u32[]{:S(2)}, u32[]{:S(2)}) collective-permute-start(bf16[2,256,256]{2,1,0:T(8,128)(2,1)S(1)} %add1_2.1), channel_id=1, source_target_pairs={{0,3},{1,2},{2,1},{3,0},{4,7},{5,6},{6,5},{7,4},{8,11},{9,10},{10,... | collective-permute-start | bytes 786440 | tf_op jit(solution)/shard_map/ppermute | solution.py:46
  54.6 17.0 %collective-permute-start.10 = (bf16[4,128,256]{2,1,0:T(8,128)(2,1)S(1)}, bf16[4,128,256]{2,1,0:T(8,128)(2,1)S(1)}, u32[]{:S(2)}, u32[]{:S(2)}) collective-permute-start(bf16[4,128,256]{2,1,0:T(8,128)(2,1)S(1)} %add2_1.1), channel_id=1, source_target_pairs={{0,12},{1,13},{2,14},{3,15},{4,8},{5,9},{6,10},{7,11},{8,4},{9,5},... | collective-permute-start | bytes 786440 | tf_op jit(solution)/shard_map/ppermute | solution.py:46
  57.8 16.1 %collective-permute-start.7 = (bf16[2,256,256]{2,1,0:T(8,128)(2,1)S(1)}, bf16[2,256,256]{2,1,0:T(8,128)(2,1)S(1)}, u32[]{:S(2)}, u32[]{:S(2)}) collective-permute-start(bf16[2,256,256]{2,1,0:T(8,128)(2,1)S(1)} %add0_2.1), channel_id=1, source_target_pairs={{0,1},{1,0},{2,3},{3,2},{4,5},{5,4},{6,7},{7,6},{8,9},{9,8},{10,11... | collective-permute-start | bytes 786440 | tf_op jit(solution)/shard_map/ppermute | solution.py:46
  64.4 8.8 %collective-permute-start.9 = (bf16[2,192,256]{2,1,0:T(8,128)(2,1)S(1)}, bf16[2,192,256]{2,1,0:T(8,128)(2,1)S(1)}, u32[]{:S(2)}, u32[]{:S(2)}) collective-permute-start(bf16[2,192,256]{2,1,0:T(8,128)(2,1)S(1)} %add3_2.1), channel_id=1, source_target_pairs={{0,4},{1,5},{2,6},{3,7},{4,0},{5,1},{6,2},{7,3},{8,12},{9,13},{10,... | collective-permute-start | bytes 589832 | tf_op jit(solution)/shard_map/ppermute | solution.py:46
  66.2 18.4 %collective-permute-start.18 = (bf16[2,192,256]{2,1,0:T(8,128)(2,1)S(1)}, bf16[2,192,256]{2,1,0:T(8,128)(2,1)S(1)}, u32[]{:S(2)}, u32[]{:S(2)}) collective-permute-start(bf16[2,192,256]{2,1,0:T(8,128)(2,1)S(1)} %add4_2.1), channel_id=1, source_target_pairs={{0,3},{1,2},{2,1},{3,0},{4,7},{5,6},{6,5},{7,4},{8,11},{9,10},{10,... | collective-permute-start | bytes 589832 | tf_op jit(solution)/shard_map/ppermute | solution.py:46
  71.6 12.3 %collective-permute-start.15 = (bf16[2,128,256]{2,1,0:T(8,128)(2,1)S(1)}, bf16[2,128,256]{2,1,0:T(8,128)(2,1)S(1)}, u32[]{:S(2)}, u32[]{:S(2)}) collective-permute-start(bf16[2,128,256]{2,1,0:T(8,128)(2,1)S(1)} %add2_2.1), channel_id=1, source_target_pairs={{0,1},{1,0},{2,3},{3,2},{4,5},{5,4},{6,7},{7,6},{8,9},{9,8},{10,11... | collective-permute-start | bytes 393224 | tf_op jit(solution)/shard_map/ppermute | solution.py:46
  74.7 14.6 %collective-permute-start.13 = (bf16[1,256,256]{2,1,0:T(8,128)(2,1)}, bf16[1,256,256]{2,1,0:T(8,128)(2,1)}, u32[]{:S(2)}, u32[]{:S(2)}) collective-permute-start(bf16[1,256,256]{2,1,0:T(8,128)(2,1)} %add0_3.1), channel_id=1, source_target_pairs={{0,3},{1,2},{2,1},{3,0},{4,7},{5,6},{6,5},{7,4},{8,11},{9,10},{10,... | collective-permute-start | bytes 393224 | tf_op jit(solution)/shard_map/ppermute | solution.py:46
  75.4 13.9 %collective-permute-start.14 = (bf16[1,256,256]{2,1,0:T(8,128)(2,1)}, bf16[1,256,256]{2,1,0:T(8,128)(2,1)}, u32[]{:S(2)}, u32[]{:S(2)}) collective-permute-start(bf16[1,256,256]{2,1,0:T(8,128)(2,1)} %add1_3.1), channel_id=1, source_target_pairs={{0,1},{1,0},{2,3},{3,2},{4,5},{5,4},{6,7},{7,6},{8,9},{9,8},{10,11... | collective-permute-start | bytes 393224 | tf_op jit(solution)/shard_map/ppermute | solution.py:46
  78.6 10.7 %collective-permute-start.17 = (bf16[1,192,256]{2,1,0:T(8,128)(2,1)}, bf16[1,192,256]{2,1,0:T(8,128)(2,1)}, u32[]{:S(2)}, u32[]{:S(2)}) collective-permute-start(bf16[1,192,256]{2,1,0:T(8,128)(2,1)} %add3_3.1), channel_id=1, source_target_pairs={{0,1},{1,0},{2,3},{3,2},{4,5},{5,4},{6,7},{7,6},{8,9},{9,8},{10,11... | collective-permute-start | bytes 294920 | tf_op jit(solution)/shard_map/ppermute | solution.py:46
  85.4 9.1 %collective-permute-start.19 = (bf16[1,192,256]{2,1,0:T(8,128)(2,1)}, bf16[1,192,256]{2,1,0:T(8,128)(2,1)}, u32[]{:S(2)}, u32[]{:S(2)}) collective-permute-start(bf16[1,192,256]{2,1,0:T(8,128)(2,1)} %add4_3.1), channel_id=1, source_target_pairs={{0,12},{1,13},{2,14},{3,15},{4,8},{5,9},{6,10},{7,11},{8,4},{9,5},... | collective-permute-start | bytes 294920 | tf_op jit(solution)/shard_map/ppermute | solution.py:46
  87.7 6.7 %collective-permute-start.16 = (bf16[1,128,256]{2,1,0:T(8,128)(2,1)}, bf16[1,128,256]{2,1,0:T(8,128)(2,1)}, u32[]{:S(2)}, u32[]{:S(2)}) collective-permute-start(bf16[1,128,256]{2,1,0:T(8,128)(2,1)} %add2_3.1), channel_id=1, source_target_pairs={{0,3},{1,2},{2,1},{3,0},{4,7},{5,6},{6,5},{7,4},{8,11},{9,10},{10,... | collective-permute-start | bytes 196616 | tf_op jit(solution)/shard_map/ppermute | solution.py:46
  115.4 3.2 %collective-permute-start.22 = (f32[16,128]{1,0:T(8,128)S(1)}, f32[16,128]{1,0:T(8,128)S(1)}, u32[]{:S(2)}, u32[]{:S(2)}) collective-permute-start(f32[16,128]{1,0:T(8,128)S(1)} %get-tuple-element.59), channel_id=1, source_target_pairs={{0,144},{16,128},{32,176},{48,160},{64,208},{80,192},{96,240},{112... | collective-permute-start | bytes 24584 | tf_op jit(solution)/shard_map/ppermute | solution.py:46
  115.5 3.7 %collective-permute-start.21 = (f32[16,128]{1,0:T(8,128)S(1)}, f32[16,128]{1,0:T(8,128)S(1)}, u32[]{:S(2)}, u32[]{:S(2)}) collective-permute-start(f32[16,128]{1,0:T(8,128)S(1)} %get-tuple-element.59), channel_id=1, source_target_pairs={{0,128},{16,144},{32,160},{48,176},{64,192},{80,208},{96,224},{112... | collective-permute-start | bytes 24584 | tf_op jit(solution)/shard_map/ppermute | solution.py:46
  115.6 3.6 %collective-permute-start.20 = (f32[16,128]{1,0:T(8,128)S(1)}, f32[16,128]{1,0:T(8,128)S(1)}, u32[]{:S(2)}, u32[]{:S(2)}) collective-permute-start(f32[16,128]{1,0:T(8,128)S(1)} %get-tuple-element.59), channel_id=1, source_target_pairs={{0,16},{16,0},{32,48},{48,32},{64,80},{80,64},{96,112},{112,96},{1... | collective-permute-start | bytes 24584 | tf_op jit(solution)/shard_map/ppermute | solution.py:46
  119.3 5.8 %collective-permute-start.25 = (f32[16,128]{1,0:T(8,128)S(1)}, f32[16,128]{1,0:T(8,128)S(1)}, u32[]{:S(2)}, u32[]{:S(2)}) collective-permute-start(f32[16,128]{1,0:T(8,128)S(1)} %add_add_fusion.a_ref), channel_id=1, source_target_pairs={{0,96},{16,112},{32,64},{48,80},{64,32},{80,48},{96,0},{112,16},{1... | collective-permute-start | bytes 24584 | tf_op jit(solution)/shard_map/ppermute | solution.py:46
  122.4 5.2 %collective-permute-start.24 = (f32[16,128]{1,0:T(8,128)S(1)}, f32[16,128]{1,0:T(8,128)S(1)}, u32[]{:S(2)}, u32[]{:S(2)}) collective-permute-start(f32[16,128]{1,0:T(8,128)S(1)} %add_add_fusion.a_ref), channel_id=1, source_target_pairs={{0,64},{16,80},{32,96},{48,112},{64,0},{80,16},{96,32},{112,48},{1... | collective-permute-start | bytes 24584 | tf_op jit(solution)/shard_map/ppermute | solution.py:46
  123.0 4.5 %collective-permute-start.23 = (f32[16,128]{1,0:T(8,128)S(1)}, f32[16,128]{1,0:T(8,128)S(1)}, u32[]{:S(2)}, u32[]{:S(2)}) collective-permute-start(f32[16,128]{1,0:T(8,128)S(1)} %add_add_fusion.a_ref), channel_id=1, source_target_pairs={{0,32},{16,48},{32,0},{48,16},{64,96},{80,112},{96,64},{112,80},{1... | collective-permute-start | bytes 24584 | tf_op jit(solution)/shard_map/ppermute | solution.py:46
  (30 other events, 191.7 us)

commit v5 on v4

--- a/solution.py
+++ b/solution.py
@@ -173,8 +173,10 @@
     )(*held)
 
 
-def band_tables(band, rows):
-    width = band.shape[1]
+def band_tables(band_ref, rows):
+    width = 4 * BAND
+    place = lax.broadcasted_iota(jnp.int32, (1, width), 1) // 4
+    band = functools.reduce(jnp.add, [jnp.where(place == k, band_ref[k], 0) for k in range(BAND)])
     column = lax.broadcasted_iota(jnp.int32, (64, width), 1) % 4 * LOW + band % BLOCK
     pick = (lax.broadcasted_iota(jnp.int32, (64, width), 0) == column).astype(jnp.bfloat16)
     keep = (lax.broadcasted_iota(jnp.int32, (rows, width), 0) % LOW == band // BLOCK).astype(jnp.float32)
@@ -201,7 +203,7 @@
     updated = DECAY * mom_ref[0] + jnp.concatenate(turned, axis=1)
     updated_ref[...] = updated
     coeff = forward(updated, low_ref[...])
-    pick, keep, gather = band_tables(band_ref[...], coeff.shape[0])
+    pick, keep, gather = band_tables(band_ref, coeff.shape[0])
     picked = both_of(coeff, pick) * keep
     first, second = split(picked)
     chosen_ref[...] = dot(gather, first) + dot(gather, second)
@@ -213,7 +215,7 @@
     arrays = [a for chain in held for a in chain]
     return pl.pallas_call(
         functools.partial(coeff_kernel, [len(chain) for chain in held]),
-        in_specs=[IN_VMEM] * (len(arrays) + 3),
+        in_specs=[IN_VMEM] * (len(arrays) + 1) + [pl.BlockSpec(memory_space=pltpu.SMEM), IN_VMEM],
         out_specs=[IN_VMEM] * 3,
         out_shape=[
             jax.ShapeDtypeStruct((rows, ncol), jnp.float32),
@@ -243,7 +245,7 @@
 
 def update_kernel(scale, a_ref, b_ref, c_ref, d_ref, band_ref, low_ref, out_ref):
     total = (a_ref[...] + b_ref[...]) + (c_ref[...] + d_ref[...])
-    pick, keep, gather = band_tables(band_ref[...], LOW * total.shape[0])
+    pick, keep, gather = band_tables(band_ref, LOW * total.shape[0])
     first, second = split(total)
     spread = (dot(gather, first, ((0,), (0,))) + dot(gather, second, ((0,), (0,)))) * keep
     coeff = both_of(spread, pick, ((1,), (1,)))
@@ -253,7 +255,7 @@
 def make_update(parts, band, low, ncols, scale):
     return pl.pallas_call(
         functools.partial(update_kernel, scale),
-        in_specs=[IN_VMEM] * 6,
+        in_specs=[IN_VMEM] * 4 + [pl.BlockSpec(memory_space=pltpu.SMEM), IN_VMEM],
         out_shape=jax.ShapeDtypeStruct((ROWS, ncols), jnp.bfloat16),
         compiler_params=pltpu.CompilerParams(vmem_limit_bytes=VMEM),
         name="update",
@@ -276,7 +278,6 @@
         held[c].append(swap(send, "fsdp", CHAINS[c][1][stage]))
         before = send if stage else before
 
-    band = jnp.repeat(band, 4)[None]
     updated, coeffs, chosen = coefficients(held, momentum, band, low)
     fresh = new_momentum(updated, coeffs, low, momentum.shape)
     a, b, c, d = [chosen] + [swap(chosen, "rep", m) for m in (1, 8, 9)]

time: 130 us -> 108 us (0.83)
  the two profiles are of different devices: /device:TPU:64 before, /device:TPU:6 now
where the time goes in v5:
time: 108 us; the launch traced here: 107 us
  starting transfers between devices  46.7 us (43%)
  waiting for transfers between devices  38 us (35%)
  Pallas kernels  21.9 us (20%)
    ppermute x26, starting transfers between devices, swap(): return lax.ppermute(value, axis, [(i, i ^ mask) for i in range(n)])  46.7 us
    ppermute x26, waiting for transfers between devices, swap(): return lax.ppermute(value, axis, [(i, i ^ mask) for i in range(n)])  38 us
    pallas_call x2, Pallas kernels, terms(): pl.pallas_call(functools.partial(terms_kernel, kept), in_specs=[pl.BlockS...  15.1 us
    pallas_call x1, Pallas kernels, make_update(): pl.pallas_call(functools.partial(update_kernel, scale), in_specs=[IN_VMEM...  2.29 us
  transfers between devices with their start and end apart: 26, of which 12 were waited for; matrix products, arithmetic and copies ran while one was open for 0% of the time, Pallas kernels for 9%

profile of v5, /device:TPU:6, one launch (start us, length us, event | category | flops | bytes accessed | tf_op | source)
XLA Modules:
  0.0 107.5 jit_solution(15273286039244442338)
XLA Ops:
  0.6 8.2 %terms_sent.1 = (bf16[8,256,256]{2,1,0:T(8,128)(2,1)S(1)}, bf16[8,256,256]{2,1,0:T(8,128)(2,1)}, bf16[8,128,256]{2,1,0:T(8,128)(2,1)S(1)}, bf16[8,192,256]{2,1,0:T(8,128)(2,1)S(1)}, bf16[8,192,256]{2,1,0:T(8,128)(2,1)S(1)}) custom-call(bf16[896,4096]{1,0:T(8,128)(2,1)} %act_ref.3, bf16[896,1024]{1,0:T(8,128)(2,1)} %cot_ref.2), custom_call_target="tpu_custom_call" | custom-call | flops 3758096384 | bytes 7340032 | tf_op jit(solution)/shard_map/terms_sent/pallas_call | solution.py:103
  8.8 0.9 collective-permute-start.1
  9.8 1.5 %collective-permute-start = (bf16[8,256,256]{2,1,0:T(8,128)(2,1)S(1)}, bf16[8,256,256]{2,1,0:T(8,128)(2,1)S(1)}, u32[]{:S(2)}, u32[]{:S(2)}) collective-permute-start(bf16[8,256,256]{2,1,0:T(8,128)(2,1)S(1)} %get-tuple-element.31), channel_id=1, source_target_pairs={{0,12},{1,13},{2,14},{3,15},{4,8},{5,9},{6,10},{7,11},{8,4},{9,5},... | collective-permute-start | bytes 3145736 | tf_op jit(solution)/shard_map/ppermute | solution.py:46
  11.2 5.9 %collective-permute-start.6 = (bf16[8,192,256]{2,1,0:T(8,128)(2,1)S(1)}, bf16[8,192,256]{2,1,0:T(8,128)(2,1)S(1)}, u32[]{:S(2)}, u32[]{:S(2)}) collective-permute-start(bf16[8,192,256]{2,1,0:T(8,128)(2,1)S(1)} %get-tuple-element.43), channel_id=1, source_target_pairs={{0,3},{1,2},{2,1},{3,0},{4,7},{5,6},{6,5},{7,4},{8,11},{9,10},{10,... | collective-permute-start | bytes 2359304 | tf_op jit(solution)/shard_map/ppermute | solution.py:46
  17.2 1.4 %collective-permute-start.4 = (bf16[8,192,256]{2,1,0:T(8,128)(2,1)S(1)}, bf16[8,192,256]{2,1,0:T(8,128)(2,1)S(1)}, u32[]{:S(2)}, u32[]{:S(2)}) collective-permute-start(bf16[8,192,256]{2,1,0:T(8,128)(2,1)S(1)} %get-tuple-element.39), channel_id=1, source_target_pairs={{0,1},{1,0},{2,3},{3,2},{4,5},{5,4},{6,7},{7,6},{8,9},{9,8},{10,11... | collective-permute-start | bytes 2359304 | tf_op jit(solution)/shard_map/ppermute | solution.py:46
  18.7 6.9 %terms_kept.1 = (bf16[8,256,256]{2,1,0:T(8,128)(2,1)S(1)}, bf16[8,256,256]{2,1,0:T(8,128)(2,1)S(1)}, bf16[8,128,256]{2,1,0:T(8,128)(2,1)S(1)}, bf16[8,192,256]{2,1,0:T(8,128)(2,1)S(1)}, bf16[8,192,256]{2,1,0:T(8,128)(2,1)S(1)}) custom-call(bf16[896,4096]{1,0:T(8,128)(2,1)} %act_ref.3, bf16[896,1024]{1,0:T(8,128)(2,1)S(1)} %copy-done.3), custom_call_target="tpu_custom_call" | custom-call | flops 3758096384 | bytes 7340032 | tf_op jit(solution)/shard_map/terms_kept/pallas_call | solution.py:103
  25.6 9.6 %collective-permute-done.1.refs_1_.refs_6_ = bf16[8,256,256]{2,1,0:T(8,128)(2,1)S(1)} collective-permute-done((bf16[8,256,256]{2,1,0:T(8,128)(2,1)}, bf16[8,256,256]{2,1,0:T(8,128)(2,1)S(1)}, u32[]{:S(2)}, u32[]{:S(2)}) %collective-permute-start.1) | collective-permute-done | bytes 1048608 | tf_op jit(solution)/shard_map/ppermute | solution.py:46
  35.3 2.5 %collective-permute-start.3 = (bf16[4,256,256]{2,1,0:T(8,128)(2,1)S(1)}, bf16[4,256,256]{2,1,0:T(8,128)(2,1)S(1)}, u32[]{:S(2)}, u32[]{:S(2)}) collective-permute-start(bf16[4,256,256]{2,1,0:T(8,128)(2,1)S(1)} %add1_1.1), channel_id=1, source_target_pairs={{0,12},{1,13},{2,14},{3,15},{4,8},{5,9},{6,10},{7,11},{8,4},{9,5},... | collective-permute-start | bytes 1572872 | tf_op jit(solution)/shard_map/ppermute | solution.py:46
  38.1 12.2 %collective-permute-done.6.refs_1_.refs_16_ = bf16[8,192,256]{2,1,0:T(8,128)(2,1)S(1)} collective-permute-done((bf16[8,192,256]{2,1,0:T(8,128)(2,1)S(1)}, bf16[8,192,256]{2,1,0:T(8,128)(2,1)S(1)}, u32[]{:S(2)}, u32[]{:S(2)}) %collective-permute-start.6) | collective-permute-done | bytes 786464 | tf_op jit(solution)/shard_map/ppermute | solution.py:46
  50.4 2.2 %collective-permute-start.8 = (bf16[4,192,256]{2,1,0:T(8,128)(2,1)S(1)}, bf16[4,192,256]{2,1,0:T(8,128)(2,1)S(1)}, u32[]{:S(2)}, u32[]{:S(2)}) collective-permute-start(bf16[4,192,256]{2,1,0:T(8,128)(2,1)S(1)} %add3_1.1), channel_id=1, source_target_pairs={{0,12},{1,13},{2,14},{3,15},{4,8},{5,9},{6,10},{7,11},{8,4},{9,5},... | collective-permute-start | bytes 1179656 | tf_op jit(solution)/shard_map/ppermute | solution.py:46
  54.0 3.6 %collective-permute-start.11 = (bf16[2,256,256]{2,1,0:T(8,128)(2,1)S(1)}, bf16[2,256,256]{2,1,0:T(8,128)(2,1)S(1)}, u32[]{:S(2)}, u32[]{:S(2)}) collective-permute-start(bf16[2,256,256]{2,1,0:T(8,128)(2,1)S(1)} %add1_2.1), channel_id=1, source_target_pairs={{0,3},{1,2},{2,1},{3,0},{4,7},{5,6},{6,5},{7,4},{8,11},{9,10},{10,... | collective-permute-start | bytes 786440 | tf_op jit(solution)/shard_map/ppermute | solution.py:46
  57.6 1.1 %collective-permute-start.10 = (bf16[4,128,256]{2,1,0:T(8,128)(2,1)S(1)}, bf16[4,128,256]{2,1,0:T(8,128)(2,1)S(1)}, u32[]{:S(2)}, u32[]{:S(2)}) collective-permute-start(bf16[4,128,256]{2,1,0:T(8,128)(2,1)S(1)} %add2_1.1), channel_id=1, source_target_pairs={{0,12},{1,13},{2,14},{3,15},{4,8},{5,9},{6,10},{7,11},{8,4},{9,5},... | collective-permute-start | bytes 786440 | tf_op jit(solution)/shard_map/ppermute | solution.py:46
  58.9 2.2 %collective-permute-start.7 = (bf16[2,256,256]{2,1,0:T(8,128)(2,1)S(1)}, bf16[2,256,256]{2,1,0:T(8,128)(2,1)S(1)}, u32[]{:S(2)}, u32[]{:S(2)}) collective-permute-start(bf16[2,256,256]{2,1,0:T(8,128)(2,1)S(1)} %add0_2.1), channel_id=1, source_target_pairs={{0,1},{1,0},{2,3},{3,2},{4,5},{5,4},{6,7},{7,6},{8,9},{9,8},{10,11... | collective-permute-start | bytes 786440 | tf_op jit(solution)/shard_map/ppermute | solution.py:46
  61.1 2.6 %collective-permute-done.8.refs_2_.refs_17_ = bf16[4,192,256]{2,1,0:T(8,128)(2,1)S(1)} collective-permute-done((bf16[4,192,256]{2,1,0:T(8,128)(2,1)S(1)}, bf16[4,192,256]{2,1,0:T(8,128)(2,1)S(1)}, u32[]{:S(2)}, u32[]{:S(2)}) %collective-permute-start.8) | collective-permute-done | bytes 393248 | tf_op jit(solution)/shard_map/ppermute | solution.py:46
  63.9 2.1 %collective-permute-done.12.refs_2_.refs_22_ = bf16[4,192,256]{2,1,0:T(8,128)(2,1)S(1)} collective-permute-done((bf16[4,192,256]{2,1,0:T(8,128)(2,1)S(1)}, bf16[4,192,256]{2,1,0:T(8,128)(2,1)S(1)}, u32[]{:S(2)}, u32[]{:S(2)}) %collective-permute-start.12) | collective-permute-done | bytes 393248 | tf_op jit(solution)/shard_map/ppermute | solution.py:46
  66.2 6.4 %collective-permute-start.18 = (bf16[2,192,256]{2,1,0:T(8,128)(2,1)S(1)}, bf16[2,192,256]{2,1,0:T(8,128)(2,1)S(1)}, u32[]{:S(2)}, u32[]{:S(2)}) collective-permute-start(bf16[2,192,256]{2,1,0:T(8,128)(2,1)S(1)} %add4_2.1), channel_id=1, source_target_pairs={{0,3},{1,2},{2,1},{3,0},{4,7},{5,6},{6,5},{7,4},{8,11},{9,10},{10,... | collective-permute-start | bytes 589832 | tf_op jit(solution)/shard_map/ppermute | solution.py:46
  72.7 1.5 %collective-permute-start.15 = (bf16[2,128,256]{2,1,0:T(8,128)(2,1)S(1)}, bf16[2,128,256]{2,1,0:T(8,128)(2,1)S(1)}, u32[]{:S(2)}, u32[]{:S(2)}) collective-permute-start(bf16[2,128,256]{2,1,0:T(8,128)(2,1)S(1)} %add2_2.1), channel_id=1, source_target_pairs={{0,1},{1,0},{2,3},{3,2},{4,5},{5,4},{6,7},{7,6},{8,9},{9,8},{10,11... | collective-permute-start | bytes 393224 | tf_op jit(solution)/shard_map/ppermute | solution.py:46
  74.4 2.6 %collective-permute-start.13 = (bf16[1,256,256]{2,1,0:T(8,128)(2,1)S(1)}, bf16[1,256,256]{2,1,0:T(8,128)(2,1)S(1)}, u32[]{:S(2)}, u32[]{:S(2)}) collective-permute-start(bf16[1,256,256]{2,1,0:T(8,128)(2,1)S(1)} %add0_3.1), channel_id=1, source_target_pairs={{0,3},{1,2},{2,1},{3,0},{4,7},{5,6},{6,5},{7,4},{8,11},{9,10},{10,... | collective-permute-start | bytes 393224 | tf_op jit(solution)/shard_map/ppermute | solution.py:46
  77.0 1.3 %collective-permute-start.14 = (bf16[1,256,256]{2,1,0:T(8,128)(2,1)S(1)}, bf16[1,256,256]{2,1,0:T(8,128)(2,1)S(1)}, u32[]{:S(2)}, u32[]{:S(2)}) collective-permute-start(bf16[1,256,256]{2,1,0:T(8,128)(2,1)S(1)} %add1_3.1), channel_id=1, source_target_pairs={{0,1},{1,0},{2,3},{3,2},{4,5},{5,4},{6,7},{7,6},{8,9},{9,8},{10,11... | collective-permute-start | bytes 393224 | tf_op jit(solution)/shard_map/ppermute | solution.py:46
  78.3 1.6 %collective-permute-start.17 = (bf16[1,192,256]{2,1,0:T(8,128)(2,1)S(1)}, bf16[1,192,256]{2,1,0:T(8,128)(2,1)S(1)}, u32[]{:S(2)}, u32[]{:S(2)}) collective-permute-start(bf16[1,192,256]{2,1,0:T(8,128)(2,1)S(1)} %add3_3.1), channel_id=1, source_target_pairs={{0,1},{1,0},{2,3},{3,2},{4,5},{5,4},{6,7},{7,6},{8,9},{9,8},{10,11... | collective-permute-start | bytes 294920 | tf_op jit(solution)/shard_map/ppermute | solution.py:46
  79.9 1.0 collective-permute-done.15.refs_3_.refs_13_
  81.0 1.9 %collective-permute-done.18.refs_3_.refs_23_ = bf16[2,192,256]{2,1,0:T(8,128)(2,1)S(1)} collective-permute-done((bf16[2,192,256]{2,1,0:T(8,128)(2,1)S(1)}, bf16[2,192,256]{2,1,0:T(8,128)(2,1)S(1)}, u32[]{:S(2)}, u32[]{:S(2)}) %collective-permute-start.18) | collective-permute-done | bytes 196640 | tf_op jit(solution)/shard_map/ppermute | solution.py:46
  83.1 4.9 %collective-permute-start.16 = (bf16[1,128,256]{2,1,0:T(8,128)(2,1)S(1)}, bf16[1,128,256]{2,1,0:T(8,128)(2,1)S(1)}, u32[]{:S(2)}, u32[]{:S(2)}) collective-permute-start(bf16[1,128,256]{2,1,0:T(8,128)(2,1)S(1)} %add2_3.1), channel_id=1, source_target_pairs={{0,3},{1,2},{2,1},{3,0},{4,7},{5,6},{6,5},{7,4},{8,11},{9,10},{10,... | collective-permute-start | bytes 196616 | tf_op jit(solution)/shard_map/ppermute | solution.py:46
  88.0 2.0 %collective-permute-done.17.refs_19_ = bf16[1,192,256]{2,1,0:T(8,128)(2,1)S(1)} collective-permute-done((bf16[1,192,256]{2,1,0:T(8,128)(2,1)S(1)}, bf16[1,192,256]{2,1,0:T(8,128)(2,1)S(1)}, u32[]{:S(2)}, u32[]{:S(2)}) %collective-permute-start.17) | collective-permute-done | bytes 98336 | tf_op jit(solution)/shard_map/ppermute | solution.py:46
  90.0 1.2 %collective-permute-done.16.refs_14_ = bf16[1,128,256]{2,1,0:T(8,128)(2,1)S(1)} collective-permute-done((bf16[1,128,256]{2,1,0:T(8,128)(2,1)S(1)}, bf16[1,128,256]{2,1,0:T(8,128)(2,1)S(1)}, u32[]{:S(2)}, u32[]{:S(2)}) %collective-permute-start.16) | collective-permute-done | bytes 65568 | tf_op jit(solution)/shard_map/ppermute | solution.py:46
  91.2 1.8 %coefficients.1 = (f32[256,1024]{1,0:T(8,128)S(1)}, f32[256,64]{1,0:T(8,128)S(1)}, f32[16,128]{1,0:T(8,128)S(1)}) custom-call(bf16[8,256,256]{2,1,0:T(8,128)(2,1)S(1)} %get-tuple-element.33.refs_0_, bf16[8,256,256]{2,1,0:T(8,128)(2,1)S(1)} %collective-permute-done.refs_1_, bf16[4,256,256]{2,1,0:T(8,128)(2,1)S(1)} %collective-permute-done.2.refs_2_, ...), custom_call_target="tpu_custom_call" | custom-call | flops 1024000000 | bytes 2097152 | tf_op jit(solution)/shard_map/coefficients/pallas_call | solution.py:216
  93.3 1.7 %collective-permute-start.20 = (f32[16,128]{1,0:T(8,128)S(1)}, f32[16,128]{1,0:T(8,128)S(1)}, u32[]{:S(2)}, u32[]{:S(2)}) collective-permute-start(f32[16,128]{1,0:T(8,128)S(1)} %get-tuple-element.59), channel_id=1, source_target_pairs={{0,16},{16,0},{32,48},{48,32},{64,80},{80,64},{96,112},{112,96},{1... | collective-permute-start | bytes 24584 | tf_op jit(solution)/shard_map/ppermute | solution.py:46
  95.0 1.2 %collective-permute-done.22 = f32[16,128]{1,0:T(8,128)S(1)} collective-permute-done((f32[16,128]{1,0:T(8,128)S(1)}, f32[16,128]{1,0:T(8,128)S(1)}, u32[]{:S(2)}, u32[]{:S(2)}) %collective-permute-start.22) | collective-permute-done | bytes 8224 | tf_op jit(solution)/shard_map/ppermute | solution.py:46
  96.9 3.1 %collective-permute-start.25 = (f32[16,128]{1,0:T(8,128)S(1)}, f32[16,128]{1,0:T(8,128)S(1)}, u32[]{:S(2)}, u32[]{:S(2)}) collective-permute-start(f32[16,128]{1,0:T(8,128)S(1)} %add_add_fusion.a_ref), channel_id=1, source_target_pairs={{0,96},{16,112},{32,64},{48,80},{64,32},{80,48},{96,0},{112,16},{1... | collective-permute-start | bytes 24584 | tf_op jit(solution)/shard_map/ppermute | solution.py:46
  101.1 1.6 %new_momentum.1 = f32[1,256,1024]{2,1,0:T(8,128)} custom-call(f32[256,1024]{1,0:T(8,128)S(1)} %get-tuple-element.57.updated_ref, f32[256,64]{1,0:T(8,128)S(1)} %get-tuple-element.58.coeff_ref, bf16[128,256]{1,0:T(8,128)(2,1)S(1)} %copy-done.1), custom_call_target="tpu_custom_call" | custom-call | flops 2000000000 | bytes 2000000 | tf_op jit(solution)/shard_map/new_momentum/pallas_call | solution.py:236
  102.7 2.5 %collective-permute-done.24.c_ref = f32[16,128]{1,0:T(8,128)S(1)} collective-permute-done((f32[16,128]{1,0:T(8,128)S(1)}, f32[16,128]{1,0:T(8,128)S(1)}, u32[]{:S(2)}, u32[]{:S(2)}) %collective-permute-start.24) | collective-permute-done | bytes 8224 | tf_op jit(solution)/shard_map/ppermute | solution.py:46
  105.2 2.3 %update.1 = bf16[256,1024]{1,0:T(8,128)(2,1)} custom-call(f32[16,128]{1,0:T(8,128)S(1)} %add_add_fusion.a_ref, f32[16,128]{1,0:T(8,128)S(1)} %collective-permute-done.23.b_ref, f32[16,128]{1,0:T(8,128)S(1)} %collective-permute-done.24.c_ref, f32[16,128]{1,0:T(8,128)S(1)} %collective-permute-done.25.d_ref, s32[32]{0:T(128)S(1)} %copy-done.2, ...), custom_call_target="tpu_custom_call" | custom-call | tf_op jit(solution)/shard_map/update/pallas_call | solution.py:256
  (49 shorter events, 4.7 us)
Async XLA Ops:
  0.6 18.1 %copy-start.3 = (bf16[896,1024]{1,0:T(8,128)(2,1)S(1)}, bf16[896,1024]{1,0:T(8,128)(2,1)}, u32[]{:S(2)}) copy-start(bf16[896,1024]{1,0:T(8,128)(2,1)} %cot_ref.2) | copy-start | bytes 5505028
  8.8 26.3 %collective-permute-start.1 = (bf16[8,256,256]{2,1,0:T(8,128)(2,1)}, bf16[8,256,256]{2,1,0:T(8,128)(2,1)S(1)}, u32[]{:S(2)}, u32[]{:S(2)}) collective-permute-start(bf16[8,256,256]{2,1,0:T(8,128)(2,1)} %get-tuple-element.35), channel_id=1, source_target_pairs={{0,4},{1,5},{2,6},{3,7},{4,0},{5,1},{6,2},{7,3},{8,12},{9,13},{10,... | collective-permute-start | bytes 3145736 | tf_op jit(solution)/shard_map/ppermute | solution.py:46
  9.8 28.1 %collective-permute-start = (bf16[8,256,256]{2,1,0:T(8,128)(2,1)S(1)}, bf16[8,256,256]{2,1,0:T(8,128)(2,1)S(1)}, u32[]{:S(2)}, u32[]{:S(2)}) collective-permute-start(bf16[8,256,256]{2,1,0:T(8,128)(2,1)S(1)} %get-tuple-element.31), channel_id=1, source_target_pairs={{0,12},{1,13},{2,14},{3,15},{4,8},{5,9},{6,10},{7,11},{8,4},{9,5},... | collective-permute-start | bytes 3145736 | tf_op jit(solution)/shard_map/ppermute | solution.py:46
  11.2 39.0 %collective-permute-start.6 = (bf16[8,192,256]{2,1,0:T(8,128)(2,1)S(1)}, bf16[8,192,256]{2,1,0:T(8,128)(2,1)S(1)}, u32[]{:S(2)}, u32[]{:S(2)}) collective-permute-start(bf16[8,192,256]{2,1,0:T(8,128)(2,1)S(1)} %get-tuple-element.43), channel_id=1, source_target_pairs={{0,3},{1,2},{2,1},{3,0},{4,7},{5,6},{6,5},{7,4},{8,11},{9,10},{10,... | collective-permute-start | bytes 2359304 | tf_op jit(solution)/shard_map/ppermute | solution.py:46
  17.2 36.2 %collective-permute-start.4 = (bf16[8,192,256]{2,1,0:T(8,128)(2,1)S(1)}, bf16[8,192,256]{2,1,0:T(8,128)(2,1)S(1)}, u32[]{:S(2)}, u32[]{:S(2)}) collective-permute-start(bf16[8,192,256]{2,1,0:T(8,128)(2,1)S(1)} %get-tuple-element.39), channel_id=1, source_target_pairs={{0,1},{1,0},{2,3},{3,2},{4,5},{5,4},{6,7},{7,6},{8,9},{9,8},{10,11... | collective-permute-start | bytes 2359304 | tf_op jit(solution)/shard_map/ppermute | solution.py:46
  18.6 33.9 %collective-permute-start.5 = (bf16[8,128,256]{2,1,0:T(8,128)(2,1)S(1)}, bf16[8,128,256]{2,1,0:T(8,128)(2,1)S(1)}, u32[]{:S(2)}, u32[]{:S(2)}) collective-permute-start(bf16[8,128,256]{2,1,0:T(8,128)(2,1)S(1)} %get-tuple-element.41), channel_id=1, source_target_pairs={{0,4},{1,5},{2,6},{3,7},{4,0},{5,1},{6,2},{7,3},{8,12},{9,13},{10,... | collective-permute-start | bytes 1572872 | tf_op jit(solution)/shard_map/ppermute | solution.py:46
  35.3 18.6 %collective-permute-start.3 = (bf16[4,256,256]{2,1,0:T(8,128)(2,1)S(1)}, bf16[4,256,256]{2,1,0:T(8,128)(2,1)S(1)}, u32[]{:S(2)}, u32[]{:S(2)}) collective-permute-start(bf16[4,256,256]{2,1,0:T(8,128)(2,1)S(1)} %add1_1.1), channel_id=1, source_target_pairs={{0,12},{1,13},{2,14},{3,15},{4,8},{5,9},{6,10},{7,11},{8,4},{9,5},... | collective-permute-start | bytes 1572872 | tf_op jit(solution)/shard_map/ppermute | solution.py:46
  38.0 20.8 %collective-permute-start.2 = (bf16[4,256,256]{2,1,0:T(8,128)(2,1)S(1)}, bf16[4,256,256]{2,1,0:T(8,128)(2,1)S(1)}, u32[]{:S(2)}, u32[]{:S(2)}) collective-permute-start(bf16[4,256,256]{2,1,0:T(8,128)(2,1)S(1)} %add0_1.1), channel_id=1, source_target_pairs={{0,4},{1,5},{2,6},{3,7},{4,0},{5,1},{6,2},{7,3},{8,12},{9,13},{10,... | collective-permute-start | bytes 1572872 | tf_op jit(solution)/shard_map/ppermute | solution.py:46
  50.4 13.3 %collective-permute-start.8 = (bf16[4,192,256]{2,1,0:T(8,128)(2,1)S(1)}, bf16[4,192,256]{2,1,0:T(8,128)(2,1)S(1)}, u32[]{:S(2)}, u32[]{:S(2)}) collective-permute-start(bf16[4,192,256]{2,1,0:T(8,128)(2,1)S(1)} %add3_1.1), channel_id=1, source_target_pairs={{0,12},{1,13},{2,14},{3,15},{4,8},{5,9},{6,10},{7,11},{8,4},{9,5},... | collective-permute-start | bytes 1179656 | tf_op jit(solution)/shard_map/ppermute | solution.py:46
  53.5 12.6 %collective-permute-start.12 = (bf16[4,192,256]{2,1,0:T(8,128)(2,1)S(1)}, bf16[4,192,256]{2,1,0:T(8,128)(2,1)S(1)}, u32[]{:S(2)}, u32[]{:S(2)}) collective-permute-start(bf16[4,192,256]{2,1,0:T(8,128)(2,1)S(1)} %add4_1.1), channel_id=1, source_target_pairs={{0,4},{1,5},{2,6},{3,7},{4,0},{5,1},{6,2},{7,3},{8,12},{9,13},{10,... | collective-permute-start | bytes 1179656 | tf_op jit(solution)/shard_map/ppermute | solution.py:46
  54.0 18.5 %collective-permute-start.11 = (bf16[2,256,256]{2,1,0:T(8,128)(2,1)S(1)}, bf16[2,256,256]{2,1,0:T(8,128)(2,1)S(1)}, u32[]{:S(2)}, u32[]{:S(2)}) collective-permute-start(bf16[2,256,256]{2,1,0:T(8,128)(2,1)S(1)} %add1_2.1), channel_id=1, source_target_pairs={{0,3},{1,2},{2,1},{3,0},{4,7},{5,6},{6,5},{7,4},{8,11},{9,10},{10,... | collective-permute-start | bytes 786440 | tf_op jit(solution)/shard_map/ppermute | solution.py:46
  57.6 15.0 %collective-permute-start.10 = (bf16[4,128,256]{2,1,0:T(8,128)(2,1)S(1)}, bf16[4,128,256]{2,1,0:T(8,128)(2,1)S(1)}, u32[]{:S(2)}, u32[]{:S(2)}) collective-permute-start(bf16[4,128,256]{2,1,0:T(8,128)(2,1)S(1)} %add2_1.1), channel_id=1, source_target_pairs={{0,12},{1,13},{2,14},{3,15},{4,8},{5,9},{6,10},{7,11},{8,4},{9,5},... | collective-permute-start | bytes 786440 | tf_op jit(solution)/shard_map/ppermute | solution.py:46
  58.9 15.4 %collective-permute-start.7 = (bf16[2,256,256]{2,1,0:T(8,128)(2,1)S(1)}, bf16[2,256,256]{2,1,0:T(8,128)(2,1)S(1)}, u32[]{:S(2)}, u32[]{:S(2)}) collective-permute-start(bf16[2,256,256]{2,1,0:T(8,128)(2,1)S(1)} %add0_2.1), channel_id=1, source_target_pairs={{0,1},{1,0},{2,3},{3,2},{4,5},{5,4},{6,7},{7,6},{8,9},{9,8},{10,11... | collective-permute-start | bytes 786440 | tf_op jit(solution)/shard_map/ppermute | solution.py:46
  63.8 27.4 %copy-start = (f32[1,256,1024]{2,1,0:T(8,128)S(1)}, f32[1,256,1024]{2,1,0:T(8,128)}, u32[]{:S(2)}) copy-start(f32[1,256,1024]{2,1,0:T(8,128)} %refs_25_.1) | copy-start | bytes 3145732
  63.8 27.4 %copy-start.1 = (bf16[128,256]{1,0:T(8,128)(2,1)S(1)}, bf16[128,256]{1,0:T(8,128)(2,1)}, u32[]{:S(2)}) copy-start(bf16[128,256]{1,0:T(8,128)(2,1)} %constant.2.clone.refs_27_.low_ref) | copy-start | bytes 196612
  63.8 27.4 %copy-start.2 = (s32[32]{0:T(128)S(1)}, s32[32]{0:T(128)}, u32[]{:S(2)}) copy-start(s32[32]{0:T(128)} %band_ref.1) | copy-start | bytes 388
  63.8 10.4 %collective-permute-start.9 = (bf16[2,192,256]{2,1,0:T(8,128)(2,1)S(1)}, bf16[2,192,256]{2,1,0:T(8,128)(2,1)S(1)}, u32[]{:S(2)}, u32[]{:S(2)}) collective-permute-start(bf16[2,192,256]{2,1,0:T(8,128)(2,1)S(1)} %add3_2.1), channel_id=1, source_target_pairs={{0,4},{1,5},{2,6},{3,7},{4,0},{5,1},{6,2},{7,3},{8,12},{9,13},{10,... | collective-permute-start | bytes 589832 | tf_op jit(solution)/shard_map/ppermute | solution.py:46
  66.2 16.8 %collective-permute-start.18 = (bf16[2,192,256]{2,1,0:T(8,128)(2,1)S(1)}, bf16[2,192,256]{2,1,0:T(8,128)(2,1)S(1)}, u32[]{:S(2)}, u32[]{:S(2)}) collective-permute-start(bf16[2,192,256]{2,1,0:T(8,128)(2,1)S(1)} %add4_2.1), channel_id=1, source_target_pairs={{0,3},{1,2},{2,1},{3,0},{4,7},{5,6},{6,5},{7,4},{8,11},{9,10},{10,... | collective-permute-start | bytes 589832 | tf_op jit(solution)/shard_map/ppermute | solution.py:46
  72.7 8.3 %collective-permute-start.15 = (bf16[2,128,256]{2,1,0:T(8,128)(2,1)S(1)}, bf16[2,128,256]{2,1,0:T(8,128)(2,1)S(1)}, u32[]{:S(2)}, u32[]{:S(2)}) collective-permute-start(bf16[2,128,256]{2,1,0:T(8,128)(2,1)S(1)} %add2_2.1), channel_id=1, source_target_pairs={{0,1},{1,0},{2,3},{3,2},{4,5},{5,4},{6,7},{7,6},{8,9},{9,8},{10,11... | collective-permute-start | bytes 393224 | tf_op jit(solution)/shard_map/ppermute | solution.py:46
  74.4 15.6 %collective-permute-start.13 = (bf16[1,256,256]{2,1,0:T(8,128)(2,1)S(1)}, bf16[1,256,256]{2,1,0:T(8,128)(2,1)S(1)}, u32[]{:S(2)}, u32[]{:S(2)}) collective-permute-start(bf16[1,256,256]{2,1,0:T(8,128)(2,1)S(1)} %add0_3.1), channel_id=1, source_target_pairs={{0,3},{1,2},{2,1},{3,0},{4,7},{5,6},{6,5},{7,4},{8,11},{9,10},{10,... | collective-permute-start | bytes 393224 | tf_op jit(solution)/shard_map/ppermute | solution.py:46
  77.0 13.0 %collective-permute-start.14 = (bf16[1,256,256]{2,1,0:T(8,128)(2,1)S(1)}, bf16[1,256,256]{2,1,0:T(8,128)(2,1)S(1)}, u32[]{:S(2)}, u32[]{:S(2)}) collective-permute-start(bf16[1,256,256]{2,1,0:T(8,128)(2,1)S(1)} %add1_3.1), channel_id=1, source_target_pairs={{0,1},{1,0},{2,3},{3,2},{4,5},{5,4},{6,7},{7,6},{8,9},{9,8},{10,11... | collective-permute-start | bytes 393224 | tf_op jit(solution)/shard_map/ppermute | solution.py:46
  78.3 11.6 %collective-permute-start.17 = (bf16[1,192,256]{2,1,0:T(8,128)(2,1)S(1)}, bf16[1,192,256]{2,1,0:T(8,128)(2,1)S(1)}, u32[]{:S(2)}, u32[]{:S(2)}) collective-permute-start(bf16[1,192,256]{2,1,0:T(8,128)(2,1)S(1)} %add3_3.1), channel_id=1, source_target_pairs={{0,1},{1,0},{2,3},{3,2},{4,5},{5,4},{6,7},{7,6},{8,9},{9,8},{10,11... | collective-permute-start | bytes 294920 | tf_op jit(solution)/shard_map/ppermute | solution.py:46
  83.0 8.2 %collective-permute-start.19 = (bf16[1,192,256]{2,1,0:T(8,128)(2,1)S(1)}, bf16[1,192,256]{2,1,0:T(8,128)(2,1)S(1)}, u32[]{:S(2)}, u32[]{:S(2)}) collective-permute-start(bf16[1,192,256]{2,1,0:T(8,128)(2,1)S(1)} %add4_3.1), channel_id=1, source_target_pairs={{0,12},{1,13},{2,14},{3,15},{4,8},{5,9},{6,10},{7,11},{8,4},{9,5},... | collective-permute-start | bytes 294920 | tf_op jit(solution)/shard_map/ppermute | solution.py:46
  83.1 8.1 %collective-permute-start.16 = (bf16[1,128,256]{2,1,0:T(8,128)(2,1)S(1)}, bf16[1,128,256]{2,1,0:T(8,128)(2,1)S(1)}, u32[]{:S(2)}, u32[]{:S(2)}) collective-permute-start(bf16[1,128,256]{2,1,0:T(8,128)(2,1)S(1)} %add2_3.1), channel_id=1, source_target_pairs={{0,3},{1,2},{2,1},{3,0},{4,7},{5,6},{6,5},{7,4},{8,11},{9,10},{10,... | collective-permute-start | bytes 196616 | tf_op jit(solution)/shard_map/ppermute | solution.py:46
  93.1 3.2 %collective-permute-start.22 = (f32[16,128]{1,0:T(8,128)S(1)}, f32[16,128]{1,0:T(8,128)S(1)}, u32[]{:S(2)}, u32[]{:S(2)}) collective-permute-start(f32[16,128]{1,0:T(8,128)S(1)} %get-tuple-element.59), channel_id=1, source_target_pairs={{0,144},{16,128},{32,176},{48,160},{64,208},{80,192},{96,240},{112... | collective-permute-start | bytes 24584 | tf_op jit(solution)/shard_map/ppermute | solution.py:46
  93.2 3.7 %collective-permute-start.21 = (f32[16,128]{1,0:T(8,128)S(1)}, f32[16,128]{1,0:T(8,128)S(1)}, u32[]{:S(2)}, u32[]{:S(2)}) collective-permute-start(f32[16,128]{1,0:T(8,128)S(1)} %get-tuple-element.59), channel_id=1, source_target_pairs={{0,128},{16,144},{32,160},{48,176},{64,192},{80,208},{96,224},{112... | collective-permute-start | bytes 24584 | tf_op jit(solution)/shard_map/ppermute | solution.py:46
  93.3 3.6 %collective-permute-start.20 = (f32[16,128]{1,0:T(8,128)S(1)}, f32[16,128]{1,0:T(8,128)S(1)}, u32[]{:S(2)}, u32[]{:S(2)}) collective-permute-start(f32[16,128]{1,0:T(8,128)S(1)} %get-tuple-element.59), channel_id=1, source_target_pairs={{0,16},{16,0},{32,48},{48,32},{64,80},{80,64},{96,112},{112,96},{1... | collective-permute-start | bytes 24584 | tf_op jit(solution)/shard_map/ppermute | solution.py:46
  96.9 5.8 %collective-permute-start.25 = (f32[16,128]{1,0:T(8,128)S(1)}, f32[16,128]{1,0:T(8,128)S(1)}, u32[]{:S(2)}, u32[]{:S(2)}) collective-permute-start(f32[16,128]{1,0:T(8,128)S(1)} %add_add_fusion.a_ref), channel_id=1, source_target_pairs={{0,96},{16,112},{32,64},{48,80},{64,32},{80,48},{96,0},{112,16},{1... | collective-permute-start | bytes 24584 | tf_op jit(solution)/shard_map/ppermute | solution.py:46
  100.0 5.2 %collective-permute-start.24 = (f32[16,128]{1,0:T(8,128)S(1)}, f32[16,128]{1,0:T(8,128)S(1)}, u32[]{:S(2)}, u32[]{:S(2)}) collective-permute-start(f32[16,128]{1,0:T(8,128)S(1)} %add_add_fusion.a_ref), channel_id=1, source_target_pairs={{0,64},{16,80},{32,96},{48,112},{64,0},{80,16},{96,32},{112,48},{1... | collective-permute-start | bytes 24584 | tf_op jit(solution)/shard_map/ppermute | solution.py:46
  100.7 4.5 %collective-permute-start.23 = (f32[16,128]{1,0:T(8,128)S(1)}, f32[16,128]{1,0:T(8,128)S(1)}, u32[]{:S(2)}, u32[]{:S(2)}) collective-permute-start(f32[16,128]{1,0:T(8,128)S(1)} %add_add_fusion.a_ref), channel_id=1, source_target_pairs={{0,32},{16,48},{32,0},{48,16},{64,96},{80,112},{96,64},{112,80},{1... | collective-permute-start | bytes 24584 | tf_op jit(solution)/shard_map/ppermute | solution.py:46

commit v6 on v5

--- a/solution.py
+++ b/solution.py
@@ -182,7 +182,9 @@
     keep = (lax.broadcasted_iota(jnp.int32, (rows, width), 0) % LOW == band // BLOCK).astype(jnp.float32)
     own = lax.broadcasted_iota(jnp.int32, (rows // LOW, rows), 1) // LOW
     gather = (own == lax.broadcasted_iota(jnp.int32, (rows // LOW, rows), 0)).astype(jnp.bfloat16)
-    return pick, keep, gather
+    own = lax.broadcasted_iota(jnp.int32, (rows, rows // LOW), 0) // LOW
+    spread = (own == lax.broadcasted_iota(jnp.int32, (rows, rows // LOW), 1)).astype(jnp.bfloat16)
+    return pick, keep, gather, spread
 
 
 def both_of(x, table, dims=((1,), (0,))):
@@ -192,7 +194,7 @@
 
 def coeff_kernel(counts, *refs):
     n = sum(counts)
-    mom_ref, band_ref, low_ref, updated_ref, coeff_ref, chosen_ref = refs[n:]
+    mom_ref, band_ref, low_ref, updated_ref, coeff_ref, chosen_ref, pick_ref, keep_ref, spread_ref = refs[n:]
     rows, at = [], 0
     for count in counts:
         parts = [f32(ref[0]) for ref in refs[at : at + count]]
@@ -203,7 +205,8 @@
     updated = DECAY * mom_ref[0] + jnp.concatenate(turned, axis=1)
     updated_ref[...] = updated
     coeff = forward(updated, low_ref[...])
-    pick, keep, gather = band_tables(band_ref, coeff.shape[0])
+    pick, keep, gather, spread = band_tables(band_ref, coeff.shape[0])
+    pick_ref[...], keep_ref[...], spread_ref[...] = pick, keep, spread
     picked = both_of(coeff, pick) * keep
     first, second = split(picked)
     chosen_ref[...] = dot(gather, first) + dot(gather, second)
@@ -216,11 +219,14 @@
     return pl.pallas_call(
         functools.partial(coeff_kernel, [len(chain) for chain in held]),
         in_specs=[IN_VMEM] * (len(arrays) + 1) + [pl.BlockSpec(memory_space=pltpu.SMEM), IN_VMEM],
-        out_specs=[IN_VMEM] * 3,
+        out_specs=[IN_VMEM] * 6,
         out_shape=[
             jax.ShapeDtypeStruct((rows, ncol), jnp.float32),
             jax.ShapeDtypeStruct((ncol // 4, 64), jnp.float32),
             jax.ShapeDtypeStruct((ncol // 64, 4 * BAND), jnp.float32),
+            jax.ShapeDtypeStruct((64, 4 * BAND), jnp.bfloat16),
+            jax.ShapeDtypeStruct((ncol // 4, 4 * BAND), jnp.float32),
+            jax.ShapeDtypeStruct((ncol // 4, ncol // 64), jnp.bfloat16),
         ],
         compiler_params=pltpu.CompilerParams(vmem_limit_bytes=VMEM),
         cost_estimate=pl.CostEstimate(flops=ncol * 1000000, bytes_accessed=ncol * 256 * 8, transcendentals=0),
@@ -243,23 +249,22 @@
     )(updated, coeffs, low)
 
 
-def update_kernel(scale, a_ref, b_ref, c_ref, d_ref, band_ref, low_ref, out_ref):
+def update_kernel(scale, a_ref, b_ref, c_ref, d_ref, pick_ref, keep_ref, spread_ref, low_ref, out_ref):
     total = (a_ref[...] + b_ref[...]) + (c_ref[...] + d_ref[...])
-    pick, keep, gather = band_tables(band_ref, LOW * total.shape[0])
     first, second = split(total)
-    spread = (dot(gather, first, ((0,), (0,))) + dot(gather, second, ((0,), (0,)))) * keep
-    coeff = both_of(spread, pick, ((1,), (1,)))
+    repeated = (dot(spread_ref[...], first) + dot(spread_ref[...], second)) * keep_ref[...]
+    coeff = both_of(repeated, pick_ref[...], ((1,), (1,)))
     out_ref[...] = (backward(coeff, low_ref[...]) * scale).astype(jnp.bfloat16)
 
 
-def make_update(parts, band, low, ncols, scale):
+def make_update(parts, tables, low, ncols, scale):
     return pl.pallas_call(
         functools.partial(update_kernel, scale),
-        in_specs=[IN_VMEM] * 4 + [pl.BlockSpec(memory_space=pltpu.SMEM), IN_VMEM],
+        in_specs=[IN_VMEM] * 8,
         out_shape=jax.ShapeDtypeStruct((ROWS, ncols), jnp.bfloat16),
         compiler_params=pltpu.CompilerParams(vmem_limit_bytes=VMEM),
         name="update",
-    )(*parts, band, low)
+    )(*parts, *tables, low)
 
 
 def per_device(activations, cotangent, momentum, band):
@@ -278,13 +283,13 @@
         held[c].append(swap(send, "fsdp", CHAINS[c][1][stage]))
         before = send if stage else before
 
-    updated, coeffs, chosen = coefficients(held, momentum, band, low)
+    updated, coeffs, chosen, *tables = coefficients(held, momentum, band, low)
     fresh = new_momentum(updated, coeffs, low, momentum.shape)
     a, b, c, d = [chosen] + [swap(chosen, "rep", m) for m in (1, 8, 9)]
     summed = (a + b) + (c + d)
     parts = [summed] + [swap(summed, "rep", m) for m in (2, 4, 6)]
     scale = BLOCK / math.sqrt(BAND * lax.axis_size("rep"))
-    update = make_update(parts, band, low, momentum.shape[2], scale)
+    update = make_update(parts, tables, low, momentum.shape[2], scale)
     return (fresh, update)
 
 

time: 108 us -> 108 us (level)
  no operation moved by 1% of the time
where the time goes in v6:
time: 108 us; the launch traced here: 107 us
  starting transfers between devices  46.7 us (43%)
  waiting for transfers between devices  38 us (35%)
  Pallas kernels  21.3 us (20%)
    ppermute x26, starting transfers between devices, swap(): return lax.ppermute(value, axis, [(i, i ^ mask) for i in range(n)])  46.7 us
    ppermute x26, waiting for transfers between devices, swap(): return lax.ppermute(value, axis, [(i, i ^ mask) for i in range(n)])  38 us
    pallas_call x2, Pallas kernels, terms(): pl.pallas_call(functools.partial(terms_kernel, kept), in_specs=[pl.BlockS...  15.1 us
  transfers between devices with their start and end apart: 26, of which 12 were waited for; matrix products, arithmetic and copies ran while one was open for 0% of the time, Pallas kernels for 9%

profile of v6, /device:TPU:6, one launch (start us, length us, event | category | flops | bytes accessed | tf_op | source)
XLA Modules:
  0.0 106.8 jit_solution(8312417348037292241)
XLA Ops:
  0.6 8.2 %terms_sent.1 = (bf16[8,256,256]{2,1,0:T(8,128)(2,1)S(1)}, bf16[8,256,256]{2,1,0:T(8,128)(2,1)}, bf16[8,128,256]{2,1,0:T(8,128)(2,1)S(1)}, bf16[8,192,256]{2,1,0:T(8,128)(2,1)S(1)}, bf16[8,192,256]{2,1,0:T(8,128)(2,1)S(1)}) custom-call(bf16[896,4096]{1,0:T(8,128)(2,1)} %act_ref.3, bf16[896,1024]{1,0:T(8,128)(2,1)} %cot_ref.2), custom_call_target="tpu_custom_call" | custom-call | flops 3758096384 | bytes 7340032 | tf_op jit(solution)/shard_map/terms_sent/pallas_call | solution.py:103
  8.8 0.9 collective-permute-start.1
  9.8 1.5 %collective-permute-start = (bf16[8,256,256]{2,1,0:T(8,128)(2,1)S(1)}, bf16[8,256,256]{2,1,0:T(8,128)(2,1)S(1)}, u32[]{:S(2)}, u32[]{:S(2)}) collective-permute-start(bf16[8,256,256]{2,1,0:T(8,128)(2,1)S(1)} %get-tuple-element.34), channel_id=1, source_target_pairs={{0,12},{1,13},{2,14},{3,15},{4,8},{5,9},{6,10},{7,11},{8,4},{9,5},... | collective-permute-start | bytes 3145736 | tf_op jit(solution)/shard_map/ppermute | solution.py:46
  11.2 5.9 %collective-permute-start.6 = (bf16[8,192,256]{2,1,0:T(8,128)(2,1)S(1)}, bf16[8,192,256]{2,1,0:T(8,128)(2,1)S(1)}, u32[]{:S(2)}, u32[]{:S(2)}) collective-permute-start(bf16[8,192,256]{2,1,0:T(8,128)(2,1)S(1)} %get-tuple-element.46), channel_id=1, source_target_pairs={{0,3},{1,2},{2,1},{3,0},{4,7},{5,6},{6,5},{7,4},{8,11},{9,10},{10,... | collective-permute-start | bytes 2359304 | tf_op jit(solution)/shard_map/ppermute | solution.py:46
  17.2 1.4 %collective-permute-start.4 = (bf16[8,192,256]{2,1,0:T(8,128)(2,1)S(1)}, bf16[8,192,256]{2,1,0:T(8,128)(2,1)S(1)}, u32[]{:S(2)}, u32[]{:S(2)}) collective-permute-start(bf16[8,192,256]{2,1,0:T(8,128)(2,1)S(1)} %get-tuple-element.42), channel_id=1, source_target_pairs={{0,1},{1,0},{2,3},{3,2},{4,5},{5,4},{6,7},{7,6},{8,9},{9,8},{10,11... | collective-permute-start | bytes 2359304 | tf_op jit(solution)/shard_map/ppermute | solution.py:46
  18.7 6.9 %terms_kept.1 = (bf16[8,256,256]{2,1,0:T(8,128)(2,1)S(1)}, bf16[8,256,256]{2,1,0:T(8,128)(2,1)S(1)}, bf16[8,128,256]{2,1,0:T(8,128)(2,1)S(1)}, bf16[8,192,256]{2,1,0:T(8,128)(2,1)S(1)}, bf16[8,192,256]{2,1,0:T(8,128)(2,1)S(1)}) custom-call(bf16[896,4096]{1,0:T(8,128)(2,1)} %act_ref.3, bf16[896,1024]{1,0:T(8,128)(2,1)S(1)} %copy-done.3), custom_call_target="tpu_custom_call" | custom-call | flops 3758096384 | bytes 7340032 | tf_op jit(solution)/shard_map/terms_kept/pallas_call | solution.py:103
  25.6 9.6 %collective-permute-done.1.refs_1_.refs_6_ = bf16[8,256,256]{2,1,0:T(8,128)(2,1)S(1)} collective-permute-done((bf16[8,256,256]{2,1,0:T(8,128)(2,1)}, bf16[8,256,256]{2,1,0:T(8,128)(2,1)S(1)}, u32[]{:S(2)}, u32[]{:S(2)}) %collective-permute-start.1) | collective-permute-done | bytes 1048608 | tf_op jit(solution)/shard_map/ppermute | solution.py:46
  35.3 2.5 %collective-permute-start.3 = (bf16[4,256,256]{2,1,0:T(8,128)(2,1)S(1)}, bf16[4,256,256]{2,1,0:T(8,128)(2,1)S(1)}, u32[]{:S(2)}, u32[]{:S(2)}) collective-permute-start(bf16[4,256,256]{2,1,0:T(8,128)(2,1)S(1)} %add1_1.1), channel_id=1, source_target_pairs={{0,12},{1,13},{2,14},{3,15},{4,8},{5,9},{6,10},{7,11},{8,4},{9,5},... | collective-permute-start | bytes 1572872 | tf_op jit(solution)/shard_map/ppermute | solution.py:46
  38.1 12.2 %collective-permute-done.6.refs_1_.refs_16_ = bf16[8,192,256]{2,1,0:T(8,128)(2,1)S(1)} collective-permute-done((bf16[8,192,256]{2,1,0:T(8,128)(2,1)S(1)}, bf16[8,192,256]{2,1,0:T(8,128)(2,1)S(1)}, u32[]{:S(2)}, u32[]{:S(2)}) %collective-permute-start.6) | collective-permute-done | bytes 786464 | tf_op jit(solution)/shard_map/ppermute | solution.py:46
  50.4 2.2 %collective-permute-start.8 = (bf16[4,192,256]{2,1,0:T(8,128)(2,1)S(1)}, bf16[4,192,256]{2,1,0:T(8,128)(2,1)S(1)}, u32[]{:S(2)}, u32[]{:S(2)}) collective-permute-start(bf16[4,192,256]{2,1,0:T(8,128)(2,1)S(1)} %add3_1.1), channel_id=1, source_target_pairs={{0,12},{1,13},{2,14},{3,15},{4,8},{5,9},{6,10},{7,11},{8,4},{9,5},... | collective-permute-start | bytes 1179656 | tf_op jit(solution)/shard_map/ppermute | solution.py:46
  54.0 3.6 %collective-permute-start.11 = (bf16[2,256,256]{2,1,0:T(8,128)(2,1)S(1)}, bf16[2,256,256]{2,1,0:T(8,128)(2,1)S(1)}, u32[]{:S(2)}, u32[]{:S(2)}) collective-permute-start(bf16[2,256,256]{2,1,0:T(8,128)(2,1)S(1)} %add1_2.1), channel_id=1, source_target_pairs={{0,3},{1,2},{2,1},{3,0},{4,7},{5,6},{6,5},{7,4},{8,11},{9,10},{10,... | collective-permute-start | bytes 786440 | tf_op jit(solution)/shard_map/ppermute | solution.py:46
  57.6 1.1 %collective-permute-start.10 = (bf16[4,128,256]{2,1,0:T(8,128)(2,1)S(1)}, bf16[4,128,256]{2,1,0:T(8,128)(2,1)S(1)}, u32[]{:S(2)}, u32[]{:S(2)}) collective-permute-start(bf16[4,128,256]{2,1,0:T(8,128)(2,1)S(1)} %add2_1.1), channel_id=1, source_target_pairs={{0,12},{1,13},{2,14},{3,15},{4,8},{5,9},{6,10},{7,11},{8,4},{9,5},... | collective-permute-start | bytes 786440 | tf_op jit(solution)/shard_map/ppermute | solution.py:46
  58.9 2.2 %collective-permute-start.7 = (bf16[2,256,256]{2,1,0:T(8,128)(2,1)S(1)}, bf16[2,256,256]{2,1,0:T(8,128)(2,1)S(1)}, u32[]{:S(2)}, u32[]{:S(2)}) collective-permute-start(bf16[2,256,256]{2,1,0:T(8,128)(2,1)S(1)} %add0_2.1), channel_id=1, source_target_pairs={{0,1},{1,0},{2,3},{3,2},{4,5},{5,4},{6,7},{7,6},{8,9},{9,8},{10,11... | collective-permute-start | bytes 786440 | tf_op jit(solution)/shard_map/ppermute | solution.py:46
  61.1 2.6 %collective-permute-done.8.refs_2_.refs_17_ = bf16[4,192,256]{2,1,0:T(8,128)(2,1)S(1)} collective-permute-done((bf16[4,192,256]{2,1,0:T(8,128)(2,1)S(1)}, bf16[4,192,256]{2,1,0:T(8,128)(2,1)S(1)}, u32[]{:S(2)}, u32[]{:S(2)}) %collective-permute-start.8) | collective-permute-done | bytes 393248 | tf_op jit(solution)/shard_map/ppermute | solution.py:46
  63.9 2.1 %collective-permute-done.12.refs_2_.refs_22_ = bf16[4,192,256]{2,1,0:T(8,128)(2,1)S(1)} collective-permute-done((bf16[4,192,256]{2,1,0:T(8,128)(2,1)S(1)}, bf16[4,192,256]{2,1,0:T(8,128)(2,1)S(1)}, u32[]{:S(2)}, u32[]{:S(2)}) %collective-permute-start.12) | collective-permute-done | bytes 393248 | tf_op jit(solution)/shard_map/ppermute | solution.py:46
  66.2 6.4 %collective-permute-start.18 = (bf16[2,192,256]{2,1,0:T(8,128)(2,1)S(1)}, bf16[2,192,256]{2,1,0:T(8,128)(2,1)S(1)}, u32[]{:S(2)}, u32[]{:S(2)}) collective-permute-start(bf16[2,192,256]{2,1,0:T(8,128)(2,1)S(1)} %add4_2.1), channel_id=1, source_target_pairs={{0,3},{1,2},{2,1},{3,0},{4,7},{5,6},{6,5},{7,4},{8,11},{9,10},{10,... | collective-permute-start | bytes 589832 | tf_op jit(solution)/shard_map/ppermute | solution.py:46
  72.7 1.5 %collective-permute-start.15 = (bf16[2,128,256]{2,1,0:T(8,128)(2,1)S(1)}, bf16[2,128,256]{2,1,0:T(8,128)(2,1)S(1)}, u32[]{:S(2)}, u32[]{:S(2)}) collective-permute-start(bf16[2,128,256]{2,1,0:T(8,128)(2,1)S(1)} %add2_2.1), channel_id=1, source_target_pairs={{0,1},{1,0},{2,3},{3,2},{4,5},{5,4},{6,7},{7,6},{8,9},{9,8},{10,11... | collective-permute-start | bytes 393224 | tf_op jit(solution)/shard_map/ppermute | solution.py:46
  74.4 2.6 %collective-permute-start.13 = (bf16[1,256,256]{2,1,0:T(8,128)(2,1)S(1)}, bf16[1,256,256]{2,1,0:T(8,128)(2,1)S(1)}, u32[]{:S(2)}, u32[]{:S(2)}) collective-permute-start(bf16[1,256,256]{2,1,0:T(8,128)(2,1)S(1)} %add0_3.1), channel_id=1, source_target_pairs={{0,3},{1,2},{2,1},{3,0},{4,7},{5,6},{6,5},{7,4},{8,11},{9,10},{10,... | collective-permute-start | bytes 393224 | tf_op jit(solution)/shard_map/ppermute | solution.py:46
  77.0 1.3 %collective-permute-start.14 = (bf16[1,256,256]{2,1,0:T(8,128)(2,1)S(1)}, bf16[1,256,256]{2,1,0:T(8,128)(2,1)S(1)}, u32[]{:S(2)}, u32[]{:S(2)}) collective-permute-start(bf16[1,256,256]{2,1,0:T(8,128)(2,1)S(1)} %add1_3.1), channel_id=1, source_target_pairs={{0,1},{1,0},{2,3},{3,2},{4,5},{5,4},{6,7},{7,6},{8,9},{9,8},{10,11... | collective-permute-start | bytes 393224 | tf_op jit(solution)/shard_map/ppermute | solution.py:46
  78.3 1.6 %collective-permute-start.17 = (bf16[1,192,256]{2,1,0:T(8,128)(2,1)S(1)}, bf16[1,192,256]{2,1,0:T(8,128)(2,1)S(1)}, u32[]{:S(2)}, u32[]{:S(2)}) collective-permute-start(bf16[1,192,256]{2,1,0:T(8,128)(2,1)S(1)} %add3_3.1), channel_id=1, source_target_pairs={{0,1},{1,0},{2,3},{3,2},{4,5},{5,4},{6,7},{7,6},{8,9},{9,8},{10,11... | collective-permute-start | bytes 294920 | tf_op jit(solution)/shard_map/ppermute | solution.py:46
  79.9 1.0 collective-permute-done.15.refs_3_.refs_13_
  81.0 1.9 %collective-permute-done.18.refs_3_.refs_23_ = bf16[2,192,256]{2,1,0:T(8,128)(2,1)S(1)} collective-permute-done((bf16[2,192,256]{2,1,0:T(8,128)(2,1)S(1)}, bf16[2,192,256]{2,1,0:T(8,128)(2,1)S(1)}, u32[]{:S(2)}, u32[]{:S(2)}) %collective-permute-start.18) | collective-permute-done | bytes 196640 | tf_op jit(solution)/shard_map/ppermute | solution.py:46
  83.1 4.9 %collective-permute-start.16 = (bf16[1,128,256]{2,1,0:T(8,128)(2,1)S(1)}, bf16[1,128,256]{2,1,0:T(8,128)(2,1)S(1)}, u32[]{:S(2)}, u32[]{:S(2)}) collective-permute-start(bf16[1,128,256]{2,1,0:T(8,128)(2,1)S(1)} %add2_3.1), channel_id=1, source_target_pairs={{0,3},{1,2},{2,1},{3,0},{4,7},{5,6},{6,5},{7,4},{8,11},{9,10},{10,... | collective-permute-start | bytes 196616 | tf_op jit(solution)/shard_map/ppermute | solution.py:46
  88.0 2.0 %collective-permute-done.17.refs_19_ = bf16[1,192,256]{2,1,0:T(8,128)(2,1)S(1)} collective-permute-done((bf16[1,192,256]{2,1,0:T(8,128)(2,1)S(1)}, bf16[1,192,256]{2,1,0:T(8,128)(2,1)S(1)}, u32[]{:S(2)}, u32[]{:S(2)}) %collective-permute-start.17) | collective-permute-done | bytes 98336 | tf_op jit(solution)/shard_map/ppermute | solution.py:46
  90.0 1.2 %collective-permute-done.16.refs_14_ = bf16[1,128,256]{2,1,0:T(8,128)(2,1)S(1)} collective-permute-done((bf16[1,128,256]{2,1,0:T(8,128)(2,1)S(1)}, bf16[1,128,256]{2,1,0:T(8,128)(2,1)S(1)}, u32[]{:S(2)}, u32[]{:S(2)}) %collective-permute-start.16) | collective-permute-done | bytes 65568 | tf_op jit(solution)/shard_map/ppermute | solution.py:46
  91.2 1.8 %coefficients.1 = (f32[256,1024]{1,0:T(8,128)S(1)}, f32[256,64]{1,0:T(8,128)S(1)}, f32[16,128]{1,0:T(8,128)S(1)}, bf16[64,128]{1,0:T(8,128)(2,1)S(1)}, f32[256,1...) custom-call(bf16[8,256,256]{2,1,0:T(8,128)(2,1)S(1)} %get-tuple-element.36.refs_0_, ...), custom_call_target="tpu_custom_call" | custom-call | flops 1024000000 | bytes 2097152 | tf_op jit(solution)/shard_map/coefficients/pallas_call | solution.py:219
  93.2 1.7 %collective-permute-start.20 = (f32[16,128]{1,0:T(8,128)S(1)}, f32[16,128]{1,0:T(8,128)S(1)}, u32[]{:S(2)}, u32[]{:S(2)}) collective-permute-start(f32[16,128]{1,0:T(8,128)S(1)} %get-tuple-element.62), channel_id=1, source_target_pairs={{0,16},{16,0},{32,48},{48,32},{64,80},{80,64},{96,112},{112,96},{1... | collective-permute-start | bytes 24584 | tf_op jit(solution)/shard_map/ppermute | solution.py:46
  95.0 1.2 %collective-permute-done.22 = f32[16,128]{1,0:T(8,128)S(1)} collective-permute-done((f32[16,128]{1,0:T(8,128)S(1)}, f32[16,128]{1,0:T(8,128)S(1)}, u32[]{:S(2)}, u32[]{:S(2)}) %collective-permute-start.22) | collective-permute-done | bytes 8224 | tf_op jit(solution)/shard_map/ppermute | solution.py:46
  96.9 3.1 %collective-permute-start.25 = (f32[16,128]{1,0:T(8,128)S(1)}, f32[16,128]{1,0:T(8,128)S(1)}, u32[]{:S(2)}, u32[]{:S(2)}) collective-permute-start(f32[16,128]{1,0:T(8,128)S(1)} %add_add_fusion.a_ref), channel_id=1, source_target_pairs={{0,96},{16,112},{32,64},{48,80},{64,32},{80,48},{96,0},{112,16},{1... | collective-permute-start | bytes 24584 | tf_op jit(solution)/shard_map/ppermute | solution.py:46
  101.1 1.6 %new_momentum.1 = f32[1,256,1024]{2,1,0:T(8,128)} custom-call(f32[256,1024]{1,0:T(8,128)S(1)} %get-tuple-element.60.updated_ref, f32[256,64]{1,0:T(8,128)S(1)} %get-tuple-element.61.coeff_ref, bf16[128,256]{1,0:T(8,128)(2,1)S(1)} %copy-done.1), custom_call_target="tpu_custom_call" | custom-call | flops 2000000000 | bytes 2000000 | tf_op jit(solution)/shard_map/new_momentum/pallas_call | solution.py:242
  102.6 2.5 %collective-permute-done.24.c_ref = f32[16,128]{1,0:T(8,128)S(1)} collective-permute-done((f32[16,128]{1,0:T(8,128)S(1)}, f32[16,128]{1,0:T(8,128)S(1)}, u32[]{:S(2)}, u32[]{:S(2)}) %collective-permute-start.24) | collective-permute-done | bytes 8224 | tf_op jit(solution)/shard_map/ppermute | solution.py:46
  105.1 1.7 %update.1 = bf16[256,1024]{1,0:T(8,128)(2,1)} custom-call(f32[16,128]{1,0:T(8,128)S(1)} %add_add_fusion.a_ref, f32[16,128]{1,0:T(8,128)S(1)} %collective-permute-done.23.b_ref, f32[16,128]{1,0:T(8,128)S(1)} %collective-permute-done.24.c_ref, f32[16,128]{1,0:T(8,128)S(1)} %collective-permute-done.25.d_ref, bf16[64,128]{1,0:T(8,128)(2,1)S(1)} %get-tuple-element.63.pick_ref, ...), custom_call_target="tpu_custom_call" | custom-call | tf_op jit(solution)/shard_map/update/pallas_call | solution.py:261
  (49 shorter events, 4.7 us)
Async XLA Ops:
  0.6 18.1 %copy-start.3 = (bf16[896,1024]{1,0:T(8,128)(2,1)S(1)}, bf16[896,1024]{1,0:T(8,128)(2,1)}, u32[]{:S(2)}) copy-start(bf16[896,1024]{1,0:T(8,128)(2,1)} %cot_ref.2) | copy-start | bytes 5505028
  8.8 26.3 %collective-permute-start.1 = (bf16[8,256,256]{2,1,0:T(8,128)(2,1)}, bf16[8,256,256]{2,1,0:T(8,128)(2,1)S(1)}, u32[]{:S(2)}, u32[]{:S(2)}) collective-permute-start(bf16[8,256,256]{2,1,0:T(8,128)(2,1)} %get-tuple-element.38), channel_id=1, source_target_pairs={{0,4},{1,5},{2,6},{3,7},{4,0},{5,1},{6,2},{7,3},{8,12},{9,13},{10,... | collective-permute-start | bytes 3145736 | tf_op jit(solution)/shard_map/ppermute | solution.py:46
  9.8 28.1 %collective-permute-start = (bf16[8,256,256]{2,1,0:T(8,128)(2,1)S(1)}, bf16[8,256,256]{2,1,0:T(8,128)(2,1)S(1)}, u32[]{:S(2)}, u32[]{:S(2)}) collective-permute-start(bf16[8,256,256]{2,1,0:T(8,128)(2,1)S(1)} %get-tuple-element.34), channel_id=1, source_target_pairs={{0,12},{1,13},{2,14},{3,15},{4,8},{5,9},{6,10},{7,11},{8,4},{9,5},... | collective-permute-start | bytes 3145736 | tf_op jit(solution)/shard_map/ppermute | solution.py:46
  11.2 39.0 %collective-permute-start.6 = (bf16[8,192,256]{2,1,0:T(8,128)(2,1)S(1)}, bf16[8,192,256]{2,1,0:T(8,128)(2,1)S(1)}, u32[]{:S(2)}, u32[]{:S(2)}) collective-permute-start(bf16[8,192,256]{2,1,0:T(8,128)(2,1)S(1)} %get-tuple-element.46), channel_id=1, source_target_pairs={{0,3},{1,2},{2,1},{3,0},{4,7},{5,6},{6,5},{7,4},{8,11},{9,10},{10,... | collective-permute-start | bytes 2359304 | tf_op jit(solution)/shard_map/ppermute | solution.py:46
  17.2 36.2 %collective-permute-start.4 = (bf16[8,192,256]{2,1,0:T(8,128)(2,1)S(1)}, bf16[8,192,256]{2,1,0:T(8,128)(2,1)S(1)}, u32[]{:S(2)}, u32[]{:S(2)}) collective-permute-start(bf16[8,192,256]{2,1,0:T(8,128)(2,1)S(1)} %get-tuple-element.42), channel_id=1, source_target_pairs={{0,1},{1,0},{2,3},{3,2},{4,5},{5,4},{6,7},{7,6},{8,9},{9,8},{10,11... | collective-permute-start | bytes 2359304 | tf_op jit(solution)/shard_map/ppermute | solution.py:46
  18.6 33.9 %collective-permute-start.5 = (bf16[8,128,256]{2,1,0:T(8,128)(2,1)S(1)}, bf16[8,128,256]{2,1,0:T(8,128)(2,1)S(1)}, u32[]{:S(2)}, u32[]{:S(2)}) collective-permute-start(bf16[8,128,256]{2,1,0:T(8,128)(2,1)S(1)} %get-tuple-element.44), channel_id=1, source_target_pairs={{0,4},{1,5},{2,6},{3,7},{4,0},{5,1},{6,2},{7,3},{8,12},{9,13},{10,... | collective-permute-start | bytes 1572872 | tf_op jit(solution)/shard_map/ppermute | solution.py:46
  35.3 18.6 %collective-permute-start.3 = (bf16[4,256,256]{2,1,0:T(8,128)(2,1)S(1)}, bf16[4,256,256]{2,1,0:T(8,128)(2,1)S(1)}, u32[]{:S(2)}, u32[]{:S(2)}) collective-permute-start(bf16[4,256,256]{2,1,0:T(8,128)(2,1)S(1)} %add1_1.1), channel_id=1, source_target_pairs={{0,12},{1,13},{2,14},{3,15},{4,8},{5,9},{6,10},{7,11},{8,4},{9,5},... | collective-permute-start | bytes 1572872 | tf_op jit(solution)/shard_map/ppermute | solution.py:46
  38.0 20.8 %collective-permute-start.2 = (bf16[4,256,256]{2,1,0:T(8,128)(2,1)S(1)}, bf16[4,256,256]{2,1,0:T(8,128)(2,1)S(1)}, u32[]{:S(2)}, u32[]{:S(2)}) collective-permute-start(bf16[4,256,256]{2,1,0:T(8,128)(2,1)S(1)} %add0_1.1), channel_id=1, source_target_pairs={{0,4},{1,5},{2,6},{3,7},{4,0},{5,1},{6,2},{7,3},{8,12},{9,13},{10,... | collective-permute-start | bytes 1572872 | tf_op jit(solution)/shard_map/ppermute | solution.py:46
  50.4 13.3 %collective-permute-start.8 = (bf16[4,192,256]{2,1,0:T(8,128)(2,1)S(1)}, bf16[4,192,256]{2,1,0:T(8,128)(2,1)S(1)}, u32[]{:S(2)}, u32[]{:S(2)}) collective-permute-start(bf16[4,192,256]{2,1,0:T(8,128)(2,1)S(1)} %add3_1.1), channel_id=1, source_target_pairs={{0,12},{1,13},{2,14},{3,15},{4,8},{5,9},{6,10},{7,11},{8,4},{9,5},... | collective-permute-start | bytes 1179656 | tf_op jit(solution)/shard_map/ppermute | solution.py:46
  53.5 12.6 %collective-permute-start.12 = (bf16[4,192,256]{2,1,0:T(8,128)(2,1)S(1)}, bf16[4,192,256]{2,1,0:T(8,128)(2,1)S(1)}, u32[]{:S(2)}, u32[]{:S(2)}) collective-permute-start(bf16[4,192,256]{2,1,0:T(8,128)(2,1)S(1)} %add4_1.1), channel_id=1, source_target_pairs={{0,4},{1,5},{2,6},{3,7},{4,0},{5,1},{6,2},{7,3},{8,12},{9,13},{10,... | collective-permute-start | bytes 1179656 | tf_op jit(solution)/shard_map/ppermute | solution.py:46
  54.0 18.5 %collective-permute-start.11 = (bf16[2,256,256]{2,1,0:T(8,128)(2,1)S(1)}, bf16[2,256,256]{2,1,0:T(8,128)(2,1)S(1)}, u32[]{:S(2)}, u32[]{:S(2)}) collective-permute-start(bf16[2,256,256]{2,1,0:T(8,128)(2,1)S(1)} %add1_2.1), channel_id=1, source_target_pairs={{0,3},{1,2},{2,1},{3,0},{4,7},{5,6},{6,5},{7,4},{8,11},{9,10},{10,... | collective-permute-start | bytes 786440 | tf_op jit(solution)/shard_map/ppermute | solution.py:46
  57.6 15.0 %collective-permute-start.10 = (bf16[4,128,256]{2,1,0:T(8,128)(2,1)S(1)}, bf16[4,128,256]{2,1,0:T(8,128)(2,1)S(1)}, u32[]{:S(2)}, u32[]{:S(2)}) collective-permute-start(bf16[4,128,256]{2,1,0:T(8,128)(2,1)S(1)} %add2_1.1), channel_id=1, source_target_pairs={{0,12},{1,13},{2,14},{3,15},{4,8},{5,9},{6,10},{7,11},{8,4},{9,5},... | collective-permute-start | bytes 786440 | tf_op jit(solution)/shard_map/ppermute | solution.py:46
  58.9 15.4 %collective-permute-start.7 = (bf16[2,256,256]{2,1,0:T(8,128)(2,1)S(1)}, bf16[2,256,256]{2,1,0:T(8,128)(2,1)S(1)}, u32[]{:S(2)}, u32[]{:S(2)}) collective-permute-start(bf16[2,256,256]{2,1,0:T(8,128)(2,1)S(1)} %add0_2.1), channel_id=1, source_target_pairs={{0,1},{1,0},{2,3},{3,2},{4,5},{5,4},{6,7},{7,6},{8,9},{9,8},{10,11... | collective-permute-start | bytes 786440 | tf_op jit(solution)/shard_map/ppermute | solution.py:46
  63.8 27.4 %copy-start = (f32[1,256,1024]{2,1,0:T(8,128)S(1)}, f32[1,256,1024]{2,1,0:T(8,128)}, u32[]{:S(2)}) copy-start(f32[1,256,1024]{2,1,0:T(8,128)} %refs_25_.1) | copy-start | bytes 3145732
  63.8 27.4 %copy-start.1 = (bf16[128,256]{1,0:T(8,128)(2,1)S(1)}, bf16[128,256]{1,0:T(8,128)(2,1)}, u32[]{:S(2)}) copy-start(bf16[128,256]{1,0:T(8,128)(2,1)} %constant.2.clone.refs_27_.low_ref) | copy-start | bytes 196612
  63.8 27.4 %copy-start.2 = (s32[32]{0:T(128)S(1)}, s32[32]{0:T(128)}, u32[]{:S(2)}) copy-start(s32[32]{0:T(128)} %refs_26_.1) | copy-start | bytes 388
  63.8 10.4 %collective-permute-start.9 = (bf16[2,192,256]{2,1,0:T(8,128)(2,1)S(1)}, bf16[2,192,256]{2,1,0:T(8,128)(2,1)S(1)}, u32[]{:S(2)}, u32[]{:S(2)}) collective-permute-start(bf16[2,192,256]{2,1,0:T(8,128)(2,1)S(1)} %add3_2.1), channel_id=1, source_target_pairs={{0,4},{1,5},{2,6},{3,7},{4,0},{5,1},{6,2},{7,3},{8,12},{9,13},{10,... | collective-permute-start | bytes 589832 | tf_op jit(solution)/shard_map/ppermute | solution.py:46
  66.2 16.8 %collective-permute-start.18 = (bf16[2,192,256]{2,1,0:T(8,128)(2,1)S(1)}, bf16[2,192,256]{2,1,0:T(8,128)(2,1)S(1)}, u32[]{:S(2)}, u32[]{:S(2)}) collective-permute-start(bf16[2,192,256]{2,1,0:T(8,128)(2,1)S(1)} %add4_2.1), channel_id=1, source_target_pairs={{0,3},{1,2},{2,1},{3,0},{4,7},{5,6},{6,5},{7,4},{8,11},{9,10},{10,... | collective-permute-start | bytes 589832 | tf_op jit(solution)/shard_map/ppermute | solution.py:46
  72.7 8.3 %collective-permute-start.15 = (bf16[2,128,256]{2,1,0:T(8,128)(2,1)S(1)}, bf16[2,128,256]{2,1,0:T(8,128)(2,1)S(1)}, u32[]{:S(2)}, u32[]{:S(2)}) collective-permute-start(bf16[2,128,256]{2,1,0:T(8,128)(2,1)S(1)} %add2_2.1), channel_id=1, source_target_pairs={{0,1},{1,0},{2,3},{3,2},{4,5},{5,4},{6,7},{7,6},{8,9},{9,8},{10,11... | collective-permute-start | bytes 393224 | tf_op jit(solution)/shard_map/ppermute | solution.py:46
  74.4 15.6 %collective-permute-start.13 = (bf16[1,256,256]{2,1,0:T(8,128)(2,1)S(1)}, bf16[1,256,256]{2,1,0:T(8,128)(2,1)S(1)}, u32[]{:S(2)}, u32[]{:S(2)}) collective-permute-start(bf16[1,256,256]{2,1,0:T(8,128)(2,1)S(1)} %add0_3.1), channel_id=1, source_target_pairs={{0,3},{1,2},{2,1},{3,0},{4,7},{5,6},{6,5},{7,4},{8,11},{9,10},{10,... | collective-permute-start | bytes 393224 | tf_op jit(solution)/shard_map/ppermute | solution.py:46
  77.0 13.0 %collective-permute-start.14 = (bf16[1,256,256]{2,1,0:T(8,128)(2,1)S(1)}, bf16[1,256,256]{2,1,0:T(8,128)(2,1)S(1)}, u32[]{:S(2)}, u32[]{:S(2)}) collective-permute-start(bf16[1,256,256]{2,1,0:T(8,128)(2,1)S(1)} %add1_3.1), channel_id=1, source_target_pairs={{0,1},{1,0},{2,3},{3,2},{4,5},{5,4},{6,7},{7,6},{8,9},{9,8},{10,11... | collective-permute-start | bytes 393224 | tf_op jit(solution)/shard_map/ppermute | solution.py:46
  78.3 11.6 %collective-permute-start.17 = (bf16[1,192,256]{2,1,0:T(8,128)(2,1)S(1)}, bf16[1,192,256]{2,1,0:T(8,128)(2,1)S(1)}, u32[]{:S(2)}, u32[]{:S(2)}) collective-permute-start(bf16[1,192,256]{2,1,0:T(8,128)(2,1)S(1)} %add3_3.1), channel_id=1, source_target_pairs={{0,1},{1,0},{2,3},{3,2},{4,5},{5,4},{6,7},{7,6},{8,9},{9,8},{10,11... | collective-permute-start | bytes 294920 | tf_op jit(solution)/shard_map/ppermute | solution.py:46
  83.0 8.2 %collective-permute-start.19 = (bf16[1,192,256]{2,1,0:T(8,128)(2,1)S(1)}, bf16[1,192,256]{2,1,0:T(8,128)(2,1)S(1)}, u32[]{:S(2)}, u32[]{:S(2)}) collective-permute-start(bf16[1,192,256]{2,1,0:T(8,128)(2,1)S(1)} %add4_3.1), channel_id=1, source_target_pairs={{0,12},{1,13},{2,14},{3,15},{4,8},{5,9},{6,10},{7,11},{8,4},{9,5},... | collective-permute-start | bytes 294920 | tf_op jit(solution)/shard_map/ppermute | solution.py:46
  83.1 8.1 %collective-permute-start.16 = (bf16[1,128,256]{2,1,0:T(8,128)(2,1)S(1)}, bf16[1,128,256]{2,1,0:T(8,128)(2,1)S(1)}, u32[]{:S(2)}, u32[]{:S(2)}) collective-permute-start(bf16[1,128,256]{2,1,0:T(8,128)(2,1)S(1)} %add2_3.1), channel_id=1, source_target_pairs={{0,3},{1,2},{2,1},{3,0},{4,7},{5,6},{6,5},{7,4},{8,11},{9,10},{10,... | collective-permute-start | bytes 196616 | tf_op jit(solution)/shard_map/ppermute | solution.py:46
  93.0 3.2 %collective-permute-start.22 = (f32[16,128]{1,0:T(8,128)S(1)}, f32[16,128]{1,0:T(8,128)S(1)}, u32[]{:S(2)}, u32[]{:S(2)}) collective-permute-start(f32[16,128]{1,0:T(8,128)S(1)} %get-tuple-element.62), channel_id=1, source_target_pairs={{0,144},{16,128},{32,176},{48,160},{64,208},{80,192},{96,240},{112... | collective-permute-start | bytes 24584 | tf_op jit(solution)/shard_map/ppermute | solution.py:46
  93.1 3.7 %collective-permute-start.21 = (f32[16,128]{1,0:T(8,128)S(1)}, f32[16,128]{1,0:T(8,128)S(1)}, u32[]{:S(2)}, u32[]{:S(2)}) collective-permute-start(f32[16,128]{1,0:T(8,128)S(1)} %get-tuple-element.62), channel_id=1, source_target_pairs={{0,128},{16,144},{32,160},{48,176},{64,192},{80,208},{96,224},{112... | collective-permute-start | bytes 24584 | tf_op jit(solution)/shard_map/ppermute | solution.py:46
  93.2 3.6 %collective-permute-start.20 = (f32[16,128]{1,0:T(8,128)S(1)}, f32[16,128]{1,0:T(8,128)S(1)}, u32[]{:S(2)}, u32[]{:S(2)}) collective-permute-start(f32[16,128]{1,0:T(8,128)S(1)} %get-tuple-element.62), channel_id=1, source_target_pairs={{0,16},{16,0},{32,48},{48,32},{64,80},{80,64},{96,112},{112,96},{1... | collective-permute-start | bytes 24584 | tf_op jit(solution)/shard_map/ppermute | solution.py:46
  96.9 5.8 %collective-permute-start.25 = (f32[16,128]{1,0:T(8,128)S(1)}, f32[16,128]{1,0:T(8,128)S(1)}, u32[]{:S(2)}, u32[]{:S(2)}) collective-permute-start(f32[16,128]{1,0:T(8,128)S(1)} %add_add_fusion.a_ref), channel_id=1, source_target_pairs={{0,96},{16,112},{32,64},{48,80},{64,32},{80,48},{96,0},{112,16},{1... | collective-permute-start | bytes 24584 | tf_op jit(solution)/shard_map/ppermute | solution.py:46
  100.0 5.2 %collective-permute-start.24 = (f32[16,128]{1,0:T(8,128)S(1)}, f32[16,128]{1,0:T(8,128)S(1)}, u32[]{:S(2)}, u32[]{:S(2)}) collective-permute-start(f32[16,128]{1,0:T(8,128)S(1)} %add_add_fusion.a_ref), channel_id=1, source_target_pairs={{0,64},{16,80},{32,96},{48,112},{64,0},{80,16},{96,32},{112,48},{1... | collective-permute-start | bytes 24584 | tf_op jit(solution)/shard_map/ppermute | solution.py:46
  100.6 4.5 %collective-permute-start.23 = (f32[16,128]{1,0:T(8,128)S(1)}, f32[16,128]{1,0:T(8,128)S(1)}, u32[]{:S(2)}, u32[]{:S(2)}) collective-permute-start(f32[16,128]{1,0:T(8,128)S(1)} %add_add_fusion.a_ref), channel_id=1, source_target_pairs={{0,32},{16,48},{32,0},{48,16},{64,96},{80,112},{96,64},{112,80},{1... | collective-permute-start | bytes 24584 | tf_op jit(solution)/shard_map/ppermute | solution.py:46
